TPU v7x, 512 devices: a whole 4x4x16 slice. The times are simulated.
512 devices in a mesh: tm: 128 (over x_lo, y, z), lat: 4 (over x_hi, core).
Axes of the slice: x: 4 (x_hi: 2, x_lo: 2; x = x_hi * 2 + x_lo), y: 4, z: 16, core: 2. Of those that a mesh axis runs over, the one named last changes fastest.
Arguments:
- trajectory: bfloat16 [512, 8, 64, 256], P('tm', 'lat'), may hold values from -6 to 6
- cotangent: bfloat16 [512, 8, 64, 256], P('tm', 'lat'), may hold values from -6 to 6
- conv_weight: bfloat16 [9, 256, 256], replicated, may hold values from -0.125 to 0.125
- proj_weight: bfloat16 [256, 256], replicated, may hold values from -0.375 to 0.375
- mixing: float32 [25, 256], replicated, may hold values from -2.5 to 2.5
- offsets: int32 [512], replicated, may hold values from 0 to 4
Outputs:
- grads: bfloat16 [512, 8, 64, 256], P('tm', 'lat')
All inputs are finite; a program needn't handle non-finite values.
Results may differ from a plain program's by a relative error of at most 0.005.
Values may be sent and summed in bfloat16 or wider, within the bound.
No kernel may reach another device: no remote copies, remote signals or barrier semaphores. Data moves between devices by JAX's collectives and lax.ppermute only.
A program may use at most 64 MiB of HBM per device.

v0:
```python
import jax
import jax.numpy as jnp
from jax import lax
from jax.sharding import PartitionSpec as P


def extended_2(value, sides, width):
    for axis, dim in sides:
        size, length = (lax.axis_size(axis), value.shape[dim])
        up = [(i, (i + 1) % size) for i in range(size - 1)]
        down = [(j, i) for i, j in up]
        last = lax.slice_in_dim(value, length - width, length, axis=dim)
        initial = lax.slice_in_dim(value, 0, width, axis=dim)
        before = lax.ppermute(last, axis, up)
        after = lax.ppermute(initial, axis, down)
        value = jnp.concatenate([before, value, after], axis=dim)
    return value


def silu_slope(values):
    sigma = jax.nn.sigmoid(values)
    return sigma * (1.0 + values * (1.0 - sigma))


def convolve(padded, kernel, transposed):
    frame_count, row_ext, lon_count, channels = padded.shape
    row_count = row_ext - 2
    summed = jnp.zeros((frame_count * row_count * lon_count, kernel.shape[2]), jnp.float32)
    for tap_index in range(9):
        lat_step = tap_index // 3
        lon_step = tap_index % 3
        if transposed:
            shifted = jnp.roll(
                padded[:, 2 - lat_step : 2 - lat_step + row_count], lon_step - 1, axis=2
            )
            matrix = kernel[tap_index].T
        else:
            shifted = jnp.roll(padded[:, lat_step : lat_step + row_count], 1 - lon_step, axis=2)
            matrix = kernel[tap_index]
        summed = summed + jnp.dot(
            shifted.reshape(-1, channels), matrix, preferred_element_type=jnp.float32
        )
    return summed.reshape(frame_count, row_count, lon_count, -1)


def pick_rows(row_ids, inside, mixing):
    onehot = (row_ids[:, None] == jnp.arange(25, dtype=jnp.int32)[None, :]).astype(jnp.float32)
    picked = jnp.dot(onehot, mixing, precision=lax.Precision.HIGHEST)
    return jnp.where(inside[:, None], picked, 0.0)


def own_weights(offsets, mixing, first_frame, frame_count):
    total_frames = offsets.shape[0]
    frame_ids = first_frame + jnp.arange(frame_count, dtype=jnp.int32)
    own_offsets = lax.dynamic_slice_in_dim(offsets, first_frame, frame_count, 0)
    starts = jnp.clip(frame_ids - own_offsets, 0, total_frames - 5)
    places = frame_ids - starts
    weights_list = []
    for time_lag in range(-4, 5):
        slot_pos = places + time_lag
        inside = (slot_pos >= 0) & (slot_pos <= 4)
        weights_list.append(pick_rows(5 * places + slot_pos, inside, mixing))
    return weights_list


def body(trajectory, cotangent, conv_weight, proj_weight, mixing, offsets):
    frame_count, row_count, lon_count, channels = trajectory.shape
    first_frame = lax.axis_index("tm") * frame_count
    state_rows = extended_2(trajectory, (("lat", 1),), 1)
    conv_out = convolve(state_rows, conv_weight, False).astype(jnp.bfloat16)
    near_conv = extended_2(conv_out, (("tm", 0),), 4)
    lag_weights = own_weights(offsets, mixing, first_frame, frame_count)
    pre = jnp.zeros((frame_count, row_count, lon_count, channels), jnp.float32)
    for lag_index in range(9):
        pre = pre + lag_weights[lag_index][:, None, None, :] * near_conv[
            lag_index : lag_index + frame_count
        ].astype(jnp.float32)
    g_hidden = jnp.dot(
        cotangent.reshape(-1, channels), proj_weight.T, preferred_element_type=jnp.float32
    ).reshape(pre.shape)
    g_pre = (g_hidden * silu_slope(pre)).astype(jnp.bfloat16)
    pre_grads = g_pre.astype(jnp.float32)
    extended = jnp.zeros((frame_count + 8, row_count, lon_count, channels), jnp.float32)
    for lag_index in range(9):
        extended = extended.at[lag_index : lag_index + frame_count].add(
            lag_weights[lag_index][:, None, None, :] * pre_grads
        )
    outgoing = jnp.concatenate([extended[:4], extended[frame_count + 4 :]], axis=0)
    incoming = extended_2(outgoing, (("tm", 0),), 4)
    window_sum = extended[4 : frame_count + 4]
    window_sum = window_sum.at[:4].add(incoming[:4])
    window_sum = window_sum.at[frame_count - 4 :].add(incoming[12:])
    conv_grad = window_sum.astype(jnp.bfloat16)
    grad_rows = extended_2(conv_grad, (("lat", 1),), 1)
    return (cotangent.astype(jnp.float32) + convolve(grad_rows, conv_weight, True)).astype(
        jnp.bfloat16
    )


def solution(mesh):
    in_specs = (P("tm", "lat", None, None), P("tm", "lat", None, None), P(), P(), P(), P())
    out_specs = P("tm", "lat", None, None)
    return jax.shard_map(body, mesh=mesh, in_specs=in_specs, out_specs=out_specs, check_vma=False)
```

profile of v0, /device:TPU:3, one launch (start us, length us, event | category | flops | bytes accessed | tf_op | source)
XLA Modules:
  0.0 77.8 jit_solution(1260052218992952465)
XLA Ops:
  0.0 1.0 %fusion.93 = (bf16[4,1,64,256]{3,2,1,0:T(8,128)(2,1)S(1)}, bf16[4,1,64,256]{3,2,1,0:T(8,128)(2,1)S(1)}) fusion(bf16[4,2,64,256]{3,2,1,0:T(8,128)(2,1)} %param.32), kind=kLoop, calls=%fused_computation.198 | loop fusion | bytes 524288 | tf_op jit(solution)/shard_map/slice | solution.py:12
  1.0 4.3 %collective-permute-start = (bf16[4,1,64,256]{3,2,1,0:T(8,128)(2,1)S(1)}, bf16[4,1,64,256]{3,2,1,0:T(8,128)(2,1)S(1)}, u32[]{:S(2)}, u32[]{:S(2)}) collective-permute-start(bf16[4,1,64,256]{3,2,1,0:T(8,128)(2,1)S(1)} %get-tuple-element.191), channel_id=1, source_target_pairs={{0,1},{1,2},{2,3},{4,5},{5,6},{6,7},{8,9},{9,10},{10,11},{12,13},{... | collective-permute-start | bytes 393224 | tf_op jit(solution)/shard_map/ppermute | solution.py:14
  5.4 1.9 %collective-permute-start.1 = (bf16[4,1,64,256]{3,2,1,0:T(8,128)(2,1)S(1)}, bf16[4,1,64,256]{3,2,1,0:T(8,128)(2,1)S(1)}, u32[]{:S(2)}, u32[]{:S(2)}) collective-permute-start(bf16[4,1,64,256]{3,2,1,0:T(8,128)(2,1)S(1)} %get-tuple-element.192), channel_id=1, source_target_pairs={{1,0},{2,1},{3,2},{5,4},{6,5},{7,6},{9,8},{10,9},{11,10},{13,12},{... | collective-permute-start | bytes 393224 | tf_op jit(solution)/shard_map/ppermute | solution.py:15
  7.3 0.8 add_add_fusion.7
  8.1 0.8 %fusion.92 = (bf16[4,2,1,256]{3,2,1,0:T(2,128)(2,1)S(1)}, bf16[4,2,1,256]{3,2,1,0:T(2,128)(2,1)S(1)}) fusion(bf16[4,2,64,256]{3,2,1,0:T(8,128)(2,1)} %param.32), kind=kLoop, calls=%fused_computation.197 | loop fusion | bytes 16384 | tf_op jit(solution)/shard_map/jit(_roll_static)/slice | solution.py:38
  8.9 1.1 %fusion.91 = (bf16[4,2,63,256]{3,2,1,0:T(8,128)(2,1)S(1)}, bf16[4,2,63,256]{3,2,1,0:T(8,128)(2,1)S(1)}) fusion(bf16[4,2,64,256]{3,2,1,0:T(8,128)(2,1)} %param.32), kind=kLoop, calls=%fused_computation.196 | loop fusion | bytes 1032192 | tf_op jit(solution)/shard_map/jit(_roll_static)/slice | solution.py:38
  10.0 0.2 convolution_select_fusion.8
  10.2 0.2 convolution_select_fusion.6
  10.4 0.2 convolution_select_fusion.5
  10.6 0.2 convolution_select_fusion.3
  10.8 0.2 convolution_select_fusion.2
  11.0 0.2 convolution_select_fusion.1
  11.2 0.2 convolution_select_fusion
  11.4 0.1 pad_maximum_fusion.6
  11.6 1.6 %collective-permute-done.1 = bf16[4,1,64,256]{3,2,1,0:T(8,128)(2,1)S(1)} collective-permute-done((bf16[4,1,64,256]{3,2,1,0:T(8,128)(2,1)S(1)}, bf16[4,1,64,256]{3,2,1,0:T(8,128)(2,1)S(1)}, u32[]{:S(2)}, u32[]{:S(2)}) %collective-permute-start.1) | collective-permute-done | bytes 131104 | tf_op jit(solution)/shard_map/ppermute | solution.py:15
  13.2 0.1 fusion.87
  13.5 0.1 pad_maximum_fusion.8
  13.6 1.1 %copy-done.2 = bf16[9,256,256]{2,1,0:T(8,128)(2,1)S(1)} copy-done((bf16[9,256,256]{2,1,0:T(8,128)(2,1)S(1)}, bf16[9,256,256]{2,1,0:T(8,128)(2,1)}, u32[]{:S(2)}) %copy-start.2) | copy-done | bytes 1179672
  14.6 0.2 fusion.33
  14.9 0.1 pad_maximum_fusion.4
  15.0 0.2 fusion.52
  15.2 0.2 convolution_add_fusion.13
  15.4 0.2 convolution_add_fusion.12
  15.7 0.2 convolution_add_fusion.11
  15.9 0.2 convolution_add_fusion.10
  16.1 0.2 convolution_add_fusion.9
  16.3 0.2 convolution_add_fusion.8
  16.6 0.2 fusion.2
  16.8 14.5 %collective-permute-start.3 = (bf16[4,2,64,256]{3,2,1,0:T(8,128)(2,1)S(1)}, bf16[4,2,64,256]{3,2,1,0:T(8,128)(2,1)S(1)}, u32[]{:S(2)}, u32[]{:S(2)}) collective-permute-start(bf16[4,2,64,256]{3,2,1,0:T(8,128)(2,1)S(1)} %bitcast.119), channel_id=1, source_target_pairs={{4,0},{8,4},{12,8},{16,12},{20,16},{24,20},{28,24},{32,28},{36,32}... | collective-permute-start | bytes 786440 | tf_op jit(solution)/shard_map/ppermute | solution.py:15
  31.3 1.9 %collective-permute-start.2 = (bf16[4,2,64,256]{3,2,1,0:T(8,128)(2,1)S(1)}, bf16[4,2,64,256]{3,2,1,0:T(8,128)(2,1)S(1)}, u32[]{:S(2)}, u32[]{:S(2)}) collective-permute-start(bf16[4,2,64,256]{3,2,1,0:T(8,128)(2,1)S(1)} %bitcast.120), channel_id=1, source_target_pairs={{0,4},{4,8},{8,12},{12,16},{16,20},{20,24},{24,28},{28,32},{32,36}... | collective-permute-start | bytes 786440 | tf_op jit(solution)/shard_map/ppermute | solution.py:14
  33.2 0.2 convolution_select_fusion.4
  33.4 0.2 convolution_select_fusion.7
  33.6 1.0 %collective-permute-done.3 = bf16[4,2,64,256]{3,2,1,0:T(8,128)(2,1)S(1)} collective-permute-done((bf16[4,2,64,256]{3,2,1,0:T(8,128)(2,1)S(1)}, bf16[4,2,64,256]{3,2,1,0:T(8,128)(2,1)S(1)}, u32[]{:S(2)}, u32[]{:S(2)}) %collective-permute-start.3) | collective-permute-done | bytes 262176 | tf_op jit(solution)/shard_map/ppermute | solution.py:15
  34.6 8.0 %collective-permute-done.2 = bf16[4,2,64,256]{3,2,1,0:T(8,128)(2,1)S(1)} collective-permute-done((bf16[4,2,64,256]{3,2,1,0:T(8,128)(2,1)S(1)}, bf16[4,2,64,256]{3,2,1,0:T(8,128)(2,1)S(1)}, u32[]{:S(2)}, u32[]{:S(2)}) %collective-permute-start.2) | collective-permute-done | bytes 262176 | tf_op jit(solution)/shard_map/ppermute | solution.py:14
  42.6 0.7 convert_multiply_fusion.8
  43.3 0.2 scatter-add.26
  43.5 0.1 fusion.5
  43.7 0.1 fusion.7
  43.8 0.1 fusion.9
  43.9 0.1 fusion.11
  44.1 0.1 fusion.13
  44.2 0.1 fusion.15
  44.4 0.1 fusion.17
  44.5 0.1 fusion.18
  44.6 1.9 %collective-permute-start.4 = (f32[4,2,64,256]{3,2,1,0:T(8,128)S(1)}, f32[4,2,64,256]{3,2,1,0:T(8,128)S(1)}, u32[]{:S(2)}, u32[]{:S(2)}) collective-permute-start(f32[4,2,64,256]{3,2,1,0:T(8,128)S(1)} %get-tuple-element.155), channel_id=1, source_target_pairs={{0,4},{4,8},{8,12},{12,16},{16,20},{20,24},{24,28},{28,32},{32,36}... | collective-permute-start | bytes 1572872 | tf_op jit(solution)/shard_map/ppermute | solution.py:14
  46.6 7.6 %collective-permute-start.5 = (f32[4,2,64,256]{3,2,1,0:T(8,128)S(1)}, f32[4,2,64,256]{3,2,1,0:T(8,128)S(1)}, u32[]{:S(2)}, u32[]{:S(2)}) collective-permute-start(f32[4,2,64,256]{3,2,1,0:T(8,128)S(1)} %get-tuple-element.156), channel_id=1, source_target_pairs={{4,0},{8,4},{12,8},{16,12},{20,16},{24,20},{28,24},{32,28},{36,32}... | collective-permute-start | bytes 1572872 | tf_op jit(solution)/shard_map/ppermute | solution.py:15
  54.2 7.6 %collective-permute-done.4 = f32[4,2,64,256]{3,2,1,0:T(8,128)S(1)} collective-permute-done((f32[4,2,64,256]{3,2,1,0:T(8,128)S(1)}, f32[4,2,64,256]{3,2,1,0:T(8,128)S(1)}, u32[]{:S(2)}, u32[]{:S(2)}) %collective-permute-start.4) | collective-permute-done | bytes 524320 | tf_op jit(solution)/shard_map/ppermute | solution.py:14
  61.7 1.8 %collective-permute-done.5 = f32[4,2,64,256]{3,2,1,0:T(8,128)S(1)} collective-permute-done((f32[4,2,64,256]{3,2,1,0:T(8,128)S(1)}, f32[4,2,64,256]{3,2,1,0:T(8,128)S(1)}, u32[]{:S(2)}, u32[]{:S(2)}) %collective-permute-start.5) | collective-permute-done | bytes 524320 | tf_op jit(solution)/shard_map/ppermute | solution.py:15
  63.5 0.1 fusion.20
  63.7 2.5 %collective-permute-start.7 = (bf16[4,1,64,256]{3,2,1,0:T(8,128)(2,1)S(1)}, bf16[4,1,64,256]{3,2,1,0:T(8,128)(2,1)S(1)}, u32[]{:S(2)}, u32[]{:S(2)}) collective-permute-start(bf16[4,1,64,256]{3,2,1,0:T(8,128)(2,1)S(1)} %get-tuple-element.183), channel_id=1, source_target_pairs={{0,1},{1,2},{2,3},{4,5},{5,6},{6,7},{8,9},{9,10},{10,11},{12,13},{... | collective-permute-start | bytes 393224 | tf_op jit(solution)/shard_map/ppermute | solution.py:14
  66.2 1.9 %collective-permute-start.6 = (bf16[4,1,64,256]{3,2,1,0:T(8,128)(2,1)S(1)}, bf16[4,1,64,256]{3,2,1,0:T(8,128)(2,1)S(1)}, u32[]{:S(2)}, u32[]{:S(2)}) collective-permute-start(bf16[4,1,64,256]{3,2,1,0:T(8,128)(2,1)S(1)} %get-tuple-element.184), channel_id=1, source_target_pairs={{1,0},{2,1},{3,2},{5,4},{6,5},{7,6},{9,8},{10,9},{11,10},{13,12},{... | collective-permute-start | bytes 393224 | tf_op jit(solution)/shard_map/ppermute | solution.py:15
  68.1 5.9 %collective-permute-done.6 = bf16[4,1,64,256]{3,2,1,0:T(8,128)(2,1)S(1)} collective-permute-done((bf16[4,1,64,256]{3,2,1,0:T(8,128)(2,1)S(1)}, bf16[4,1,64,256]{3,2,1,0:T(8,128)(2,1)S(1)}, u32[]{:S(2)}, u32[]{:S(2)}) %collective-permute-start.6) | collective-permute-done | bytes 131104 | tf_op jit(solution)/shard_map/ppermute | solution.py:15
  74.0 0.1 fusion.21
  74.2 0.3 fusion.39
  74.5 0.3 fusion.50
  74.9 0.2 fusion.29
  75.1 0.3 convolution_add_fusion.6
  75.4 0.3 convolution_add_fusion.5
  75.7 0.3 convolution_add_fusion.4
  75.9 0.3 fusion
  76.2 0.3 convolution_add_fusion.2
  76.5 0.3 convolution_add_fusion.1
  76.8 0.3 convolution_add_fusion
  77.0 0.8 %add_convert_fusion = bf16[4,2,64,256]{3,2,1,0:T(8,128)(2,1)} fusion(f32[4,2,64,256]{3,2,1,0:T(8,128)S(1)} %bitcast.102, bf16[4,2,64,256]{3,2,1,0:T(8,128)(2,1)S(1)} %copy-done.3), kind=kLoop, calls=%fused_computation.71 | loop fusion | flops 393216 | bytes 1048576 | tf_op jit(solution)/shard_map/convert_element_type | solution.py:95
  (27 shorter events, 0.5 us)
Async XLA Ops:
  0.0 42.6 %copy-start = (bf16[256,256]{1,0:T(8,128)(2,1)S(1)}, bf16[256,256]{1,0:T(8,128)(2,1)}, u32[]{:S(2)}) copy-start(bf16[256,256]{1,0:T(8,128)(2,1)} %param.35) | copy-start | bytes 393220
  0.0 10.0 %copy-start.4 = (f32[25,256]{1,0:T(8,128)S(1)}, f32[25,256]{1,0:T(8,128)}, u32[]{:S(2)}) copy-start(f32[25,256]{1,0:T(8,128)} %param.36) | copy-start | bytes 76804
  1.0 10.4 %collective-permute-start = (bf16[4,1,64,256]{3,2,1,0:T(8,128)(2,1)S(1)}, bf16[4,1,64,256]{3,2,1,0:T(8,128)(2,1)S(1)}, u32[]{:S(2)}, u32[]{:S(2)}) collective-permute-start(bf16[4,1,64,256]{3,2,1,0:T(8,128)(2,1)S(1)} %get-tuple-element.191), channel_id=1, source_target_pairs={{0,1},{1,2},{2,3},{4,5},{5,6},{6,7},{8,9},{9,10},{10,11},{12,13},{... | collective-permute-start | bytes 393224 | tf_op jit(solution)/shard_map/ppermute | solution.py:14
  5.4 7.8 %collective-permute-start.1 = (bf16[4,1,64,256]{3,2,1,0:T(8,128)(2,1)S(1)}, bf16[4,1,64,256]{3,2,1,0:T(8,128)(2,1)S(1)}, u32[]{:S(2)}, u32[]{:S(2)}) collective-permute-start(bf16[4,1,64,256]{3,2,1,0:T(8,128)(2,1)S(1)} %get-tuple-element.192), channel_id=1, source_target_pairs={{1,0},{2,1},{3,2},{5,4},{6,5},{7,6},{9,8},{10,9},{11,10},{13,12},{... | collective-permute-start | bytes 393224 | tf_op jit(solution)/shard_map/ppermute | solution.py:15
  10.0 1.5 %copy-start.1 = (bf16[4,2,64,256]{3,2,1,0:T(8,128)(2,1)S(1)}, bf16[4,2,64,256]{3,2,1,0:T(8,128)(2,1)}, u32[]{:S(2)}) copy-start(bf16[4,2,64,256]{3,2,1,0:T(8,128)(2,1)} %param.32) | copy-start | bytes 786436
  13.4 1.3 %copy-start.2 = (bf16[9,256,256]{2,1,0:T(8,128)(2,1)S(1)}, bf16[9,256,256]{2,1,0:T(8,128)(2,1)}, u32[]{:S(2)}) copy-start(bf16[9,256,256]{2,1,0:T(8,128)(2,1)} %param.34) | copy-start | bytes 3538948
  16.6 26.1 %copy-start.3 = (bf16[4,2,64,256]{3,2,1,0:T(8,128)(2,1)S(1)}, bf16[4,2,64,256]{3,2,1,0:T(8,128)(2,1)}, u32[]{:S(2)}) copy-start(bf16[4,2,64,256]{3,2,1,0:T(8,128)(2,1)} %param.33) | copy-start | bytes 786436
  16.8 17.8 %collective-permute-start.3 = (bf16[4,2,64,256]{3,2,1,0:T(8,128)(2,1)S(1)}, bf16[4,2,64,256]{3,2,1,0:T(8,128)(2,1)S(1)}, u32[]{:S(2)}, u32[]{:S(2)}) collective-permute-start(bf16[4,2,64,256]{3,2,1,0:T(8,128)(2,1)S(1)} %bitcast.119), channel_id=1, source_target_pairs={{4,0},{8,4},{12,8},{16,12},{20,16},{24,20},{28,24},{32,28},{36,32}... | collective-permute-start | bytes 786440 | tf_op jit(solution)/shard_map/ppermute | solution.py:15
  31.3 11.3 %collective-permute-start.2 = (bf16[4,2,64,256]{3,2,1,0:T(8,128)(2,1)S(1)}, bf16[4,2,64,256]{3,2,1,0:T(8,128)(2,1)S(1)}, u32[]{:S(2)}, u32[]{:S(2)}) collective-permute-start(bf16[4,2,64,256]{3,2,1,0:T(8,128)(2,1)S(1)} %bitcast.120), channel_id=1, source_target_pairs={{0,4},{4,8},{8,12},{12,16},{16,20},{20,24},{24,28},{28,32},{32,36}... | collective-permute-start | bytes 786440 | tf_op jit(solution)/shard_map/ppermute | solution.py:14
  44.6 17.1 %collective-permute-start.4 = (f32[4,2,64,256]{3,2,1,0:T(8,128)S(1)}, f32[4,2,64,256]{3,2,1,0:T(8,128)S(1)}, u32[]{:S(2)}, u32[]{:S(2)}) collective-permute-start(f32[4,2,64,256]{3,2,1,0:T(8,128)S(1)} %get-tuple-element.155), channel_id=1, source_target_pairs={{0,4},{4,8},{8,12},{12,16},{16,20},{20,24},{24,28},{28,32},{32,36}... | collective-permute-start | bytes 1572872 | tf_op jit(solution)/shard_map/ppermute | solution.py:14
  46.6 16.9 %collective-permute-start.5 = (f32[4,2,64,256]{3,2,1,0:T(8,128)S(1)}, f32[4,2,64,256]{3,2,1,0:T(8,128)S(1)}, u32[]{:S(2)}, u32[]{:S(2)}) collective-permute-start(f32[4,2,64,256]{3,2,1,0:T(8,128)S(1)} %get-tuple-element.156), channel_id=1, source_target_pairs={{4,0},{8,4},{12,8},{16,12},{20,16},{24,20},{28,24},{32,28},{36,32}... | collective-permute-start | bytes 1572872 | tf_op jit(solution)/shard_map/ppermute | solution.py:15
  63.7 4.4 %collective-permute-start.7 = (bf16[4,1,64,256]{3,2,1,0:T(8,128)(2,1)S(1)}, bf16[4,1,64,256]{3,2,1,0:T(8,128)(2,1)S(1)}, u32[]{:S(2)}, u32[]{:S(2)}) collective-permute-start(bf16[4,1,64,256]{3,2,1,0:T(8,128)(2,1)S(1)} %get-tuple-element.183), channel_id=1, source_target_pairs={{0,1},{1,2},{2,3},{4,5},{5,6},{6,7},{8,9},{9,10},{10,11},{12,13},{... | collective-permute-start | bytes 393224 | tf_op jit(solution)/shard_map/ppermute | solution.py:14
  66.2 7.8 %collective-permute-start.6 = (bf16[4,1,64,256]{3,2,1,0:T(8,128)(2,1)S(1)}, bf16[4,1,64,256]{3,2,1,0:T(8,128)(2,1)S(1)}, u32[]{:S(2)}, u32[]{:S(2)}) collective-permute-start(bf16[4,1,64,256]{3,2,1,0:T(8,128)(2,1)S(1)} %get-tuple-element.184), channel_id=1, source_target_pairs={{1,0},{2,1},{3,2},{5,4},{6,5},{7,6},{9,8},{10,9},{11,10},{13,12},{... | collective-permute-start | bytes 393224 | tf_op jit(solution)/shard_map/ppermute | solution.py:15
where the time goes:
time: 78.3 us; the launch traced here: 77.8 us
  starting transfers between devices  36.5 us (47%)
  waiting for transfers between devices  25.8 us (33%)
  matrix products  6.81 us (9%)
  local copies, waits for them, and re-layouts  4.48 us (6%)
  other arithmetic  3.71 us (5%)
    ppermute x4, starting transfers between devices, extended_2(): after = lax.ppermute(initial, axis, down)  25.9 us
    ppermute x4, waiting for transfers between devices, extended_2(): before = lax.ppermute(last, axis, up)  15.6 us
    ppermute x4, starting transfers between devices, extended_2(): before = lax.ppermute(last, axis, up)  10.7 us
    ppermute x4, waiting for transfers between devices, extended_2(): after = lax.ppermute(initial, axis, down)  10.2 us
    dot_general x18, matrix products, convolve(): jnp.dot(shifted.reshape(-1, channels), matrix, preferred_element_type=jnp...  4.39 us
    slice x6, local copies, waits for them, and re-layouts, convolve(): jnp.roll(padded[:, lat_step:lat_step + row_count], 1 - lon_step, axis=2)  2.08 us
    dot_general x9, matrix products, pick_rows(): picked = jnp.dot(onehot, mixing, precision=lax.Precision.HIGHEST)  1.72 us
  transfers between devices with their start and end apart: 8, of which 6 were waited for; matrix products, arithmetic and copies ran while one was open for 6% of the time, Pallas kernels for 0%

commit v1 on v0

v1 whole, which is shorter than its diff:
```python
import jax
import jax.numpy as jnp
from jax import lax
from jax.experimental import pallas as pl
from jax.experimental.pallas import tpu as pltpu
from jax.sharding import PartitionSpec as P

VMEM = pl.BlockSpec(memory_space=pltpu.VMEM)
SMEM = pl.BlockSpec(memory_space=pltpu.SMEM)
REACH = 4


def shift(value, axis, step):
    size = lax.axis_size(axis)
    return lax.ppermute(
        value, axis, [(i, i + step) for i in range(size) if 0 <= i + step < size]
    )


def taps(rows, weight_ref, transposed):
    summed = []
    for lon_tap in range(3):
        total = None
        for lat_tap in range(3):
            value = jnp.concatenate([r[lat_tap] for r in rows], axis=0)
            matrix = weight_ref[3 * lat_tap + lon_tap]
            term = lax.dot_general(
                value,
                matrix,
                (((1,), (1 if transposed else 0,)), ((), ())),
                preferred_element_type=jnp.float32,
            )
            total = term if total is None else total + term
        summed.append(total)
    return summed


def rolled(value, lon_count, step):
    split = value.reshape(-1, lon_count, value.shape[-1])
    return pltpu.roll(split, step % lon_count, axis=1).reshape(value.shape)


def flat(value):
    return value.reshape(-1, value.shape[-1])


def conv_kernel(x_ref, before_ref, after_ref, weight_ref, out_ref):
    frames, _, lon_count, channels = x_ref.shape
    first, second = flat(x_ref[:, 0]), flat(x_ref[:, 1])
    before, after = flat(before_ref[...]), flat(after_ref[...])
    low, mid, high = taps(
        [(before, first, second), (first, second, after)], weight_ref, False
    )
    total = mid + rolled(low, lon_count, 1) + rolled(high, lon_count, -1)
    total = total.astype(out_ref.dtype).reshape(2, frames, lon_count, channels)
    out_ref[:, 0] = total[0]
    out_ref[:, 1] = total[1]


def back_kernel(x_ref, before_ref, after_ref, weight_ref, cot_ref, out_ref):
    frames, _, lon_count, channels = x_ref.shape
    first, second = flat(x_ref[:, 0]), flat(x_ref[:, 1])
    before, after = flat(before_ref[...]), flat(after_ref[...])
    low, mid, high = taps(
        [(second, first, before), (after, second, first)], weight_ref, True
    )
    total = mid + rolled(low, lon_count, -1) + rolled(high, lon_count, 1)
    total = total.reshape(2, frames, lon_count, channels)
    for row in range(2):
        out_ref[:, row] = (cot_ref[:, row].astype(jnp.float32) + total[row]).astype(out_ref.dtype)


def start_of(offsets_ref, frame):
    total_frames = offsets_ref.shape[0]
    inside = jnp.clip(frame, 0, total_frames - 1)
    return jnp.clip(inside - offsets_ref[inside], 0, total_frames - 5)


def mid_kernel(offsets_ref, mixing_ref, left_ref, own_ref, right_ref, cot_ref, proj_ref, out_ref, near_ref):
    frames, row_count, lon_count, channels = own_ref.shape
    first_frame = lax.axis_index("tm") * frames
    near_ref[:REACH] = left_ref[...]
    near_ref[REACH : REACH + frames] = own_ref[...]
    near_ref[REACH + frames :] = right_ref[...]
    hidden = lax.dot_general(
        flat(cot_ref[...]), proj_ref[...], (((1,), (1,)), ((), ())), preferred_element_type=jnp.float32
    ).reshape(own_ref.shape)
    for frame in range(frames):
        start = start_of(offsets_ref, first_frame + frame)
        place = first_frame + frame - start
        base = start - first_frame + REACH
        for row in range(row_count):
            pre = jnp.zeros((lon_count, channels), jnp.float32)
            for j in range(5):
                weight = mixing_ref[pl.ds(5 * place + j, 1), :]
                pre = pre + weight * near_ref[base + j, row].astype(jnp.float32)
            sigma = jax.nn.sigmoid(pre)
            slope = sigma * (1.0 + pre * (1.0 - sigma))
            out_ref[frame, row] = (hidden[frame, row] * slope).astype(out_ref.dtype)


def sum_kernel(offsets_ref, mixing_ref, left_ref, own_ref, right_ref, out_ref, top_ref, bottom_ref):
    frames, row_count, lon_count, channels = own_ref.shape
    first_frame = lax.axis_index("tm") * frames
    total_frames = offsets_ref.shape[0]
    starts = [start_of(offsets_ref, first_frame + k - REACH) for k in range(frames + 2 * REACH)]
    for frame in range(frames):
        weights = []
        for k in range(frame, frame + 2 * REACH + 1):
            source = first_frame + k - REACH
            slot = first_frame + frame - starts[k]
            good = (slot >= 0) & (slot <= 4) & (source >= 0) & (source < total_frames)
            place = source - starts[k]
            row_id = jnp.where(good, 5 * place + slot, 0)
            weight = mixing_ref[pl.ds(row_id, 1), :]
            weights.append((k, jnp.where(good, weight, 0.0)))
        for row in range(row_count):
            total = jnp.zeros((lon_count, channels), jnp.float32)
            for k, weight in weights:
                if k < REACH:
                    value = left_ref[k, row]
                elif k < REACH + frames:
                    value = own_ref[k - REACH, row]
                else:
                    value = right_ref[k - REACH - frames, row]
                total = total + weight * value.astype(jnp.float32)
            rounded = total.astype(out_ref.dtype)
            out_ref[frame, row] = rounded
            if row == 0:
                top_ref[frame] = rounded
            if row == row_count - 1:
                bottom_ref[frame] = rounded


def call(kernel, out_shapes, specs, cost, **extra):
    return pl.pallas_call(
        kernel,
        out_shape=out_shapes,
        in_specs=specs,
        out_specs=jax.tree.map(lambda _: VMEM, out_shapes),
        compiler_params=pltpu.CompilerParams(vmem_limit_bytes=40 * 1024 * 1024),
        cost_estimate=pl.CostEstimate(flops=cost[0], bytes_accessed=cost[1], transcendentals=0),
        **extra,
    )


def body(trajectory, cotangent, conv_weight, proj_weight, mixing, offsets):
    frames, row_count, lon_count, channels = trajectory.shape
    block = jax.ShapeDtypeStruct(trajectory.shape, jnp.bfloat16)
    edge = jax.ShapeDtypeStruct((frames, lon_count, channels), jnp.bfloat16)
    conv_cost = (2 * 9 * frames * row_count * lon_count * channels * channels, 2_000_000)
    before = shift(trajectory[:, row_count - 1], "lat", 1)
    after = shift(trajectory[:, 0], "lat", -1)
    conv_out = call(conv_kernel, block, [VMEM] * 4, conv_cost)(trajectory, before, after, conv_weight)
    left, right = shift(conv_out, "tm", 1), shift(conv_out, "tm", -1)
    g_pre = call(
        mid_kernel, block, [SMEM] + [VMEM] * 6, (80_000_000, 1_400_000),
        scratch_shapes=[pltpu.VMEM((frames + 2 * REACH, row_count, lon_count, channels), jnp.bfloat16)],
    )(offsets, mixing, left, conv_out, right, cotangent, proj_weight)
    left, right = shift(g_pre, "tm", 1), shift(g_pre, "tm", -1)
    conv_grad, top, bottom = call(
        sum_kernel, (block, edge, edge), [SMEM] + [VMEM] * 4, (10_000_000, 1_400_000)
    )(offsets, mixing, left, g_pre, right)
    before, after = shift(bottom, "lat", 1), shift(top, "lat", -1)
    return call(back_kernel, block, [VMEM] * 5, conv_cost)(conv_grad, before, after, conv_weight, cotangent)


def solution(mesh):
    in_specs = (P("tm", "lat", None, None), P("tm", "lat", None, None), P(), P(), P(), P())
    out_specs = P("tm", "lat", None, None)
    return jax.shard_map(body, mesh=mesh, in_specs=in_specs, out_specs=out_specs, check_vma=False)
```

time: 78.3 us -> 71.2 us (0.909)
  matrix products: 6.81 us -> 0 us
  Pallas kernels: 0 us -> 4.47 us
  other arithmetic: 3.71 us -> 0 us
  waiting for transfers between devices: 25.8 us -> 27.1 us
  local copies, waits for them, and re-layouts: 4.48 us -> 3.28 us
    dot_general x28 -> x0, matrix products: 6.81 us -> none  [the longest x18 4.39 us: convolve(): jnp.dot(shifted.reshape(-1, channels), matrix, preferred_element_type=jnp...]
    pallas_call x0 -> x4, Pallas kernels: none -> 4.47 us  [the longest x1 1.52 us: body(): call(back_kernel, block, [VMEM] * 5, conv_cost)]
    slice x10 -> x0, local copies, waits for them, and re-layouts: 3.17 us -> none  [the longest x6 2.08 us: convolve(): jnp.roll(padded[:, lat_step:lat_step + row_count], 1 - lon_step, axis=2)]
    ppermute x8, waiting for transfers between devices: 25.8 us -> 27.1 us  [shift(): lax.ppermute(value, axis, [(i, i + step) for i in range(size) if 0 <= i +...]
    unnamed x11 -> x14, local copies, waits for them, and re-layouts: 1.11 us -> 2.24 us
    squeeze x0 -> x1, local copies, waits for them, and re-layouts: none -> 1.04 us  [body(): after = shift(trajectory[:, 0], 'lat', -1)]
    scatter-add x7 -> x0, other arithmetic: 0.99 us -> none  [body(): extended.at[lag_index:lag_index + frame_count]]
    concatenate x10 -> x0, other arithmetic: 0.91 us -> none  [the longest x5 0.4 us: convolve(): jnp.roll(padded[:, 2 - lat_step:2 - lat_step + row_count], lon_step - 1,...]
  transfers between devices with their start and end apart: 8 -> 8, of which waited for: 6 -> 7; matrix products, arithmetic and copies ran while one was open for 6% -> 0% of each run, Pallas kernels for 0% -> 0%
where the time goes in v1:
time: 71.2 us; the launch traced here: 70.8 us
  starting transfers between devices  35.8 us (50%)
  waiting for transfers between devices  27.1 us (38%)
  Pallas kernels  4.47 us (6%)
  local copies, waits for them, and re-layouts  3.28 us (5%)
    ppermute x8, starting transfers between devices, shift(): lax.ppermute(value, axis, [(i, i + step) for i in range(size) if 0 <= i +...  35.8 us
    ppermute x8, waiting for transfers between devices, shift(): lax.ppermute(value, axis, [(i, i + step) for i in range(size) if 0 <= i +...  27.1 us
    unnamed x14, local copies, waits for them, and re-layouts  2.24 us
    pallas_call x1, Pallas kernels, body(): call(back_kernel, block, [VMEM] * 5, conv_cost)  1.52 us
  transfers between devices with their start and end apart: 8, of which 7 were waited for; matrix products, arithmetic and copies ran while one was open for 0% of the time, Pallas kernels for 0%

profile of v1, /device:TPU:3, one launch (start us, length us, event | category | flops | bytes accessed | tf_op | source)
XLA Modules:
  0.0 70.8 jit_solution(1568248019377439833)
XLA Ops:
  0.0 0.0 copy-start.1
  0.0 0.0 copy-start.2
  0.0 0.0 copy-start.3
  0.0 1.0 %slice_bitcast_fusion = (bf16[4,64,256]{2,1,0:T(8,128)(2,1)S(1)}, bf16[4,64,256]{2,1,0:T(8,128)(2,1)S(1)}) fusion(bf16[4,2,64,256]{3,2,1,0:T(8,128)(2,1)} %x_ref.1), kind=kLoop, calls=%fused_computation | loop fusion | bytes 524288 | tf_op jit(solution)/shard_map/squeeze | solution.py:153
  1.1 0.0 copy-start.4
  1.1 2.6 %collective-permute-start.1 = (bf16[4,64,256]{2,1,0:T(8,128)(2,1)S(1)}, bf16[4,64,256]{2,1,0:T(8,128)(2,1)S(1)}, u32[]{:S(2)}, u32[]{:S(2)}) collective-permute-start(bf16[4,64,256]{2,1,0:T(8,128)(2,1)S(1)} %get-tuple-element.11), channel_id=1, source_target_pairs={{1,0},{2,1},{3,2},{5,4},{6,5},{7,6},{9,8},{10,9},{11,10},{13,12},{... | collective-permute-start | bytes 393224 | tf_op jit(solution)/shard_map/ppermute | solution.py:15
  3.7 4.5 %collective-permute-start = (bf16[4,64,256]{2,1,0:T(8,128)(2,1)S(1)}, bf16[4,64,256]{2,1,0:T(8,128)(2,1)S(1)}, u32[]{:S(2)}, u32[]{:S(2)}) collective-permute-start(bf16[4,64,256]{2,1,0:T(8,128)(2,1)S(1)} %get-tuple-element.12), channel_id=1, source_target_pairs={{0,1},{1,2},{2,3},{4,5},{5,6},{6,7},{8,9},{9,10},{10,11},{12,13},{... | collective-permute-start | bytes 393224 | tf_op jit(solution)/shard_map/ppermute | solution.py:15
  8.1 0.7 %collective-permute-done.1.after_ref = bf16[4,64,256]{2,1,0:T(8,128)(2,1)S(1)} collective-permute-done((bf16[4,64,256]{2,1,0:T(8,128)(2,1)S(1)}, bf16[4,64,256]{2,1,0:T(8,128)(2,1)S(1)}, u32[]{:S(2)}, u32[]{:S(2)}) %collective-permute-start.1) | collective-permute-done | bytes 131104 | tf_op jit(solution)/shard_map/ppermute | solution.py:15
  8.9 1.2 %collective-permute-done.before_ref = bf16[4,64,256]{2,1,0:T(8,128)(2,1)S(1)} collective-permute-done((bf16[4,64,256]{2,1,0:T(8,128)(2,1)S(1)}, bf16[4,64,256]{2,1,0:T(8,128)(2,1)S(1)}, u32[]{:S(2)}, u32[]{:S(2)}) %collective-permute-start) | collective-permute-done | bytes 131104 | tf_op jit(solution)/shard_map/ppermute | solution.py:15
  10.1 0.0 copy-start
  10.1 0.9 %copy-done = bf16[4,2,64,256]{3,2,1,0:T(8,128)(2,1)S(1)} copy-done((bf16[4,2,64,256]{3,2,1,0:T(8,128)(2,1)S(1)}, bf16[4,2,64,256]{3,2,1,0:T(8,128)(2,1)}, u32[]{:S(2)}) %copy-start) | copy-done | bytes 262168
  11.0 0.0 copy-start.5
  11.0 1.3 %copy-done.5 = bf16[9,256,256]{2,1,0:T(8,128)(2,1)S(1)} copy-done((bf16[9,256,256]{2,1,0:T(8,128)(2,1)S(1)}, bf16[9,256,256]{2,1,0:T(8,128)(2,1)}, u32[]{:S(2)}) %copy-start.5) | copy-done | bytes 1179672
  12.3 0.8 %shard_map.64.own_ref = bf16[4,2,64,256]{3,2,1,0:T(8,128)(2,1)S(1)} custom-call(bf16[4,2,64,256]{3,2,1,0:T(8,128)(2,1)S(1)} %copy-done, bf16[4,64,256]{2,1,0:T(8,128)(2,1)S(1)} %collective-permute-done.before_ref, bf16[4,64,256]{2,1,0:T(8,128)(2,1)S(1)} %collective-permute-done.1.after_ref, bf16[9,256,256]{2,1,0:T(8,128)(2,1)S(1)} %copy-done.5), custom_call_target="tpu_custom_call" | custom-call | flops 603979776 | bytes 2000000 | tf_op jit(solution)/shard_map/pallas_call | solution.py:154
  13.1 0.0 copy-start.6
  13.1 13.7 %collective-permute-start.3 = (bf16[4,2,64,256]{3,2,1,0:T(8,128)(2,1)S(1)}, bf16[4,2,64,256]{3,2,1,0:T(8,128)(2,1)S(1)}, u32[]{:S(2)}, u32[]{:S(2)}) collective-permute-start(bf16[4,2,64,256]{3,2,1,0:T(8,128)(2,1)S(1)} %shard_map.64.own_ref), channel_id=1, source_target_pairs={{4,0},{8,4},{12,8},{16,12},{20,16},{24,20},{28,24},{32,28},{36,32}... | collective-permute-start | bytes 786440 | tf_op jit(solution)/shard_map/ppermute | solution.py:15
  26.8 1.9 %collective-permute-start.2 = (bf16[4,2,64,256]{3,2,1,0:T(8,128)(2,1)S(1)}, bf16[4,2,64,256]{3,2,1,0:T(8,128)(2,1)S(1)}, u32[]{:S(2)}, u32[]{:S(2)}) collective-permute-start(bf16[4,2,64,256]{3,2,1,0:T(8,128)(2,1)S(1)} %shard_map.64.own_ref), channel_id=1, source_target_pairs={{0,4},{4,8},{8,12},{12,16},{16,20},{20,24},{24,28},{28,32},{32,36}... | collective-permute-start | bytes 786440 | tf_op jit(solution)/shard_map/ppermute | solution.py:15
  28.8 1.5 %collective-permute-done.3.right_ref = bf16[4,2,64,256]{3,2,1,0:T(8,128)(2,1)S(1)} collective-permute-done((bf16[4,2,64,256]{3,2,1,0:T(8,128)(2,1)S(1)}, bf16[4,2,64,256]{3,2,1,0:T(8,128)(2,1)S(1)}, u32[]{:S(2)}, u32[]{:S(2)}) %collective-permute-start.3) | collective-permute-done | bytes 262176 | tf_op jit(solution)/shard_map/ppermute | solution.py:15
  30.3 8.3 %collective-permute-done.2.left_ref = bf16[4,2,64,256]{3,2,1,0:T(8,128)(2,1)S(1)} collective-permute-done((bf16[4,2,64,256]{3,2,1,0:T(8,128)(2,1)S(1)}, bf16[4,2,64,256]{3,2,1,0:T(8,128)(2,1)S(1)}, u32[]{:S(2)}, u32[]{:S(2)}) %collective-permute-start.2) | collective-permute-done | bytes 262176 | tf_op jit(solution)/shard_map/ppermute | solution.py:15
  38.6 0.0 copy-done.1
  38.6 0.0 copy-done.2
  38.6 0.0 copy-done.3
  38.6 0.0 copy-done.4
  38.7 1.1 %shard_map.65.own_ref = bf16[4,2,64,256]{3,2,1,0:T(8,128)(2,1)S(1)} custom-call(s32[512]{0:T(512)S(1)} %copy-done.4, f32[25,256]{1,0:T(8,128)S(1)} %copy-done.3, bf16[4,2,64,256]{3,2,1,0:T(8,128)(2,1)S(1)} %collective-permute-done.2.left_ref, bf16[4,2,64,256]{3,2,1,0:T(8,128)(2,1)S(1)} %shard_map.64.own_ref, ...), custom_call_target="tpu_custom_call" | custom-call | flops 80000000 | bytes 1400000 | tf_op jit(solution)/shard_map/pallas_call | solution.py:156
  39.7 1.9 %collective-permute-start.5 = (bf16[4,2,64,256]{3,2,1,0:T(8,128)(2,1)S(1)}, bf16[4,2,64,256]{3,2,1,0:T(8,128)(2,1)S(1)}, u32[]{:S(2)}, u32[]{:S(2)}) collective-permute-start(bf16[4,2,64,256]{3,2,1,0:T(8,128)(2,1)S(1)} %shard_map.65.own_ref), channel_id=1, source_target_pairs={{4,0},{8,4},{12,8},{16,12},{20,16},{24,20},{28,24},{32,28},{36,32}... | collective-permute-start | bytes 786440 | tf_op jit(solution)/shard_map/ppermute | solution.py:15
  41.7 3.4 %collective-permute-start.4 = (bf16[4,2,64,256]{3,2,1,0:T(8,128)(2,1)S(1)}, bf16[4,2,64,256]{3,2,1,0:T(8,128)(2,1)S(1)}, u32[]{:S(2)}, u32[]{:S(2)}) collective-permute-start(bf16[4,2,64,256]{3,2,1,0:T(8,128)(2,1)S(1)} %shard_map.65.own_ref), channel_id=1, source_target_pairs={{0,4},{4,8},{8,12},{12,16},{16,20},{20,24},{24,28},{28,32},{32,36}... | collective-permute-start | bytes 786440 | tf_op jit(solution)/shard_map/ppermute | solution.py:15
  45.0 3.4 %collective-permute-done.5.right_ref = bf16[4,2,64,256]{3,2,1,0:T(8,128)(2,1)S(1)} collective-permute-done((bf16[4,2,64,256]{3,2,1,0:T(8,128)(2,1)S(1)}, bf16[4,2,64,256]{3,2,1,0:T(8,128)(2,1)S(1)}, u32[]{:S(2)}, u32[]{:S(2)}) %collective-permute-start.5) | collective-permute-done | bytes 262176 | tf_op jit(solution)/shard_map/ppermute | solution.py:15
  48.4 6.1 %collective-permute-done.4.left_ref = bf16[4,2,64,256]{3,2,1,0:T(8,128)(2,1)S(1)} collective-permute-done((bf16[4,2,64,256]{3,2,1,0:T(8,128)(2,1)S(1)}, bf16[4,2,64,256]{3,2,1,0:T(8,128)(2,1)S(1)}, u32[]{:S(2)}, u32[]{:S(2)}) %collective-permute-start.4) | collective-permute-done | bytes 262176 | tf_op jit(solution)/shard_map/ppermute | solution.py:15
  54.5 1.1 %shard_map.66 = (bf16[4,2,64,256]{3,2,1,0:T(8,128)(2,1)S(1)}, bf16[4,64,256]{2,1,0:T(8,128)(2,1)S(1)}, bf16[4,64,256]{2,1,0:T(8,128)(2,1)S(1)}) custom-call(s32[512]{0:T(512)S(1)} %copy-done.4, f32[25,256]{1,0:T(8,128)S(1)} %copy-done.3, bf16[4,2,64,256]{3,2,1,0:T(8,128)(2,1)S(1)} %collective-permute-done.4.left_ref, ...), custom_call_target="tpu_custom_call" | custom-call | flops 10000000 | bytes 1400000 | tf_op jit(solution)/shard_map/pallas_call | solution.py:161
  55.6 5.8 %collective-permute-start.6 = (bf16[4,64,256]{2,1,0:T(8,128)(2,1)S(1)}, bf16[4,64,256]{2,1,0:T(8,128)(2,1)S(1)}, u32[]{:S(2)}, u32[]{:S(2)}) collective-permute-start(bf16[4,64,256]{2,1,0:T(8,128)(2,1)S(1)} %get-tuple-element.9), channel_id=1, source_target_pairs={{0,1},{1,2},{2,3},{4,5},{5,6},{6,7},{8,9},{9,10},{10,11},{12,13},{... | collective-permute-start | bytes 393224 | tf_op jit(solution)/shard_map/ppermute | solution.py:15
  61.5 1.9 %collective-permute-start.7 = (bf16[4,64,256]{2,1,0:T(8,128)(2,1)S(1)}, bf16[4,64,256]{2,1,0:T(8,128)(2,1)S(1)}, u32[]{:S(2)}, u32[]{:S(2)}) collective-permute-start(bf16[4,64,256]{2,1,0:T(8,128)(2,1)S(1)} %get-tuple-element.10), channel_id=1, source_target_pairs={{1,0},{2,1},{3,2},{5,4},{6,5},{7,6},{9,8},{10,9},{11,10},{13,12},{... | collective-permute-start | bytes 393224 | tf_op jit(solution)/shard_map/ppermute | solution.py:15
  63.4 0.0 collective-permute-done.6.before_ref
  63.4 5.9 %collective-permute-done.7.after_ref = bf16[4,64,256]{2,1,0:T(8,128)(2,1)S(1)} collective-permute-done((bf16[4,64,256]{2,1,0:T(8,128)(2,1)S(1)}, bf16[4,64,256]{2,1,0:T(8,128)(2,1)S(1)}, u32[]{:S(2)}, u32[]{:S(2)}) %collective-permute-start.7) | collective-permute-done | bytes 131104 | tf_op jit(solution)/shard_map/ppermute | solution.py:15
  69.3 0.0 copy-done.6
  69.3 1.5 %shard_map.67 = bf16[4,2,64,256]{3,2,1,0:T(8,128)(2,1)} custom-call(bf16[4,2,64,256]{3,2,1,0:T(8,128)(2,1)S(1)} %get-tuple-element.8.x_ref, bf16[4,64,256]{2,1,0:T(8,128)(2,1)S(1)} %collective-permute-done.6.before_ref, bf16[4,64,256]{2,1,0:T(8,128)(2,1)S(1)} %collective-permute-done.7.after_ref, bf16[9,256,256]{2,1,0:T(8,128)(2,1)S(1)} %copy-done.6, ...), custom_call_target="tpu_custom_call" | custom-call | flops 603979776 | bytes 2000000 | tf_op jit(solution)/shard_map/pallas_call | solution.py:165
Async XLA Ops:
  0.0 38.6 %copy-start.1 = (bf16[4,2,64,256]{3,2,1,0:T(8,128)(2,1)S(1)}, bf16[4,2,64,256]{3,2,1,0:T(8,128)(2,1)}, u32[]{:S(2)}) copy-start(bf16[4,2,64,256]{3,2,1,0:T(8,128)(2,1)} %cot_ref.3) | copy-start | bytes 786436
  0.0 38.6 %copy-start.2 = (bf16[256,256]{1,0:T(8,128)(2,1)S(1)}, bf16[256,256]{1,0:T(8,128)(2,1)}, u32[]{:S(2)}) copy-start(bf16[256,256]{1,0:T(8,128)(2,1)} %proj_ref.1) | copy-start | bytes 393220
  0.0 38.6 %copy-start.3 = (f32[25,256]{1,0:T(8,128)S(1)}, f32[25,256]{1,0:T(8,128)}, u32[]{:S(2)}) copy-start(f32[25,256]{1,0:T(8,128)} %mixing_ref.3) | copy-start | bytes 76804
  1.1 37.6 %copy-start.4 = (s32[512]{0:T(512)S(1)}, s32[512]{0:T(512)}, u32[]{:S(2)}) copy-start(s32[512]{0:T(512)} %offsets_ref.3) | copy-start | bytes 6148
  1.1 7.8 %collective-permute-start.1 = (bf16[4,64,256]{2,1,0:T(8,128)(2,1)S(1)}, bf16[4,64,256]{2,1,0:T(8,128)(2,1)S(1)}, u32[]{:S(2)}, u32[]{:S(2)}) collective-permute-start(bf16[4,64,256]{2,1,0:T(8,128)(2,1)S(1)} %get-tuple-element.11), channel_id=1, source_target_pairs={{1,0},{2,1},{3,2},{5,4},{6,5},{7,6},{9,8},{10,9},{11,10},{13,12},{... | collective-permute-start | bytes 393224 | tf_op jit(solution)/shard_map/ppermute | solution.py:15
  3.7 6.4 %collective-permute-start = (bf16[4,64,256]{2,1,0:T(8,128)(2,1)S(1)}, bf16[4,64,256]{2,1,0:T(8,128)(2,1)S(1)}, u32[]{:S(2)}, u32[]{:S(2)}) collective-permute-start(bf16[4,64,256]{2,1,0:T(8,128)(2,1)S(1)} %get-tuple-element.12), channel_id=1, source_target_pairs={{0,1},{1,2},{2,3},{4,5},{5,6},{6,7},{8,9},{9,10},{10,11},{12,13},{... | collective-permute-start | bytes 393224 | tf_op jit(solution)/shard_map/ppermute | solution.py:15
  10.1 0.9 %copy-start = (bf16[4,2,64,256]{3,2,1,0:T(8,128)(2,1)S(1)}, bf16[4,2,64,256]{3,2,1,0:T(8,128)(2,1)}, u32[]{:S(2)}) copy-start(bf16[4,2,64,256]{3,2,1,0:T(8,128)(2,1)} %x_ref.1) | copy-start | bytes 786436
  11.0 1.3 %copy-start.5 = (bf16[9,256,256]{2,1,0:T(8,128)(2,1)S(1)}, bf16[9,256,256]{2,1,0:T(8,128)(2,1)}, u32[]{:S(2)}) copy-start(bf16[9,256,256]{2,1,0:T(8,128)(2,1)} %weight_ref.3) | copy-start | bytes 3538948
  13.1 56.2 %copy-start.6 = (bf16[9,256,256]{2,1,0:T(8,128)(2,1)S(1)}, bf16[9,256,256]{2,1,0:T(8,128)(2,1)}, u32[]{:S(2)}) copy-start(bf16[9,256,256]{2,1,0:T(8,128)(2,1)} %weight_ref.3) | copy-start | bytes 3538948
  13.1 17.2 %collective-permute-start.3 = (bf16[4,2,64,256]{3,2,1,0:T(8,128)(2,1)S(1)}, bf16[4,2,64,256]{3,2,1,0:T(8,128)(2,1)S(1)}, u32[]{:S(2)}, u32[]{:S(2)}) collective-permute-start(bf16[4,2,64,256]{3,2,1,0:T(8,128)(2,1)S(1)} %shard_map.64.own_ref), channel_id=1, source_target_pairs={{4,0},{8,4},{12,8},{16,12},{20,16},{24,20},{28,24},{32,28},{36,32}... | collective-permute-start | bytes 786440 | tf_op jit(solution)/shard_map/ppermute | solution.py:15
  26.8 11.8 %collective-permute-start.2 = (bf16[4,2,64,256]{3,2,1,0:T(8,128)(2,1)S(1)}, bf16[4,2,64,256]{3,2,1,0:T(8,128)(2,1)S(1)}, u32[]{:S(2)}, u32[]{:S(2)}) collective-permute-start(bf16[4,2,64,256]{3,2,1,0:T(8,128)(2,1)S(1)} %shard_map.64.own_ref), channel_id=1, source_target_pairs={{0,4},{4,8},{8,12},{12,16},{16,20},{20,24},{24,28},{28,32},{32,36}... | collective-permute-start | bytes 786440 | tf_op jit(solution)/shard_map/ppermute | solution.py:15
  39.7 8.7 %collective-permute-start.5 = (bf16[4,2,64,256]{3,2,1,0:T(8,128)(2,1)S(1)}, bf16[4,2,64,256]{3,2,1,0:T(8,128)(2,1)S(1)}, u32[]{:S(2)}, u32[]{:S(2)}) collective-permute-start(bf16[4,2,64,256]{3,2,1,0:T(8,128)(2,1)S(1)} %shard_map.65.own_ref), channel_id=1, source_target_pairs={{4,0},{8,4},{12,8},{16,12},{20,16},{24,20},{28,24},{32,28},{36,32}... | collective-permute-start | bytes 786440 | tf_op jit(solution)/shard_map/ppermute | solution.py:15
  41.7 12.9 %collective-permute-start.4 = (bf16[4,2,64,256]{3,2,1,0:T(8,128)(2,1)S(1)}, bf16[4,2,64,256]{3,2,1,0:T(8,128)(2,1)S(1)}, u32[]{:S(2)}, u32[]{:S(2)}) collective-permute-start(bf16[4,2,64,256]{3,2,1,0:T(8,128)(2,1)S(1)} %shard_map.65.own_ref), channel_id=1, source_target_pairs={{0,4},{4,8},{8,12},{12,16},{16,20},{20,24},{24,28},{28,32},{32,36}... | collective-permute-start | bytes 786440 | tf_op jit(solution)/shard_map/ppermute | solution.py:15
  55.6 7.8 %collective-permute-start.6 = (bf16[4,64,256]{2,1,0:T(8,128)(2,1)S(1)}, bf16[4,64,256]{2,1,0:T(8,128)(2,1)S(1)}, u32[]{:S(2)}, u32[]{:S(2)}) collective-permute-start(bf16[4,64,256]{2,1,0:T(8,128)(2,1)S(1)} %get-tuple-element.9), channel_id=1, source_target_pairs={{0,1},{1,2},{2,3},{4,5},{5,6},{6,7},{8,9},{9,10},{10,11},{12,13},{... | collective-permute-start | bytes 393224 | tf_op jit(solution)/shard_map/ppermute | solution.py:15
  61.5 7.8 %collective-permute-start.7 = (bf16[4,64,256]{2,1,0:T(8,128)(2,1)S(1)}, bf16[4,64,256]{2,1,0:T(8,128)(2,1)S(1)}, u32[]{:S(2)}, u32[]{:S(2)}) collective-permute-start(bf16[4,64,256]{2,1,0:T(8,128)(2,1)S(1)} %get-tuple-element.10), channel_id=1, source_target_pairs={{1,0},{2,1},{3,2},{5,4},{6,5},{7,6},{9,8},{10,9},{11,10},{13,12},{... | collective-permute-start | bytes 393224 | tf_op jit(solution)/shard_map/ppermute | solution.py:15

commit v2 on v1

v2 whole, which is shorter than its diff:
```python
import functools

import jax
import jax.numpy as jnp
from jax import lax
from jax.experimental import pallas as pl
from jax.experimental.pallas import tpu as pltpu
from jax.sharding import PartitionSpec as P

VMEM = pl.BlockSpec(memory_space=pltpu.VMEM)
SMEM = pl.BlockSpec(memory_space=pltpu.SMEM)
REACH = 4


def shift(value, axis, step):
    size = lax.axis_size(axis)
    return lax.ppermute(
        value, axis, [(i, i + step) for i in range(size) if 0 <= i + step < size]
    )


def swap(value, axis, offset):
    size = lax.axis_size(axis)
    pairs = [(i, i + 1) for i in range(offset, size - 1, 2)]
    return lax.ppermute(value, axis, pairs + [(j, i) for i, j in pairs])


def product(value, matrix, transposed):
    return lax.dot_general(
        value,
        matrix,
        (((1,), (1 if transposed else 0,)), ((), ())),
        preferred_element_type=jnp.float32,
    )


def rolled(value, lon_count, step):
    split = value.reshape(-1, lon_count, value.shape[-1])
    return pltpu.roll(split, step % lon_count, axis=1).reshape(value.shape)


def aligned(low, mid, high, lon_count, transposed):
    step = -1 if transposed else 1
    return mid + rolled(low, lon_count, step) + rolled(high, lon_count, -step)


def flat(value):
    return value.reshape(-1, value.shape[-1])


def local_kernel(transposed, x_ref, weight_ref, *refs):
    total_ref = refs[-1]
    lon_count = x_ref.shape[2]
    first, second = flat(x_ref[:, 0]), flat(x_ref[:, 1])
    half = first.shape[0]
    both = jnp.concatenate([first, second], axis=0)
    ahead, behind = (0, 2) if transposed else (2, 0)
    sums = [[], []]
    for lon_tap in range(3):
        middle = product(both, weight_ref[3 + lon_tap], transposed)
        sums[0].append(middle[:half] + product(second, weight_ref[3 * ahead + lon_tap], transposed))
        sums[1].append(middle[half:] + product(first, weight_ref[3 * behind + lon_tap], transposed))
    for row in range(2):
        total = aligned(*sums[row], lon_count, transposed)
        if transposed:
            total = total + flat(refs[0][:, row]).astype(jnp.float32)
        total_ref[row] = total


def halo_kernel(transposed, total_ref, far_ref, near_ref, weight_ref, out_ref):
    frames, lon_count, channels = far_ref.shape
    parity = lax.rem(lax.axis_index("lat"), 2)
    for row, edge_ref in ((1 - parity, near_ref), (parity, far_ref)):
        tap = 2 - 2 * row if transposed else 2 * row
        value = flat(edge_ref[...])
        parts = [product(value, weight_ref[3 * tap + lon_tap], transposed) for lon_tap in range(3)]
        total = total_ref[row] + aligned(*parts, lon_count, transposed)
        out_ref[:, row] = total.astype(out_ref.dtype).reshape(frames, lon_count, channels)


def start_of(offsets_ref, frame):
    total_frames = offsets_ref.shape[0]
    inside = jnp.clip(frame, 0, total_frames - 1)
    return jnp.clip(inside - offsets_ref[inside], 0, total_frames - 5)


def mid_kernel(offsets_ref, mixing_ref, left_ref, own_ref, right_ref, cot_ref, proj_ref, out_ref, near_ref):
    frames, row_count, lon_count, channels = own_ref.shape
    first_frame = lax.axis_index("tm") * frames
    near_ref[:REACH] = left_ref[...]
    near_ref[REACH : REACH + frames] = own_ref[...]
    near_ref[REACH + frames :] = right_ref[...]
    hidden = lax.dot_general(
        flat(cot_ref[...]), proj_ref[...], (((1,), (1,)), ((), ())), preferred_element_type=jnp.float32
    ).reshape(own_ref.shape)
    for frame in range(frames):
        start = start_of(offsets_ref, first_frame + frame)
        place = first_frame + frame - start
        base = start - first_frame + REACH
        for row in range(row_count):
            pre = jnp.zeros((lon_count, channels), jnp.float32)
            for j in range(5):
                weight = mixing_ref[pl.ds(5 * place + j, 1), :]
                pre = pre + weight * near_ref[base + j, row].astype(jnp.float32)
            sigma = jax.nn.sigmoid(pre)
            slope = sigma * (1.0 + pre * (1.0 - sigma))
            out_ref[frame, row] = (hidden[frame, row] * slope).astype(out_ref.dtype)


def sum_kernel(offsets_ref, mixing_ref, left_ref, own_ref, right_ref, out_ref, far_ref, near_ref):
    frames, row_count, lon_count, channels = own_ref.shape
    first_frame = lax.axis_index("tm") * frames
    total_frames = offsets_ref.shape[0]
    starts = [start_of(offsets_ref, first_frame + k - REACH) for k in range(frames + 2 * REACH)]
    for frame in range(frames):
        weights = []
        for k in range(frame, frame + 2 * REACH + 1):
            source = first_frame + k - REACH
            slot = first_frame + frame - starts[k]
            good = (slot >= 0) & (slot <= 4) & (source >= 0) & (source < total_frames)
            place = source - starts[k]
            row_id = jnp.where(good, 5 * place + slot, 0)
            weight = mixing_ref[pl.ds(row_id, 1), :]
            weights.append((k, jnp.where(good, weight, 0.0)))
        for row in range(row_count):
            total = jnp.zeros((lon_count, channels), jnp.float32)
            for k, weight in weights:
                if k < REACH:
                    value = left_ref[k, row]
                elif k < REACH + frames:
                    value = own_ref[k - REACH, row]
                else:
                    value = right_ref[k - REACH - frames, row]
                total = total + weight * value.astype(jnp.float32)
            out_ref[frame, row] = total.astype(out_ref.dtype)
    parity = lax.rem(lax.axis_index("lat"), 2)
    far_ref[...] = out_ref[:, parity]
    near_ref[...] = out_ref[:, 1 - parity]


def call(kernel, out_shapes, specs, cost, **extra):
    return pl.pallas_call(
        kernel,
        out_shape=out_shapes,
        in_specs=specs,
        out_specs=jax.tree.map(lambda _: VMEM, out_shapes),
        compiler_params=pltpu.CompilerParams(vmem_limit_bytes=24 * 1024 * 1024),
        cost_estimate=pl.CostEstimate(flops=cost[0], bytes_accessed=cost[1], transcendentals=0),
        **extra,
    )


def convolve(block, far, near, weight, transposed, *added):
    frames, row_count, lon_count, channels = block.shape
    half = 2 * 3 * frames * row_count * lon_count * channels * channels
    sums = jax.ShapeDtypeStruct((row_count, frames * lon_count, channels), jnp.float32)
    total = call(
        functools.partial(local_kernel, transposed), sums, [VMEM] * (2 + len(added)), (2 * half, 2_000_000)
    )(block, weight, *added)
    far, near = swap(far, "lat", 1), swap(near, "lat", 0)
    result = jax.ShapeDtypeStruct(block.shape, jnp.bfloat16)
    return call(functools.partial(halo_kernel, transposed), result, [VMEM] * 4, (half, 2_000_000))(
        total, far, near, weight
    )


def body(trajectory, cotangent, conv_weight, proj_weight, mixing, offsets):
    frames, row_count, lon_count, channels = trajectory.shape
    block = jax.ShapeDtypeStruct(trajectory.shape, jnp.bfloat16)
    edge = jax.ShapeDtypeStruct((frames, lon_count, channels), jnp.bfloat16)
    odd = lax.rem(lax.axis_index("lat"), 2) == 1
    top, bottom = trajectory[:, 0], trajectory[:, 1]
    far, near = jnp.where(odd, bottom, top), jnp.where(odd, top, bottom)
    conv_out = convolve(trajectory, far, near, conv_weight, False)
    right, left = shift(conv_out, "tm", -1), shift(conv_out, "tm", 1)
    g_pre = call(
        mid_kernel, block, [SMEM] + [VMEM] * 6, (80_000_000, 1_400_000),
        scratch_shapes=[pltpu.VMEM((frames + 2 * REACH, row_count, lon_count, channels), jnp.bfloat16)],
    )(offsets, mixing, left, conv_out, right, cotangent, proj_weight)
    right, left = shift(g_pre, "tm", -1), shift(g_pre, "tm", 1)
    conv_grad, far, near = call(
        sum_kernel, (block, edge, edge), [SMEM] + [VMEM] * 4, (10_000_000, 1_400_000)
    )(offsets, mixing, left, g_pre, right)
    return convolve(conv_grad, far, near, conv_weight, True, cotangent)


def solution(mesh):
    in_specs = (P("tm", "lat", None, None), P("tm", "lat", None, None), P(), P(), P(), P())
    out_specs = P("tm", "lat", None, None)
    return jax.shard_map(body, mesh=mesh, in_specs=in_specs, out_specs=out_specs, check_vma=False)
```

time: 71.2 us -> 63.6 us (0.89)
  the two profiles are of different devices: /device:TPU:3 before, /device:TPU:6 now
where the time goes in v2:
time: 63.6 us; the launch traced here: 63.2 us
  starting transfers between devices  31.1 us (49%)
  waiting for transfers between devices  23.9 us (38%)
  Pallas kernels  4.86 us (8%)
  local copies, waits for them, and re-layouts  2.24 us (4%)
  other arithmetic  0.99 us (2%)
    ppermute x4, starting transfers between devices, shift(): lax.ppermute(value, axis, [(i, i + step) for i in range(size) if 0 <= i +...  21.9 us
    ppermute x4, waiting for transfers between devices, shift(): lax.ppermute(value, axis, [(i, i + step) for i in range(size) if 0 <= i +...  19.1 us
    ppermute x4, starting transfers between devices, swap(): return lax.ppermute(value, axis, pairs + [(j, i) for i, j in pairs])  9.18 us
    ppermute x4, waiting for transfers between devices, swap(): return lax.ppermute(value, axis, pairs + [(j, i) for i, j in pairs])  4.82 us
    unnamed x14, local copies, waits for them, and re-layouts  2.24 us
    pallas_call x2, Pallas kernels, convolve(): call(functools.partial(halo_kernel, transposed), result, [VMEM] * 4, (hal...  1.49 us
  transfers between devices with their start and end apart: 8, of which 6 were waited for; matrix products, arithmetic and copies ran while one was open for 0% of the time, Pallas kernels for 2%

profile of v2, /device:TPU:6, one launch (start us, length us, event | category | flops | bytes accessed | tf_op | source)
XLA Modules:
  0.0 63.2 jit_solution(13585475183017781347)
XLA Ops:
  0.0 1.0 %fusion.1 = (bf16[4,64,256]{2,1,0:T(8,128)(2,1)S(1)}, bf16[4,64,256]{2,1,0:T(8,128)(2,1)S(1)}) fusion(pred[]{:T(512)S(6)} %eq.3, bf16[4,2,64,256]{3,2,1,0:T(8,128)(2,1)} %x_ref.1), kind=kLoop, calls=%fused_computation.3 | loop fusion | flops 131072 | bytes 524289 | tf_op jit(solution)/shard_map/jit(_where)/select_n | solution.py:173
  1.0 1.9 %collective-permute-start.1 = (bf16[4,64,256]{2,1,0:T(8,128)(2,1)S(1)}, bf16[4,64,256]{2,1,0:T(8,128)(2,1)S(1)}, u32[]{:S(2)}, u32[]{:S(2)}) collective-permute-start(bf16[4,64,256]{2,1,0:T(8,128)(2,1)S(1)} %get-tuple-element.11), channel_id=1, source_target_pairs={{0,1},{2,3},{1,0},{3,2},{4,5},{6,7},{5,4},{7,6},{8,9},{10,11},{9,8... | collective-permute-start | bytes 393224 | tf_op jit(solution)/shard_map/ppermute | solution.py:25
  2.9 3.4 %collective-permute-start = (bf16[4,64,256]{2,1,0:T(8,128)(2,1)S(1)}, bf16[4,64,256]{2,1,0:T(8,128)(2,1)S(1)}, u32[]{:S(2)}, u32[]{:S(2)}) collective-permute-start(bf16[4,64,256]{2,1,0:T(8,128)(2,1)S(1)} %get-tuple-element.12), channel_id=1, source_target_pairs={{1,2},{2,1},{5,6},{6,5},{9,10},{10,9},{13,14},{14,13},{17,18},{18,... | collective-permute-start | bytes 393224 | tf_op jit(solution)/shard_map/ppermute | solution.py:25
  6.3 0.0 copy-start
  6.4 1.3 %copy-done = bf16[9,256,256]{2,1,0:T(8,128)(2,1)S(1)} copy-done((bf16[9,256,256]{2,1,0:T(8,128)(2,1)S(1)}, bf16[9,256,256]{2,1,0:T(8,128)(2,1)}, u32[]{:S(2)}) %copy-start) | copy-done | bytes 1179672
  7.6 0.0 copy-start.2
  7.6 0.9 %copy-done.2 = bf16[4,2,64,256]{3,2,1,0:T(8,128)(2,1)S(1)} copy-done((bf16[4,2,64,256]{3,2,1,0:T(8,128)(2,1)S(1)}, bf16[4,2,64,256]{3,2,1,0:T(8,128)(2,1)}, u32[]{:S(2)}) %copy-start.2) | copy-done | bytes 262168
  8.6 0.0 copy-start.1
  8.6 0.6 shard_map.64.total_ref
  9.2 0.0 copy-start.3
  9.2 0.0 copy-start.4
  9.2 0.0 copy-start.5
  9.2 0.0 copy-start.6
  9.2 0.0 collective-permute-done.1.near_ref
  9.2 1.5 %collective-permute-done.far_ref = bf16[4,64,256]{2,1,0:T(8,128)(2,1)S(1)} collective-permute-done((bf16[4,64,256]{2,1,0:T(8,128)(2,1)S(1)}, bf16[4,64,256]{2,1,0:T(8,128)(2,1)S(1)}, u32[]{:S(2)}, u32[]{:S(2)}) %collective-permute-start) | collective-permute-done | bytes 131104 | tf_op jit(solution)/shard_map/ppermute | solution.py:25
  10.7 0.0 copy-done.1
  10.7 0.4 shard_map.65.own_ref
  11.1 14.1 %collective-permute-start.3 = (bf16[4,2,64,256]{3,2,1,0:T(8,128)(2,1)S(1)}, bf16[4,2,64,256]{3,2,1,0:T(8,128)(2,1)S(1)}, u32[]{:S(2)}, u32[]{:S(2)}) collective-permute-start(bf16[4,2,64,256]{3,2,1,0:T(8,128)(2,1)S(1)} %shard_map.65.own_ref), channel_id=1, source_target_pairs={{4,0},{8,4},{12,8},{16,12},{20,16},{24,20},{28,24},{32,28},{36,32}... | collective-permute-start | bytes 786440 | tf_op jit(solution)/shard_map/ppermute | solution.py:17
  25.2 1.9 %collective-permute-start.2 = (bf16[4,2,64,256]{3,2,1,0:T(8,128)(2,1)S(1)}, bf16[4,2,64,256]{3,2,1,0:T(8,128)(2,1)S(1)}, u32[]{:S(2)}, u32[]{:S(2)}) collective-permute-start(bf16[4,2,64,256]{3,2,1,0:T(8,128)(2,1)S(1)} %shard_map.65.own_ref), channel_id=1, source_target_pairs={{0,4},{4,8},{8,12},{12,16},{16,20},{20,24},{24,28},{28,32},{32,36}... | collective-permute-start | bytes 786440 | tf_op jit(solution)/shard_map/ppermute | solution.py:17
  27.2 1.9 %collective-permute-done.3.right_ref = bf16[4,2,64,256]{3,2,1,0:T(8,128)(2,1)S(1)} collective-permute-done((bf16[4,2,64,256]{3,2,1,0:T(8,128)(2,1)S(1)}, bf16[4,2,64,256]{3,2,1,0:T(8,128)(2,1)S(1)}, u32[]{:S(2)}, u32[]{:S(2)}) %collective-permute-start.3) | collective-permute-done | bytes 262176 | tf_op jit(solution)/shard_map/ppermute | solution.py:17
  29.1 8.6 %collective-permute-done.2.left_ref = bf16[4,2,64,256]{3,2,1,0:T(8,128)(2,1)S(1)} collective-permute-done((bf16[4,2,64,256]{3,2,1,0:T(8,128)(2,1)S(1)}, bf16[4,2,64,256]{3,2,1,0:T(8,128)(2,1)S(1)}, u32[]{:S(2)}, u32[]{:S(2)}) %collective-permute-start.2) | collective-permute-done | bytes 262176 | tf_op jit(solution)/shard_map/ppermute | solution.py:17
  37.7 0.0 copy-done.3
  37.7 0.0 copy-done.4
  37.7 0.0 copy-done.5
  37.7 0.0 copy-done.6
  37.7 1.1 %shard_map.66.own_ref = bf16[4,2,64,256]{3,2,1,0:T(8,128)(2,1)S(1)} custom-call(s32[512]{0:T(512)S(1)} %copy-done.6, f32[25,256]{1,0:T(8,128)S(1)} %copy-done.5, bf16[4,2,64,256]{3,2,1,0:T(8,128)(2,1)S(1)} %collective-permute-done.2.left_ref, bf16[4,2,64,256]{3,2,1,0:T(8,128)(2,1)S(1)} %shard_map.65.own_ref, ...), custom_call_target="tpu_custom_call" | custom-call | flops 80000000 | bytes 1400000 | tf_op jit(solution)/shard_map/pallas_call | solution.py:176
  38.8 1.9 %collective-permute-start.5 = (bf16[4,2,64,256]{3,2,1,0:T(8,128)(2,1)S(1)}, bf16[4,2,64,256]{3,2,1,0:T(8,128)(2,1)S(1)}, u32[]{:S(2)}, u32[]{:S(2)}) collective-permute-start(bf16[4,2,64,256]{3,2,1,0:T(8,128)(2,1)S(1)} %shard_map.66.own_ref), channel_id=1, source_target_pairs={{4,0},{8,4},{12,8},{16,12},{20,16},{24,20},{28,24},{32,28},{36,32}... | collective-permute-start | bytes 786440 | tf_op jit(solution)/shard_map/ppermute | solution.py:17
  40.7 3.9 %collective-permute-start.4 = (bf16[4,2,64,256]{3,2,1,0:T(8,128)(2,1)S(1)}, bf16[4,2,64,256]{3,2,1,0:T(8,128)(2,1)S(1)}, u32[]{:S(2)}, u32[]{:S(2)}) collective-permute-start(bf16[4,2,64,256]{3,2,1,0:T(8,128)(2,1)S(1)} %shard_map.66.own_ref), channel_id=1, source_target_pairs={{0,4},{4,8},{8,12},{12,16},{16,20},{20,24},{24,28},{28,32},{32,36}... | collective-permute-start | bytes 786440 | tf_op jit(solution)/shard_map/ppermute | solution.py:17
  44.7 2.4 %collective-permute-done.5.right_ref = bf16[4,2,64,256]{3,2,1,0:T(8,128)(2,1)S(1)} collective-permute-done((bf16[4,2,64,256]{3,2,1,0:T(8,128)(2,1)S(1)}, bf16[4,2,64,256]{3,2,1,0:T(8,128)(2,1)S(1)}, u32[]{:S(2)}, u32[]{:S(2)}) %collective-permute-start.5) | collective-permute-done | bytes 262176 | tf_op jit(solution)/shard_map/ppermute | solution.py:17
  47.1 6.1 %collective-permute-done.4.left_ref = bf16[4,2,64,256]{3,2,1,0:T(8,128)(2,1)S(1)} collective-permute-done((bf16[4,2,64,256]{3,2,1,0:T(8,128)(2,1)S(1)}, bf16[4,2,64,256]{3,2,1,0:T(8,128)(2,1)S(1)}, u32[]{:S(2)}, u32[]{:S(2)}) %collective-permute-start.4) | collective-permute-done | bytes 262176 | tf_op jit(solution)/shard_map/ppermute | solution.py:17
  53.2 1.1 %shard_map.67 = (bf16[4,2,64,256]{3,2,1,0:T(8,128)(2,1)S(1)}, bf16[4,64,256]{2,1,0:T(8,128)(2,1)S(1)}, bf16[4,64,256]{2,1,0:T(8,128)(2,1)S(1)}) custom-call(s32[512]{0:T(512)S(1)} %copy-done.6, f32[25,256]{1,0:T(8,128)S(1)} %copy-done.5, bf16[4,2,64,256]{3,2,1,0:T(8,128)(2,1)S(1)} %collective-permute-done.4.left_ref, ...), custom_call_target="tpu_custom_call" | custom-call | flops 10000000 | bytes 1400000 | tf_op jit(solution)/shard_map/pallas_call | solution.py:181
  54.3 1.9 %collective-permute-start.6 = (bf16[4,64,256]{2,1,0:T(8,128)(2,1)S(1)}, bf16[4,64,256]{2,1,0:T(8,128)(2,1)S(1)}, u32[]{:S(2)}, u32[]{:S(2)}) collective-permute-start(bf16[4,64,256]{2,1,0:T(8,128)(2,1)S(1)} %get-tuple-element.9), channel_id=1, source_target_pairs={{1,2},{2,1},{5,6},{6,5},{9,10},{10,9},{13,14},{14,13},{17,18},{18,... | collective-permute-start | bytes 393224 | tf_op jit(solution)/shard_map/ppermute | solution.py:25
  56.3 1.9 %collective-permute-start.7 = (bf16[4,64,256]{2,1,0:T(8,128)(2,1)S(1)}, bf16[4,64,256]{2,1,0:T(8,128)(2,1)S(1)}, u32[]{:S(2)}, u32[]{:S(2)}) collective-permute-start(bf16[4,64,256]{2,1,0:T(8,128)(2,1)S(1)} %get-tuple-element.10), channel_id=1, source_target_pairs={{0,1},{2,3},{1,0},{3,2},{4,5},{6,7},{5,4},{7,6},{8,9},{10,11},{9,8... | collective-permute-start | bytes 393224 | tf_op jit(solution)/shard_map/ppermute | solution.py:25
  58.2 0.6 shard_map.68.total_ref
  58.8 3.3 %collective-permute-done.6.far_ref = bf16[4,64,256]{2,1,0:T(8,128)(2,1)S(1)} collective-permute-done((bf16[4,64,256]{2,1,0:T(8,128)(2,1)S(1)}, bf16[4,64,256]{2,1,0:T(8,128)(2,1)S(1)}, u32[]{:S(2)}, u32[]{:S(2)}) %collective-permute-start.6) | collective-permute-done | bytes 131104 | tf_op jit(solution)/shard_map/ppermute | solution.py:25
  62.1 0.0 collective-permute-done.7.near_ref
  62.1 1.1 %shard_map.69 = bf16[4,2,64,256]{3,2,1,0:T(8,128)(2,1)} custom-call(f32[2,256,256]{2,1,0:T(8,128)S(1)} %shard_map.68.total_ref, bf16[4,64,256]{2,1,0:T(8,128)(2,1)S(1)} %collective-permute-done.6.far_ref, bf16[4,64,256]{2,1,0:T(8,128)(2,1)S(1)} %collective-permute-done.7.near_ref, bf16[9,256,256]{2,1,0:T(8,128)(2,1)S(1)} %copy-done.1), custom_call_target="tpu_custom_call" | custom-call | flops 201326592 | bytes 2000000 | tf_op jit(solution)/shard_map/pallas_call | solution.py:162
Async XLA Ops:
  1.0 8.2 %collective-permute-start.1 = (bf16[4,64,256]{2,1,0:T(8,128)(2,1)S(1)}, bf16[4,64,256]{2,1,0:T(8,128)(2,1)S(1)}, u32[]{:S(2)}, u32[]{:S(2)}) collective-permute-start(bf16[4,64,256]{2,1,0:T(8,128)(2,1)S(1)} %get-tuple-element.11), channel_id=1, source_target_pairs={{0,1},{2,3},{1,0},{3,2},{4,5},{6,7},{5,4},{7,6},{8,9},{10,11},{9,8... | collective-permute-start | bytes 393224 | tf_op jit(solution)/shard_map/ppermute | solution.py:25
  2.9 7.8 %collective-permute-start = (bf16[4,64,256]{2,1,0:T(8,128)(2,1)S(1)}, bf16[4,64,256]{2,1,0:T(8,128)(2,1)S(1)}, u32[]{:S(2)}, u32[]{:S(2)}) collective-permute-start(bf16[4,64,256]{2,1,0:T(8,128)(2,1)S(1)} %get-tuple-element.12), channel_id=1, source_target_pairs={{1,2},{2,1},{5,6},{6,5},{9,10},{10,9},{13,14},{14,13},{17,18},{18,... | collective-permute-start | bytes 393224 | tf_op jit(solution)/shard_map/ppermute | solution.py:25
  6.3 1.3 %copy-start = (bf16[9,256,256]{2,1,0:T(8,128)(2,1)S(1)}, bf16[9,256,256]{2,1,0:T(8,128)(2,1)}, u32[]{:S(2)}) copy-start(bf16[9,256,256]{2,1,0:T(8,128)(2,1)} %weight_ref.7) | copy-start | bytes 3538948
  7.6 0.9 %copy-start.2 = (bf16[4,2,64,256]{3,2,1,0:T(8,128)(2,1)S(1)}, bf16[4,2,64,256]{3,2,1,0:T(8,128)(2,1)}, u32[]{:S(2)}) copy-start(bf16[4,2,64,256]{3,2,1,0:T(8,128)(2,1)} %x_ref.1) | copy-start | bytes 786436
  8.6 2.1 %copy-start.1 = (bf16[9,256,256]{2,1,0:T(8,128)(2,1)S(1)}, bf16[9,256,256]{2,1,0:T(8,128)(2,1)}, u32[]{:S(2)}) copy-start(bf16[9,256,256]{2,1,0:T(8,128)(2,1)} %weight_ref.7) | copy-start | bytes 3538948
  9.2 28.6 %copy-start.3 = (bf16[4,2,64,256]{3,2,1,0:T(8,128)(2,1)S(1)}, bf16[4,2,64,256]{3,2,1,0:T(8,128)(2,1)}, u32[]{:S(2)}) copy-start(bf16[4,2,64,256]{3,2,1,0:T(8,128)(2,1)} %refs_0_.1) | copy-start | bytes 786436
  9.2 28.5 %copy-start.4 = (bf16[256,256]{1,0:T(8,128)(2,1)S(1)}, bf16[256,256]{1,0:T(8,128)(2,1)}, u32[]{:S(2)}) copy-start(bf16[256,256]{1,0:T(8,128)(2,1)} %proj_ref.1) | copy-start | bytes 393220
  9.2 28.5 %copy-start.5 = (f32[25,256]{1,0:T(8,128)S(1)}, f32[25,256]{1,0:T(8,128)}, u32[]{:S(2)}) copy-start(f32[25,256]{1,0:T(8,128)} %mixing_ref.3) | copy-start | bytes 76804
  9.2 28.5 %copy-start.6 = (s32[512]{0:T(512)S(1)}, s32[512]{0:T(512)}, u32[]{:S(2)}) copy-start(s32[512]{0:T(512)} %offsets_ref.3) | copy-start | bytes 6148
  11.1 18.0 %collective-permute-start.3 = (bf16[4,2,64,256]{3,2,1,0:T(8,128)(2,1)S(1)}, bf16[4,2,64,256]{3,2,1,0:T(8,128)(2,1)S(1)}, u32[]{:S(2)}, u32[]{:S(2)}) collective-permute-start(bf16[4,2,64,256]{3,2,1,0:T(8,128)(2,1)S(1)} %shard_map.65.own_ref), channel_id=1, source_target_pairs={{4,0},{8,4},{12,8},{16,12},{20,16},{24,20},{28,24},{32,28},{36,32}... | collective-permute-start | bytes 786440 | tf_op jit(solution)/shard_map/ppermute | solution.py:17
  25.2 12.5 %collective-permute-start.2 = (bf16[4,2,64,256]{3,2,1,0:T(8,128)(2,1)S(1)}, bf16[4,2,64,256]{3,2,1,0:T(8,128)(2,1)S(1)}, u32[]{:S(2)}, u32[]{:S(2)}) collective-permute-start(bf16[4,2,64,256]{3,2,1,0:T(8,128)(2,1)S(1)} %shard_map.65.own_ref), channel_id=1, source_target_pairs={{0,4},{4,8},{8,12},{12,16},{16,20},{20,24},{24,28},{28,32},{32,36}... | collective-permute-start | bytes 786440 | tf_op jit(solution)/shard_map/ppermute | solution.py:17
  38.8 8.3 %collective-permute-start.5 = (bf16[4,2,64,256]{3,2,1,0:T(8,128)(2,1)S(1)}, bf16[4,2,64,256]{3,2,1,0:T(8,128)(2,1)S(1)}, u32[]{:S(2)}, u32[]{:S(2)}) collective-permute-start(bf16[4,2,64,256]{3,2,1,0:T(8,128)(2,1)S(1)} %shard_map.66.own_ref), channel_id=1, source_target_pairs={{4,0},{8,4},{12,8},{16,12},{20,16},{24,20},{28,24},{32,28},{36,32}... | collective-permute-start | bytes 786440 | tf_op jit(solution)/shard_map/ppermute | solution.py:17
  40.7 12.5 %collective-permute-start.4 = (bf16[4,2,64,256]{3,2,1,0:T(8,128)(2,1)S(1)}, bf16[4,2,64,256]{3,2,1,0:T(8,128)(2,1)S(1)}, u32[]{:S(2)}, u32[]{:S(2)}) collective-permute-start(bf16[4,2,64,256]{3,2,1,0:T(8,128)(2,1)S(1)} %shard_map.66.own_ref), channel_id=1, source_target_pairs={{0,4},{4,8},{8,12},{12,16},{16,20},{20,24},{24,28},{28,32},{32,36}... | collective-permute-start | bytes 786440 | tf_op jit(solution)/shard_map/ppermute | solution.py:17
  54.3 7.8 %collective-permute-start.6 = (bf16[4,64,256]{2,1,0:T(8,128)(2,1)S(1)}, bf16[4,64,256]{2,1,0:T(8,128)(2,1)S(1)}, u32[]{:S(2)}, u32[]{:S(2)}) collective-permute-start(bf16[4,64,256]{2,1,0:T(8,128)(2,1)S(1)} %get-tuple-element.9), channel_id=1, source_target_pairs={{1,2},{2,1},{5,6},{6,5},{9,10},{10,9},{13,14},{14,13},{17,18},{18,... | collective-permute-start | bytes 393224 | tf_op jit(solution)/shard_map/ppermute | solution.py:25
  56.3 5.9 %collective-permute-start.7 = (bf16[4,64,256]{2,1,0:T(8,128)(2,1)S(1)}, bf16[4,64,256]{2,1,0:T(8,128)(2,1)S(1)}, u32[]{:S(2)}, u32[]{:S(2)}) collective-permute-start(bf16[4,64,256]{2,1,0:T(8,128)(2,1)S(1)} %get-tuple-element.10), channel_id=1, source_target_pairs={{0,1},{2,3},{1,0},{3,2},{4,5},{6,7},{5,4},{7,6},{8,9},{10,11},{9,8... | collective-permute-start | bytes 393224 | tf_op jit(solution)/shard_map/ppermute | solution.py:25

commit v3 on v2

--- a/solution.py
+++ b/solution.py
@@ -10,13 +10,6 @@
 VMEM = pl.BlockSpec(memory_space=pltpu.VMEM)
 SMEM = pl.BlockSpec(memory_space=pltpu.SMEM)
 REACH = 4
-
-
-def shift(value, axis, step):
-    size = lax.axis_size(axis)
-    return lax.ppermute(
-        value, axis, [(i, i + step) for i in range(size) if 0 <= i + step < size]
-    )
 
 
 def swap(value, axis, offset):
@@ -84,12 +77,19 @@
     return jnp.clip(inside - offsets_ref[inside], 0, total_frames - 5)
 
 
-def mid_kernel(offsets_ref, mixing_ref, left_ref, own_ref, right_ref, cot_ref, proj_ref, out_ref, near_ref):
+def gather(odd_ref, own_ref, even_ref, near_ref):
+    frames = own_ref.shape[0]
+    parity = lax.rem(lax.axis_index("tm"), 2)
+    span = REACH + frames
+    near_ref[pl.ds(span * parity, frames)] = odd_ref[...]
+    near_ref[REACH:span] = own_ref[...]
+    near_ref[pl.ds(span * (1 - parity), frames)] = even_ref[...]
+
+
+def mid_kernel(offsets_ref, mixing_ref, odd_ref, own_ref, even_ref, cot_ref, proj_ref, out_ref, near_ref):
     frames, row_count, lon_count, channels = own_ref.shape
     first_frame = lax.axis_index("tm") * frames
-    near_ref[:REACH] = left_ref[...]
-    near_ref[REACH : REACH + frames] = own_ref[...]
-    near_ref[REACH + frames :] = right_ref[...]
+    gather(odd_ref, own_ref, even_ref, near_ref)
     hidden = lax.dot_general(
         flat(cot_ref[...]), proj_ref[...], (((1,), (1,)), ((), ())), preferred_element_type=jnp.float32
     ).reshape(own_ref.shape)
@@ -107,8 +107,15 @@
             out_ref[frame, row] = (hidden[frame, row] * slope).astype(out_ref.dtype)
 
 
-def sum_kernel(offsets_ref, mixing_ref, left_ref, own_ref, right_ref, out_ref, far_ref, near_ref):
+def cut_kernel(x_ref, far_ref, near_ref):
+    parity = lax.rem(lax.axis_index("lat"), 2)
+    far_ref[...] = x_ref[:, parity]
+    near_ref[...] = x_ref[:, 1 - parity]
+
+
+def sum_kernel(offsets_ref, mixing_ref, odd_ref, own_ref, even_ref, out_ref, far_ref, near_ref, span_ref):
     frames, row_count, lon_count, channels = own_ref.shape
+    gather(odd_ref, own_ref, even_ref, span_ref)
     first_frame = lax.axis_index("tm") * frames
     total_frames = offsets_ref.shape[0]
     starts = [start_of(offsets_ref, first_frame + k - REACH) for k in range(frames + 2 * REACH)]
@@ -125,12 +132,7 @@
         for row in range(row_count):
             total = jnp.zeros((lon_count, channels), jnp.float32)
             for k, weight in weights:
-                if k < REACH:
-                    value = left_ref[k, row]
-                elif k < REACH + frames:
-                    value = own_ref[k - REACH, row]
-                else:
-                    value = right_ref[k - REACH - frames, row]
+                value = span_ref[k, row]
                 total = total + weight * value.astype(jnp.float32)
             out_ref[frame, row] = total.astype(out_ref.dtype)
     parity = lax.rem(lax.axis_index("lat"), 2)
@@ -168,19 +170,18 @@
     frames, row_count, lon_count, channels = trajectory.shape
     block = jax.ShapeDtypeStruct(trajectory.shape, jnp.bfloat16)
     edge = jax.ShapeDtypeStruct((frames, lon_count, channels), jnp.bfloat16)
-    odd = lax.rem(lax.axis_index("lat"), 2) == 1
-    top, bottom = trajectory[:, 0], trajectory[:, 1]
-    far, near = jnp.where(odd, bottom, top), jnp.where(odd, top, bottom)
+    far, near = call(cut_kernel, (edge, edge), [VMEM], (1_000, 600_000))(trajectory)
+    scratch = [pltpu.VMEM((frames + 2 * REACH, row_count, lon_count, channels), jnp.bfloat16)]
     conv_out = convolve(trajectory, far, near, conv_weight, False)
-    right, left = shift(conv_out, "tm", -1), shift(conv_out, "tm", 1)
+    odd, even = swap(conv_out, "tm", 1), swap(conv_out, "tm", 0)
     g_pre = call(
         mid_kernel, block, [SMEM] + [VMEM] * 6, (80_000_000, 1_400_000),
-        scratch_shapes=[pltpu.VMEM((frames + 2 * REACH, row_count, lon_count, channels), jnp.bfloat16)],
-    )(offsets, mixing, left, conv_out, right, cotangent, proj_weight)
-    right, left = shift(g_pre, "tm", -1), shift(g_pre, "tm", 1)
+        scratch_shapes=scratch,
+    )(offsets, mixing, odd, conv_out, even, cotangent, proj_weight)
+    odd, even = swap(g_pre, "tm", 1), swap(g_pre, "tm", 0)
     conv_grad, far, near = call(
-        sum_kernel, (block, edge, edge), [SMEM] + [VMEM] * 4, (10_000_000, 1_400_000)
-    )(offsets, mixing, left, g_pre, right)
+        sum_kernel, (block, edge, edge), [SMEM] + [VMEM] * 4, (10_000_000, 1_400_000), scratch_shapes=scratch
+    )(offsets, mixing, odd, g_pre, even)
     return convolve(conv_grad, far, near, conv_weight, True, cotangent)
 
 

time: 63.6 us -> 59.2 us (0.931)
  the two profiles are of different devices: /device:TPU:6 before, /device:TPU:3 now
where the time goes in v3:
time: 59.2 us; the launch traced here: 58.8 us
  starting transfers between devices  37.3 us (63%)
  waiting for transfers between devices  13.5 us (23%)
  Pallas kernels  4.94 us (8%)
  local copies, waits for them, and re-layouts  2.86 us (5%)
    ppermute x8, starting transfers between devices, swap(): return lax.ppermute(value, axis, pairs + [(j, i) for i, j in pairs])  37.3 us
    ppermute x8, waiting for transfers between devices, swap(): return lax.ppermute(value, axis, pairs + [(j, i) for i, j in pairs])  13.5 us
    unnamed x14, local copies, waits for them, and re-layouts  2.86 us
    pallas_call x2, Pallas kernels, convolve(): call(functools.partial(halo_kernel, transposed), result, [VMEM] * 4, (hal...  1.49 us
  transfers between devices with their start and end apart: 8, of which 3 were waited for; matrix products, arithmetic and copies ran while one was open for 0% of the time, Pallas kernels for 2%

profile of v3, /device:TPU:3, one launch (start us, length us, event | category | flops | bytes accessed | tf_op | source)
XLA Modules:
  0.0 58.8 jit_solution(10582722664718350125)
XLA Ops:
  0.0 0.0 copy-start.2
  0.0 0.9 %copy-done.2 = bf16[4,2,64,256]{3,2,1,0:T(8,128)(2,1)S(1)} copy-done((bf16[4,2,64,256]{3,2,1,0:T(8,128)(2,1)S(1)}, bf16[4,2,64,256]{3,2,1,0:T(8,128)(2,1)}, u32[]{:S(2)}) %copy-start.2) | copy-done | bytes 262168
  1.0 4.3 %collective-permute-start = (bf16[4,64,256]{2,1,0:T(8,128)(2,1)S(1)}, bf16[4,64,256]{2,1,0:T(8,128)(2,1)S(1)}, u32[]{:S(2)}, u32[]{:S(2)}) collective-permute-start(bf16[4,64,256]{2,1,0:T(8,128)(2,1)S(1)} %get-tuple-element.10), channel_id=1, source_target_pairs={{1,2},{2,1},{5,6},{6,5},{9,10},{10,9},{13,14},{14,13},{17,18},{18,... | collective-permute-start | bytes 393224 | tf_op jit(solution)/shard_map/ppermute | solution.py:18
  5.3 1.9 %collective-permute-start.1 = (bf16[4,64,256]{2,1,0:T(8,128)(2,1)S(1)}, bf16[4,64,256]{2,1,0:T(8,128)(2,1)S(1)}, u32[]{:S(2)}, u32[]{:S(2)}) collective-permute-start(bf16[4,64,256]{2,1,0:T(8,128)(2,1)S(1)} %get-tuple-element.11), channel_id=1, source_target_pairs={{0,1},{2,3},{1,0},{3,2},{4,5},{6,7},{5,4},{7,6},{8,9},{10,11},{9,8... | collective-permute-start | bytes 393224 | tf_op jit(solution)/shard_map/ppermute | solution.py:18
  7.2 0.0 copy-start
  7.2 1.3 %copy-done = bf16[9,256,256]{2,1,0:T(8,128)(2,1)S(1)} copy-done((bf16[9,256,256]{2,1,0:T(8,128)(2,1)S(1)}, bf16[9,256,256]{2,1,0:T(8,128)(2,1)}, u32[]{:S(2)}) %copy-start) | copy-done | bytes 1179672
  8.5 0.0 copy-start.1
  8.5 0.6 shard_map.64.total_ref
  9.1 0.0 copy-start.3
  9.1 0.0 copy-start.4
  9.1 0.0 copy-start.5
  9.1 0.0 copy-start.6
  9.1 0.0 collective-permute-done.far_ref
  9.1 0.0 collective-permute-done.1.near_ref
  9.2 0.6 %copy-done.1 = bf16[9,256,256]{2,1,0:T(8,128)(2,1)S(1)} copy-done((bf16[9,256,256]{2,1,0:T(8,128)(2,1)S(1)}, bf16[9,256,256]{2,1,0:T(8,128)(2,1)}, u32[]{:S(2)}) %copy-start.1) | copy-done | bytes 1179672
  9.8 0.4 shard_map.66.own_ref
  10.2 3.5 %collective-permute-start.3 = (bf16[4,2,64,256]{3,2,1,0:T(8,128)(2,1)S(1)}, bf16[4,2,64,256]{3,2,1,0:T(8,128)(2,1)S(1)}, u32[]{:S(2)}, u32[]{:S(2)}) collective-permute-start(bf16[4,2,64,256]{3,2,1,0:T(8,128)(2,1)S(1)} %shard_map.66.own_ref), channel_id=1, source_target_pairs={{0,4},{8,12},{16,20},{24,28},{32,36},{40,44},{48,52},{56,60},{64,6... | collective-permute-start | bytes 786440 | tf_op jit(solution)/shard_map/ppermute | solution.py:18
  13.7 13.5 %collective-permute-start.2 = (bf16[4,2,64,256]{3,2,1,0:T(8,128)(2,1)S(1)}, bf16[4,2,64,256]{3,2,1,0:T(8,128)(2,1)S(1)}, u32[]{:S(2)}, u32[]{:S(2)}) collective-permute-start(bf16[4,2,64,256]{3,2,1,0:T(8,128)(2,1)S(1)} %shard_map.66.own_ref), channel_id=1, source_target_pairs={{4,8},{12,16},{20,24},{28,32},{36,40},{44,48},{52,56},{60,64},{68,... | collective-permute-start | bytes 786440 | tf_op jit(solution)/shard_map/ppermute | solution.py:18
  27.2 0.0 collective-permute-done.3.even_ref
  27.3 5.9 %collective-permute-done.2.odd_ref = bf16[4,2,64,256]{3,2,1,0:T(8,128)(2,1)S(1)} collective-permute-done((bf16[4,2,64,256]{3,2,1,0:T(8,128)(2,1)S(1)}, bf16[4,2,64,256]{3,2,1,0:T(8,128)(2,1)S(1)}, u32[]{:S(2)}, u32[]{:S(2)}) %collective-permute-start.2) | collective-permute-done | bytes 262176 | tf_op jit(solution)/shard_map/ppermute | solution.py:18
  33.1 0.0 copy-done.3
  33.1 0.0 copy-done.4
  33.1 0.0 copy-done.5
  33.2 0.0 copy-done.6
  33.2 1.1 %shard_map.67.own_ref = bf16[4,2,64,256]{3,2,1,0:T(8,128)(2,1)S(1)} custom-call(s32[512]{0:T(512)S(1)} %copy-done.6, f32[25,256]{1,0:T(8,128)S(1)} %copy-done.5, bf16[4,2,64,256]{3,2,1,0:T(8,128)(2,1)S(1)} %collective-permute-done.2.odd_ref, bf16[4,2,64,256]{3,2,1,0:T(8,128)(2,1)S(1)} %shard_map.66.own_ref, ...), custom_call_target="tpu_custom_call" | custom-call | flops 80000000 | bytes 1400000 | tf_op jit(solution)/shard_map/pallas_call | solution.py:177
  34.3 1.9 %collective-permute-start.5 = (bf16[4,2,64,256]{3,2,1,0:T(8,128)(2,1)S(1)}, bf16[4,2,64,256]{3,2,1,0:T(8,128)(2,1)S(1)}, u32[]{:S(2)}, u32[]{:S(2)}) collective-permute-start(bf16[4,2,64,256]{3,2,1,0:T(8,128)(2,1)S(1)} %shard_map.67.own_ref), channel_id=1, source_target_pairs={{0,4},{8,12},{16,20},{24,28},{32,36},{40,44},{48,52},{56,60},{64,6... | collective-permute-start | bytes 786440 | tf_op jit(solution)/shard_map/ppermute | solution.py:18
  36.2 7.3 %collective-permute-start.4 = (bf16[4,2,64,256]{3,2,1,0:T(8,128)(2,1)S(1)}, bf16[4,2,64,256]{3,2,1,0:T(8,128)(2,1)S(1)}, u32[]{:S(2)}, u32[]{:S(2)}) collective-permute-start(bf16[4,2,64,256]{3,2,1,0:T(8,128)(2,1)S(1)} %shard_map.67.own_ref), channel_id=1, source_target_pairs={{4,8},{12,16},{20,24},{28,32},{36,40},{44,48},{52,56},{60,64},{68,... | collective-permute-start | bytes 786440 | tf_op jit(solution)/shard_map/ppermute | solution.py:18
  43.5 0.0 collective-permute-done.5.even_ref
  43.5 5.3 %collective-permute-done.4.odd_ref = bf16[4,2,64,256]{3,2,1,0:T(8,128)(2,1)S(1)} collective-permute-done((bf16[4,2,64,256]{3,2,1,0:T(8,128)(2,1)S(1)}, bf16[4,2,64,256]{3,2,1,0:T(8,128)(2,1)S(1)}, u32[]{:S(2)}, u32[]{:S(2)}) %collective-permute-start.4) | collective-permute-done | bytes 262176 | tf_op jit(solution)/shard_map/ppermute | solution.py:18
  48.8 1.1 %shard_map.68 = (bf16[4,2,64,256]{3,2,1,0:T(8,128)(2,1)S(1)}, bf16[4,64,256]{2,1,0:T(8,128)(2,1)S(1)}, bf16[4,64,256]{2,1,0:T(8,128)(2,1)S(1)}) custom-call(s32[512]{0:T(512)S(1)} %copy-done.6, f32[25,256]{1,0:T(8,128)S(1)} %copy-done.5, bf16[4,2,64,256]{3,2,1,0:T(8,128)(2,1)S(1)} %collective-permute-done.4.odd_ref, ...), custom_call_target="tpu_custom_call" | custom-call | flops 10000000 | bytes 1400000 | tf_op jit(solution)/shard_map/pallas_call | solution.py:182
  49.9 2.6 %collective-permute-start.6 = (bf16[4,64,256]{2,1,0:T(8,128)(2,1)S(1)}, bf16[4,64,256]{2,1,0:T(8,128)(2,1)S(1)}, u32[]{:S(2)}, u32[]{:S(2)}) collective-permute-start(bf16[4,64,256]{2,1,0:T(8,128)(2,1)S(1)} %get-tuple-element.13), channel_id=1, source_target_pairs={{1,2},{2,1},{5,6},{6,5},{9,10},{10,9},{13,14},{14,13},{17,18},{18,... | collective-permute-start | bytes 393224 | tf_op jit(solution)/shard_map/ppermute | solution.py:18
  52.5 2.3 %collective-permute-start.7 = (bf16[4,64,256]{2,1,0:T(8,128)(2,1)S(1)}, bf16[4,64,256]{2,1,0:T(8,128)(2,1)S(1)}, u32[]{:S(2)}, u32[]{:S(2)}) collective-permute-start(bf16[4,64,256]{2,1,0:T(8,128)(2,1)S(1)} %get-tuple-element.14), channel_id=1, source_target_pairs={{0,1},{2,3},{1,0},{3,2},{4,5},{6,7},{5,4},{7,6},{8,9},{10,11},{9,8... | collective-permute-start | bytes 393224 | tf_op jit(solution)/shard_map/ppermute | solution.py:18
  54.8 0.6 %shard_map.69.total_ref = f32[2,256,256]{2,1,0:T(8,128)S(1)} custom-call(bf16[4,2,64,256]{3,2,1,0:T(8,128)(2,1)S(1)} %get-tuple-element.12.x_ref, bf16[9,256,256]{2,1,0:T(8,128)(2,1)S(1)} %copy-done.1, bf16[4,2,64,256]{3,2,1,0:T(8,128)(2,1)S(1)} %copy-done.3), custom_call_target="tpu_custom_call" | custom-call | flops 402653184 | bytes 2000000 | tf_op jit(solution)/shard_map/pallas_call | solution.py:159
  55.4 2.3 %collective-permute-done.6.far_ref = bf16[4,64,256]{2,1,0:T(8,128)(2,1)S(1)} collective-permute-done((bf16[4,64,256]{2,1,0:T(8,128)(2,1)S(1)}, bf16[4,64,256]{2,1,0:T(8,128)(2,1)S(1)}, u32[]{:S(2)}, u32[]{:S(2)}) %collective-permute-start.6) | collective-permute-done | bytes 131104 | tf_op jit(solution)/shard_map/ppermute | solution.py:18
  57.7 0.0 collective-permute-done.7.near_ref
  57.7 1.1 %shard_map.70 = bf16[4,2,64,256]{3,2,1,0:T(8,128)(2,1)} custom-call(f32[2,256,256]{2,1,0:T(8,128)S(1)} %shard_map.69.total_ref, bf16[4,64,256]{2,1,0:T(8,128)(2,1)S(1)} %collective-permute-done.6.far_ref, bf16[4,64,256]{2,1,0:T(8,128)(2,1)S(1)} %collective-permute-done.7.near_ref, bf16[9,256,256]{2,1,0:T(8,128)(2,1)S(1)} %copy-done.1), custom_call_target="tpu_custom_call" | custom-call | flops 201326592 | bytes 2000000 | tf_op jit(solution)/shard_map/pallas_call | solution.py:164
  (1 shorter events, 0.0 us)
Async XLA Ops:
  0.0 0.9 %copy-start.2 = (bf16[4,2,64,256]{3,2,1,0:T(8,128)(2,1)S(1)}, bf16[4,2,64,256]{3,2,1,0:T(8,128)(2,1)}, u32[]{:S(2)}) copy-start(bf16[4,2,64,256]{3,2,1,0:T(8,128)(2,1)} %x_ref.3) | copy-start | bytes 786436
  1.0 8.2 %collective-permute-start = (bf16[4,64,256]{2,1,0:T(8,128)(2,1)S(1)}, bf16[4,64,256]{2,1,0:T(8,128)(2,1)S(1)}, u32[]{:S(2)}, u32[]{:S(2)}) collective-permute-start(bf16[4,64,256]{2,1,0:T(8,128)(2,1)S(1)} %get-tuple-element.10), channel_id=1, source_target_pairs={{1,2},{2,1},{5,6},{6,5},{9,10},{10,9},{13,14},{14,13},{17,18},{18,... | collective-permute-start | bytes 393224 | tf_op jit(solution)/shard_map/ppermute | solution.py:18
  5.3 3.8 %collective-permute-start.1 = (bf16[4,64,256]{2,1,0:T(8,128)(2,1)S(1)}, bf16[4,64,256]{2,1,0:T(8,128)(2,1)S(1)}, u32[]{:S(2)}, u32[]{:S(2)}) collective-permute-start(bf16[4,64,256]{2,1,0:T(8,128)(2,1)S(1)} %get-tuple-element.11), channel_id=1, source_target_pairs={{0,1},{2,3},{1,0},{3,2},{4,5},{6,7},{5,4},{7,6},{8,9},{10,11},{9,8... | collective-permute-start | bytes 393224 | tf_op jit(solution)/shard_map/ppermute | solution.py:18
  7.2 1.3 %copy-start = (bf16[9,256,256]{2,1,0:T(8,128)(2,1)S(1)}, bf16[9,256,256]{2,1,0:T(8,128)(2,1)}, u32[]{:S(2)}) copy-start(bf16[9,256,256]{2,1,0:T(8,128)(2,1)} %weight_ref.7) | copy-start | bytes 3538948
  8.5 1.3 %copy-start.1 = (bf16[9,256,256]{2,1,0:T(8,128)(2,1)S(1)}, bf16[9,256,256]{2,1,0:T(8,128)(2,1)}, u32[]{:S(2)}) copy-start(bf16[9,256,256]{2,1,0:T(8,128)(2,1)} %weight_ref.7) | copy-start | bytes 3538948
  9.1 24.1 %copy-start.3 = (bf16[4,2,64,256]{3,2,1,0:T(8,128)(2,1)S(1)}, bf16[4,2,64,256]{3,2,1,0:T(8,128)(2,1)}, u32[]{:S(2)}) copy-start(bf16[4,2,64,256]{3,2,1,0:T(8,128)(2,1)} %refs_0_.1) | copy-start | bytes 786436
  9.1 24.1 %copy-start.4 = (bf16[256,256]{1,0:T(8,128)(2,1)S(1)}, bf16[256,256]{1,0:T(8,128)(2,1)}, u32[]{:S(2)}) copy-start(bf16[256,256]{1,0:T(8,128)(2,1)} %proj_ref.1) | copy-start | bytes 393220
  9.1 24.0 %copy-start.5 = (f32[25,256]{1,0:T(8,128)S(1)}, f32[25,256]{1,0:T(8,128)}, u32[]{:S(2)}) copy-start(f32[25,256]{1,0:T(8,128)} %mixing_ref.3) | copy-start | bytes 76804
  9.1 24.0 %copy-start.6 = (s32[512]{0:T(512)S(1)}, s32[512]{0:T(512)}, u32[]{:S(2)}) copy-start(s32[512]{0:T(512)} %offsets_ref.3) | copy-start | bytes 6148
  10.2 17.1 %collective-permute-start.3 = (bf16[4,2,64,256]{3,2,1,0:T(8,128)(2,1)S(1)}, bf16[4,2,64,256]{3,2,1,0:T(8,128)(2,1)S(1)}, u32[]{:S(2)}, u32[]{:S(2)}) collective-permute-start(bf16[4,2,64,256]{3,2,1,0:T(8,128)(2,1)S(1)} %shard_map.66.own_ref), channel_id=1, source_target_pairs={{0,4},{8,12},{16,20},{24,28},{32,36},{40,44},{48,52},{56,60},{64,6... | collective-permute-start | bytes 786440 | tf_op jit(solution)/shard_map/ppermute | solution.py:18
  13.7 19.4 %collective-permute-start.2 = (bf16[4,2,64,256]{3,2,1,0:T(8,128)(2,1)S(1)}, bf16[4,2,64,256]{3,2,1,0:T(8,128)(2,1)S(1)}, u32[]{:S(2)}, u32[]{:S(2)}) collective-permute-start(bf16[4,2,64,256]{3,2,1,0:T(8,128)(2,1)S(1)} %shard_map.66.own_ref), channel_id=1, source_target_pairs={{4,8},{12,16},{20,24},{28,32},{36,40},{44,48},{52,56},{60,64},{68,... | collective-permute-start | bytes 786440 | tf_op jit(solution)/shard_map/ppermute | solution.py:18
  34.3 9.2 %collective-permute-start.5 = (bf16[4,2,64,256]{3,2,1,0:T(8,128)(2,1)S(1)}, bf16[4,2,64,256]{3,2,1,0:T(8,128)(2,1)S(1)}, u32[]{:S(2)}, u32[]{:S(2)}) collective-permute-start(bf16[4,2,64,256]{3,2,1,0:T(8,128)(2,1)S(1)} %shard_map.67.own_ref), channel_id=1, source_target_pairs={{0,4},{8,12},{16,20},{24,28},{32,36},{40,44},{48,52},{56,60},{64,6... | collective-permute-start | bytes 786440 | tf_op jit(solution)/shard_map/ppermute | solution.py:18
  36.2 12.6 %collective-permute-start.4 = (bf16[4,2,64,256]{3,2,1,0:T(8,128)(2,1)S(1)}, bf16[4,2,64,256]{3,2,1,0:T(8,128)(2,1)S(1)}, u32[]{:S(2)}, u32[]{:S(2)}) collective-permute-start(bf16[4,2,64,256]{3,2,1,0:T(8,128)(2,1)S(1)} %shard_map.67.own_ref), channel_id=1, source_target_pairs={{4,8},{12,16},{20,24},{28,32},{36,40},{44,48},{52,56},{60,64},{68,... | collective-permute-start | bytes 786440 | tf_op jit(solution)/shard_map/ppermute | solution.py:18
  49.9 7.8 %collective-permute-start.6 = (bf16[4,64,256]{2,1,0:T(8,128)(2,1)S(1)}, bf16[4,64,256]{2,1,0:T(8,128)(2,1)S(1)}, u32[]{:S(2)}, u32[]{:S(2)}) collective-permute-start(bf16[4,64,256]{2,1,0:T(8,128)(2,1)S(1)} %get-tuple-element.13), channel_id=1, source_target_pairs={{1,2},{2,1},{5,6},{6,5},{9,10},{10,9},{13,14},{14,13},{17,18},{18,... | collective-permute-start | bytes 393224 | tf_op jit(solution)/shard_map/ppermute | solution.py:18
  52.5 5.2 %collective-permute-start.7 = (bf16[4,64,256]{2,1,0:T(8,128)(2,1)S(1)}, bf16[4,64,256]{2,1,0:T(8,128)(2,1)S(1)}, u32[]{:S(2)}, u32[]{:S(2)}) collective-permute-start(bf16[4,64,256]{2,1,0:T(8,128)(2,1)S(1)} %get-tuple-element.14), channel_id=1, source_target_pairs={{0,1},{2,3},{1,0},{3,2},{4,5},{6,7},{5,4},{7,6},{8,9},{10,11},{9,8... | collective-permute-start | bytes 393224 | tf_op jit(solution)/shard_map/ppermute | solution.py:18

commit v4 on v3

--- a/solution.py
+++ b/solution.py
@@ -16,6 +16,15 @@
     size = lax.axis_size(axis)
     pairs = [(i, i + 1) for i in range(offset, size - 1, 2)]
     return lax.ppermute(value, axis, pairs + [(j, i) for i, j in pairs])
+
+
+def crossed(value, turn):
+    frames, bands = lax.axis_size("tm"), lax.axis_size("lat")
+    pairs = []
+    for band in range(bands):
+        for i in range((band + turn) % 2, frames - 1, 2):
+            pairs.append((i * bands + band, (i + 1) * bands + band))
+    return lax.ppermute(value, ("tm", "lat"), pairs + [(j, i) for i, j in pairs])
 
 
 def product(value, matrix, transposed):
@@ -77,19 +86,19 @@
     return jnp.clip(inside - offsets_ref[inside], 0, total_frames - 5)
 
 
-def gather(odd_ref, own_ref, even_ref, near_ref):
+def gather(first_ref, own_ref, second_ref, near_ref):
     frames = own_ref.shape[0]
-    parity = lax.rem(lax.axis_index("tm"), 2)
+    side = lax.rem(lax.axis_index("tm") + lax.axis_index("lat"), 2)
     span = REACH + frames
-    near_ref[pl.ds(span * parity, frames)] = odd_ref[...]
+    near_ref[pl.ds(span * (1 - side), frames)] = first_ref[...]
     near_ref[REACH:span] = own_ref[...]
-    near_ref[pl.ds(span * (1 - parity), frames)] = even_ref[...]
-
-
-def mid_kernel(offsets_ref, mixing_ref, odd_ref, own_ref, even_ref, cot_ref, proj_ref, out_ref, near_ref):
+    near_ref[pl.ds(span * side, frames)] = second_ref[...]
+
+
+def mid_kernel(offsets_ref, mixing_ref, second_ref, own_ref, first_ref, cot_ref, proj_ref, out_ref, near_ref):
     frames, row_count, lon_count, channels = own_ref.shape
     first_frame = lax.axis_index("tm") * frames
-    gather(odd_ref, own_ref, even_ref, near_ref)
+    gather(first_ref, own_ref, second_ref, near_ref)
     hidden = lax.dot_general(
         flat(cot_ref[...]), proj_ref[...], (((1,), (1,)), ((), ())), preferred_element_type=jnp.float32
     ).reshape(own_ref.shape)
@@ -113,9 +122,9 @@
     near_ref[...] = x_ref[:, 1 - parity]
 
 
-def sum_kernel(offsets_ref, mixing_ref, odd_ref, own_ref, even_ref, out_ref, far_ref, near_ref, span_ref):
+def sum_kernel(offsets_ref, mixing_ref, second_ref, own_ref, first_ref, out_ref, far_ref, near_ref, span_ref):
     frames, row_count, lon_count, channels = own_ref.shape
-    gather(odd_ref, own_ref, even_ref, span_ref)
+    gather(first_ref, own_ref, second_ref, span_ref)
     first_frame = lax.axis_index("tm") * frames
     total_frames = offsets_ref.shape[0]
     starts = [start_of(offsets_ref, first_frame + k - REACH) for k in range(frames + 2 * REACH)]
@@ -173,15 +182,15 @@
     far, near = call(cut_kernel, (edge, edge), [VMEM], (1_000, 600_000))(trajectory)
     scratch = [pltpu.VMEM((frames + 2 * REACH, row_count, lon_count, channels), jnp.bfloat16)]
     conv_out = convolve(trajectory, far, near, conv_weight, False)
-    odd, even = swap(conv_out, "tm", 1), swap(conv_out, "tm", 0)
+    first, second = crossed(conv_out, 0), crossed(conv_out, 1)
     g_pre = call(
         mid_kernel, block, [SMEM] + [VMEM] * 6, (80_000_000, 1_400_000),
         scratch_shapes=scratch,
-    )(offsets, mixing, odd, conv_out, even, cotangent, proj_weight)
-    odd, even = swap(g_pre, "tm", 1), swap(g_pre, "tm", 0)
+    )(offsets, mixing, second, conv_out, first, cotangent, proj_weight)
+    first, second = crossed(g_pre, 0), crossed(g_pre, 1)
     conv_grad, far, near = call(
         sum_kernel, (block, edge, edge), [SMEM] + [VMEM] * 4, (10_000_000, 1_400_000), scratch_shapes=scratch
-    )(offsets, mixing, odd, g_pre, even)
+    )(offsets, mixing, second, g_pre, first)
     return convolve(conv_grad, far, near, conv_weight, True, cotangent)
 
 

time: 59.2 us -> 56.5 us (0.954)
  the two profiles are of different devices: /device:TPU:3 before, /device:TPU:6 now
where the time goes in v4:
time: 56.5 us; the launch traced here: 56.1 us
  starting transfers between devices  35.6 us (63%)
  waiting for transfers between devices  13.2 us (23%)
  Pallas kernels  4.91 us (9%)
  local copies, waits for them, and re-layouts  2.24 us (4%)
    ppermute x4, starting transfers between devices, crossed(): lax.ppermute(value, ('tm', 'lat'), pairs + [(j, i) for i, j in pairs])  27.1 us
    ppermute x4, waiting for transfers between devices, crossed(): lax.ppermute(value, ('tm', 'lat'), pairs + [(j, i) for i, j in pairs])  8.66 us
    ppermute x4, starting transfers between devices, swap(): return lax.ppermute(value, axis, pairs + [(j, i) for i, j in pairs])  8.51 us
    ppermute x4, waiting for transfers between devices, swap(): return lax.ppermute(value, axis, pairs + [(j, i) for i, j in pairs])  4.52 us
    unnamed x14, local copies, waits for them, and re-layouts  2.24 us
    pallas_call x2, Pallas kernels, convolve(): call(functools.partial(halo_kernel, transposed), result, [VMEM] * 4, (hal...  1.49 us
    pallas_call x2, Pallas kernels, convolve(): call(functools.partial(local_kernel, transposed), sums, [VMEM] * (2 + len...  1.18 us
    pallas_call x1, Pallas kernels, body(): call(sum_kernel, (block, edge, edge), [SMEM] + [VMEM] * 4, (10000000, 140...  1.14 us
  transfers between devices with their start and end apart: 8, of which 4 were waited for; matrix products, arithmetic and copies ran while one was open for 0% of the time, Pallas kernels for 2%

profile of v4, /device:TPU:6, one launch (start us, length us, event | category | flops | bytes accessed | tf_op | source)
XLA Modules:
  0.0 56.1 jit_solution(8484708823930184747)
XLA Ops:
  0.0 0.0 copy-start.2
  0.0 0.9 %copy-done.2 = bf16[4,2,64,256]{3,2,1,0:T(8,128)(2,1)S(1)} copy-done((bf16[4,2,64,256]{3,2,1,0:T(8,128)(2,1)S(1)}, bf16[4,2,64,256]{3,2,1,0:T(8,128)(2,1)}, u32[]{:S(2)}) %copy-start.2) | copy-done | bytes 262168
  1.0 2.8 %collective-permute-start = (bf16[4,64,256]{2,1,0:T(8,128)(2,1)S(1)}, bf16[4,64,256]{2,1,0:T(8,128)(2,1)S(1)}, u32[]{:S(2)}, u32[]{:S(2)}) collective-permute-start(bf16[4,64,256]{2,1,0:T(8,128)(2,1)S(1)} %get-tuple-element.10), channel_id=1, source_target_pairs={{1,2},{2,1},{5,6},{6,5},{9,10},{10,9},{13,14},{14,13},{17,18},{18,... | collective-permute-start | bytes 393224 | tf_op jit(solution)/shard_map/ppermute | solution.py:18
  3.7 1.9 %collective-permute-start.1 = (bf16[4,64,256]{2,1,0:T(8,128)(2,1)S(1)}, bf16[4,64,256]{2,1,0:T(8,128)(2,1)S(1)}, u32[]{:S(2)}, u32[]{:S(2)}) collective-permute-start(bf16[4,64,256]{2,1,0:T(8,128)(2,1)S(1)} %get-tuple-element.11), channel_id=1, source_target_pairs={{0,1},{2,3},{1,0},{3,2},{4,5},{6,7},{5,4},{7,6},{8,9},{10,11},{9,8... | collective-permute-start | bytes 393224 | tf_op jit(solution)/shard_map/ppermute | solution.py:18
  5.7 0.0 copy-start
  5.7 1.3 %copy-done = bf16[9,256,256]{2,1,0:T(8,128)(2,1)S(1)} copy-done((bf16[9,256,256]{2,1,0:T(8,128)(2,1)S(1)}, bf16[9,256,256]{2,1,0:T(8,128)(2,1)}, u32[]{:S(2)}) %copy-start) | copy-done | bytes 1179672
  6.9 0.0 copy-start.1
  6.9 0.6 %shard_map.64.total_ref = f32[2,256,256]{2,1,0:T(8,128)S(1)} custom-call(bf16[4,2,64,256]{3,2,1,0:T(8,128)(2,1)S(1)} %copy-done.2, bf16[9,256,256]{2,1,0:T(8,128)(2,1)S(1)} %copy-done), custom_call_target="tpu_custom_call" | custom-call | flops 402653184 | bytes 2000000 | tf_op jit(solution)/shard_map/pallas_call | solution.py:168
  7.5 0.0 copy-start.3
  7.5 0.0 copy-start.4
  7.5 0.0 copy-start.5
  7.6 0.0 copy-start.6
  7.6 1.2 %collective-permute-done.far_ref = bf16[4,64,256]{2,1,0:T(8,128)(2,1)S(1)} collective-permute-done((bf16[4,64,256]{2,1,0:T(8,128)(2,1)S(1)}, bf16[4,64,256]{2,1,0:T(8,128)(2,1)S(1)}, u32[]{:S(2)}, u32[]{:S(2)}) %collective-permute-start) | collective-permute-done | bytes 131104 | tf_op jit(solution)/shard_map/ppermute | solution.py:18
  8.8 0.0 collective-permute-done.1.near_ref
  8.8 0.0 copy-done.1
  8.8 0.4 shard_map.66.own_ref
  9.2 3.8 %collective-permute-start.3 = (bf16[4,2,64,256]{3,2,1,0:T(8,128)(2,1)S(1)}, bf16[4,2,64,256]{3,2,1,0:T(8,128)(2,1)S(1)}, u32[]{:S(2)}, u32[]{:S(2)}) collective-permute-start(bf16[4,2,64,256]{3,2,1,0:T(8,128)(2,1)S(1)} %shard_map.66.own_ref), channel_id=1, source_target_pairs={{0,4},{8,12},{16,20},{24,28},{32,36},{40,44},{48,52},{56,60},{64,6... | collective-permute-start | bytes 786440 | tf_op jit(solution)/shard_map/ppermute | solution.py:27
  13.0 13.2 %collective-permute-start.2 = (bf16[4,2,64,256]{3,2,1,0:T(8,128)(2,1)S(1)}, bf16[4,2,64,256]{3,2,1,0:T(8,128)(2,1)S(1)}, u32[]{:S(2)}, u32[]{:S(2)}) collective-permute-start(bf16[4,2,64,256]{3,2,1,0:T(8,128)(2,1)S(1)} %shard_map.66.own_ref), channel_id=1, source_target_pairs={{4,8},{12,16},{20,24},{28,32},{36,40},{44,48},{52,56},{60,64},{68,... | collective-permute-start | bytes 786440 | tf_op jit(solution)/shard_map/ppermute | solution.py:27
  26.2 0.0 collective-permute-done.3.first_ref
  26.2 4.3 %collective-permute-done.2.second_ref = bf16[4,2,64,256]{3,2,1,0:T(8,128)(2,1)S(1)} collective-permute-done((bf16[4,2,64,256]{3,2,1,0:T(8,128)(2,1)S(1)}, bf16[4,2,64,256]{3,2,1,0:T(8,128)(2,1)S(1)}, u32[]{:S(2)}, u32[]{:S(2)}) %collective-permute-start.2) | collective-permute-done | bytes 262176 | tf_op jit(solution)/shard_map/ppermute | solution.py:27
  30.5 0.0 copy-done.3
  30.5 0.0 copy-done.4
  30.5 0.0 copy-done.5
  30.6 0.0 copy-done.6
  30.6 1.1 %shard_map.67.own_ref = bf16[4,2,64,256]{3,2,1,0:T(8,128)(2,1)S(1)} custom-call(s32[512]{0:T(512)S(1)} %copy-done.6, f32[25,256]{1,0:T(8,128)S(1)} %copy-done.5, bf16[4,2,64,256]{3,2,1,0:T(8,128)(2,1)S(1)} %collective-permute-done.2.second_ref, bf16[4,2,64,256]{3,2,1,0:T(8,128)(2,1)S(1)} %shard_map.66.own_ref, ...), custom_call_target="tpu_custom_call" | custom-call | flops 80000000 | bytes 1400000 | tf_op jit(solution)/shard_map/pallas_call | solution.py:186
  31.7 1.9 %collective-permute-start.5 = (bf16[4,2,64,256]{3,2,1,0:T(8,128)(2,1)S(1)}, bf16[4,2,64,256]{3,2,1,0:T(8,128)(2,1)S(1)}, u32[]{:S(2)}, u32[]{:S(2)}) collective-permute-start(bf16[4,2,64,256]{3,2,1,0:T(8,128)(2,1)S(1)} %shard_map.67.own_ref), channel_id=1, source_target_pairs={{0,4},{8,12},{16,20},{24,28},{32,36},{40,44},{48,52},{56,60},{64,6... | collective-permute-start | bytes 786440 | tf_op jit(solution)/shard_map/ppermute | solution.py:27
  33.6 8.1 %collective-permute-start.4 = (bf16[4,2,64,256]{3,2,1,0:T(8,128)(2,1)S(1)}, bf16[4,2,64,256]{3,2,1,0:T(8,128)(2,1)S(1)}, u32[]{:S(2)}, u32[]{:S(2)}) collective-permute-start(bf16[4,2,64,256]{3,2,1,0:T(8,128)(2,1)S(1)} %shard_map.67.own_ref), channel_id=1, source_target_pairs={{4,8},{12,16},{20,24},{28,32},{36,40},{44,48},{52,56},{60,64},{68,... | collective-permute-start | bytes 786440 | tf_op jit(solution)/shard_map/ppermute | solution.py:27
  41.7 0.0 collective-permute-done.5.first_ref
  41.7 4.3 %collective-permute-done.4.second_ref = bf16[4,2,64,256]{3,2,1,0:T(8,128)(2,1)S(1)} collective-permute-done((bf16[4,2,64,256]{3,2,1,0:T(8,128)(2,1)S(1)}, bf16[4,2,64,256]{3,2,1,0:T(8,128)(2,1)S(1)}, u32[]{:S(2)}, u32[]{:S(2)}) %collective-permute-start.4) | collective-permute-done | bytes 262176 | tf_op jit(solution)/shard_map/ppermute | solution.py:27
  46.1 1.1 %shard_map.68 = (bf16[4,2,64,256]{3,2,1,0:T(8,128)(2,1)S(1)}, bf16[4,64,256]{2,1,0:T(8,128)(2,1)S(1)}, bf16[4,64,256]{2,1,0:T(8,128)(2,1)S(1)}) custom-call(s32[512]{0:T(512)S(1)} %copy-done.6, f32[25,256]{1,0:T(8,128)S(1)} %copy-done.5, bf16[4,2,64,256]{3,2,1,0:T(8,128)(2,1)S(1)} %collective-permute-done.4.second_ref, ...), custom_call_target="tpu_custom_call" | custom-call | flops 10000000 | bytes 1400000 | tf_op jit(solution)/shard_map/pallas_call | solution.py:191
  47.2 1.9 %collective-permute-start.6 = (bf16[4,64,256]{2,1,0:T(8,128)(2,1)S(1)}, bf16[4,64,256]{2,1,0:T(8,128)(2,1)S(1)}, u32[]{:S(2)}, u32[]{:S(2)}) collective-permute-start(bf16[4,64,256]{2,1,0:T(8,128)(2,1)S(1)} %get-tuple-element.13), channel_id=1, source_target_pairs={{1,2},{2,1},{5,6},{6,5},{9,10},{10,9},{13,14},{14,13},{17,18},{18,... | collective-permute-start | bytes 393224 | tf_op jit(solution)/shard_map/ppermute | solution.py:18
  49.1 1.9 %collective-permute-start.7 = (bf16[4,64,256]{2,1,0:T(8,128)(2,1)S(1)}, bf16[4,64,256]{2,1,0:T(8,128)(2,1)S(1)}, u32[]{:S(2)}, u32[]{:S(2)}) collective-permute-start(bf16[4,64,256]{2,1,0:T(8,128)(2,1)S(1)} %get-tuple-element.14), channel_id=1, source_target_pairs={{0,1},{2,3},{1,0},{3,2},{4,5},{6,7},{5,4},{7,6},{8,9},{10,11},{9,8... | collective-permute-start | bytes 393224 | tf_op jit(solution)/shard_map/ppermute | solution.py:18
  51.1 0.6 %shard_map.69.total_ref = f32[2,256,256]{2,1,0:T(8,128)S(1)} custom-call(bf16[4,2,64,256]{3,2,1,0:T(8,128)(2,1)S(1)} %get-tuple-element.12.x_ref, bf16[9,256,256]{2,1,0:T(8,128)(2,1)S(1)} %copy-done.1, bf16[4,2,64,256]{3,2,1,0:T(8,128)(2,1)S(1)} %copy-done.3), custom_call_target="tpu_custom_call" | custom-call | flops 402653184 | bytes 2000000 | tf_op jit(solution)/shard_map/pallas_call | solution.py:168
  51.7 3.3 %collective-permute-done.6.far_ref = bf16[4,64,256]{2,1,0:T(8,128)(2,1)S(1)} collective-permute-done((bf16[4,64,256]{2,1,0:T(8,128)(2,1)S(1)}, bf16[4,64,256]{2,1,0:T(8,128)(2,1)S(1)}, u32[]{:S(2)}, u32[]{:S(2)}) %collective-permute-start.6) | collective-permute-done | bytes 131104 | tf_op jit(solution)/shard_map/ppermute | solution.py:18
  55.0 0.0 collective-permute-done.7.near_ref
  55.0 1.1 %shard_map.70 = bf16[4,2,64,256]{3,2,1,0:T(8,128)(2,1)} custom-call(f32[2,256,256]{2,1,0:T(8,128)S(1)} %shard_map.69.total_ref, bf16[4,64,256]{2,1,0:T(8,128)(2,1)S(1)} %collective-permute-done.6.far_ref, bf16[4,64,256]{2,1,0:T(8,128)(2,1)S(1)} %collective-permute-done.7.near_ref, bf16[9,256,256]{2,1,0:T(8,128)(2,1)S(1)} %copy-done.1), custom_call_target="tpu_custom_call" | custom-call | flops 201326592 | bytes 2000000 | tf_op jit(solution)/shard_map/pallas_call | solution.py:173
  (1 shorter events, 0.0 us)
Async XLA Ops:
  0.0 0.9 %copy-start.2 = (bf16[4,2,64,256]{3,2,1,0:T(8,128)(2,1)S(1)}, bf16[4,2,64,256]{3,2,1,0:T(8,128)(2,1)}, u32[]{:S(2)}) copy-start(bf16[4,2,64,256]{3,2,1,0:T(8,128)(2,1)} %x_ref.3) | copy-start | bytes 786436
  1.0 7.8 %collective-permute-start = (bf16[4,64,256]{2,1,0:T(8,128)(2,1)S(1)}, bf16[4,64,256]{2,1,0:T(8,128)(2,1)S(1)}, u32[]{:S(2)}, u32[]{:S(2)}) collective-permute-start(bf16[4,64,256]{2,1,0:T(8,128)(2,1)S(1)} %get-tuple-element.10), channel_id=1, source_target_pairs={{1,2},{2,1},{5,6},{6,5},{9,10},{10,9},{13,14},{14,13},{17,18},{18,... | collective-permute-start | bytes 393224 | tf_op jit(solution)/shard_map/ppermute | solution.py:18
  3.7 5.0 %collective-permute-start.1 = (bf16[4,64,256]{2,1,0:T(8,128)(2,1)S(1)}, bf16[4,64,256]{2,1,0:T(8,128)(2,1)S(1)}, u32[]{:S(2)}, u32[]{:S(2)}) collective-permute-start(bf16[4,64,256]{2,1,0:T(8,128)(2,1)S(1)} %get-tuple-element.11), channel_id=1, source_target_pairs={{0,1},{2,3},{1,0},{3,2},{4,5},{6,7},{5,4},{7,6},{8,9},{10,11},{9,8... | collective-permute-start | bytes 393224 | tf_op jit(solution)/shard_map/ppermute | solution.py:18
  5.7 1.3 %copy-start = (bf16[9,256,256]{2,1,0:T(8,128)(2,1)S(1)}, bf16[9,256,256]{2,1,0:T(8,128)(2,1)}, u32[]{:S(2)}) copy-start(bf16[9,256,256]{2,1,0:T(8,128)(2,1)} %weight_ref.7) | copy-start | bytes 3538948
  6.9 1.8 %copy-start.1 = (bf16[9,256,256]{2,1,0:T(8,128)(2,1)S(1)}, bf16[9,256,256]{2,1,0:T(8,128)(2,1)}, u32[]{:S(2)}) copy-start(bf16[9,256,256]{2,1,0:T(8,128)(2,1)} %weight_ref.7) | copy-start | bytes 3538948
  7.5 23.0 %copy-start.3 = (bf16[4,2,64,256]{3,2,1,0:T(8,128)(2,1)S(1)}, bf16[4,2,64,256]{3,2,1,0:T(8,128)(2,1)}, u32[]{:S(2)}) copy-start(bf16[4,2,64,256]{3,2,1,0:T(8,128)(2,1)} %refs_0_.1) | copy-start | bytes 786436
  7.5 23.0 %copy-start.4 = (bf16[256,256]{1,0:T(8,128)(2,1)S(1)}, bf16[256,256]{1,0:T(8,128)(2,1)}, u32[]{:S(2)}) copy-start(bf16[256,256]{1,0:T(8,128)(2,1)} %proj_ref.1) | copy-start | bytes 393220
  7.5 23.0 %copy-start.5 = (f32[25,256]{1,0:T(8,128)S(1)}, f32[25,256]{1,0:T(8,128)}, u32[]{:S(2)}) copy-start(f32[25,256]{1,0:T(8,128)} %mixing_ref.3) | copy-start | bytes 76804
  7.6 23.0 %copy-start.6 = (s32[512]{0:T(512)S(1)}, s32[512]{0:T(512)}, u32[]{:S(2)}) copy-start(s32[512]{0:T(512)} %offsets_ref.3) | copy-start | bytes 6148
  9.2 17.1 %collective-permute-start.3 = (bf16[4,2,64,256]{3,2,1,0:T(8,128)(2,1)S(1)}, bf16[4,2,64,256]{3,2,1,0:T(8,128)(2,1)S(1)}, u32[]{:S(2)}, u32[]{:S(2)}) collective-permute-start(bf16[4,2,64,256]{3,2,1,0:T(8,128)(2,1)S(1)} %shard_map.66.own_ref), channel_id=1, source_target_pairs={{0,4},{8,12},{16,20},{24,28},{32,36},{40,44},{48,52},{56,60},{64,6... | collective-permute-start | bytes 786440 | tf_op jit(solution)/shard_map/ppermute | solution.py:27
  13.0 17.6 %collective-permute-start.2 = (bf16[4,2,64,256]{3,2,1,0:T(8,128)(2,1)S(1)}, bf16[4,2,64,256]{3,2,1,0:T(8,128)(2,1)S(1)}, u32[]{:S(2)}, u32[]{:S(2)}) collective-permute-start(bf16[4,2,64,256]{3,2,1,0:T(8,128)(2,1)S(1)} %shard_map.66.own_ref), channel_id=1, source_target_pairs={{4,8},{12,16},{20,24},{28,32},{36,40},{44,48},{52,56},{60,64},{68,... | collective-permute-start | bytes 786440 | tf_op jit(solution)/shard_map/ppermute | solution.py:27
  31.7 10.1 %collective-permute-start.5 = (bf16[4,2,64,256]{3,2,1,0:T(8,128)(2,1)S(1)}, bf16[4,2,64,256]{3,2,1,0:T(8,128)(2,1)S(1)}, u32[]{:S(2)}, u32[]{:S(2)}) collective-permute-start(bf16[4,2,64,256]{3,2,1,0:T(8,128)(2,1)S(1)} %shard_map.67.own_ref), channel_id=1, source_target_pairs={{0,4},{8,12},{16,20},{24,28},{32,36},{40,44},{48,52},{56,60},{64,6... | collective-permute-start | bytes 786440 | tf_op jit(solution)/shard_map/ppermute | solution.py:27
  33.6 12.5 %collective-permute-start.4 = (bf16[4,2,64,256]{3,2,1,0:T(8,128)(2,1)S(1)}, bf16[4,2,64,256]{3,2,1,0:T(8,128)(2,1)S(1)}, u32[]{:S(2)}, u32[]{:S(2)}) collective-permute-start(bf16[4,2,64,256]{3,2,1,0:T(8,128)(2,1)S(1)} %shard_map.67.own_ref), channel_id=1, source_target_pairs={{4,8},{12,16},{20,24},{28,32},{36,40},{44,48},{52,56},{60,64},{68,... | collective-permute-start | bytes 786440 | tf_op jit(solution)/shard_map/ppermute | solution.py:27
  47.2 7.8 %collective-permute-start.6 = (bf16[4,64,256]{2,1,0:T(8,128)(2,1)S(1)}, bf16[4,64,256]{2,1,0:T(8,128)(2,1)S(1)}, u32[]{:S(2)}, u32[]{:S(2)}) collective-permute-start(bf16[4,64,256]{2,1,0:T(8,128)(2,1)S(1)} %get-tuple-element.13), channel_id=1, source_target_pairs={{1,2},{2,1},{5,6},{6,5},{9,10},{10,9},{13,14},{14,13},{17,18},{18,... | collective-permute-start | bytes 393224 | tf_op jit(solution)/shard_map/ppermute | solution.py:18
  49.1 5.9 %collective-permute-start.7 = (bf16[4,64,256]{2,1,0:T(8,128)(2,1)S(1)}, bf16[4,64,256]{2,1,0:T(8,128)(2,1)S(1)}, u32[]{:S(2)}, u32[]{:S(2)}) collective-permute-start(bf16[4,64,256]{2,1,0:T(8,128)(2,1)S(1)} %get-tuple-element.14), channel_id=1, source_target_pairs={{0,1},{2,3},{1,0},{3,2},{4,5},{6,7},{5,4},{7,6},{8,9},{10,11},{9,8... | collective-permute-start | bytes 393224 | tf_op jit(solution)/shard_map/ppermute | solution.py:18

commit v5 on v4

v5 whole, which is shorter than its diff:
```python
import functools

import jax
import jax.numpy as jnp
from jax import lax
from jax.experimental import pallas as pl
from jax.experimental.pallas import tpu as pltpu
from jax.sharding import PartitionSpec as P

VMEM = pl.BlockSpec(memory_space=pltpu.VMEM)
SMEM = pl.BlockSpec(memory_space=pltpu.SMEM)
REACH = 4


def swap(value, axis, offset):
    size = lax.axis_size(axis)
    pairs = [(i, i + 1) for i in range(offset, size - 1, 2)]
    return lax.ppermute(value, axis, pairs + [(j, i) for i, j in pairs])


def crossed(value, turn):
    frames, bands = lax.axis_size("tm"), lax.axis_size("lat")
    pairs = []
    for band in range(bands):
        for i in range((band + turn) % 2, frames - 1, 2):
            pairs.append((i * bands + band, (i + 1) * bands + band))
    return lax.ppermute(value, ("tm", "lat"), pairs + [(j, i) for i, j in pairs])


def product(value, matrix, transposed):
    return lax.dot_general(
        value,
        matrix,
        (((1,), (1 if transposed else 0,)), ((), ())),
        preferred_element_type=jnp.float32,
    )


def rolled(value, lon_count, step):
    split = value.reshape(-1, lon_count, value.shape[-1])
    return pltpu.roll(split, step % lon_count, axis=1).reshape(value.shape)


def aligned(low, mid, high, lon_count, transposed):
    step = -1 if transposed else 1
    return mid + rolled(low, lon_count, step) + rolled(high, lon_count, -step)


def flat(value):
    return value.reshape(-1, value.shape[-1])


def local_kernel(transposed, x_ref, weight_ref, *refs):
    total_ref = refs[-1]
    lon_count = x_ref.shape[2]
    first, second = flat(x_ref[:, 0]), flat(x_ref[:, 1])
    half = first.shape[0]
    both = jnp.concatenate([first, second], axis=0)
    ahead, behind = (0, 2) if transposed else (2, 0)
    sums = [[], []]
    for lon_tap in range(3):
        middle = product(both, weight_ref[3 + lon_tap], transposed)
        sums[0].append(middle[:half] + product(second, weight_ref[3 * ahead + lon_tap], transposed))
        sums[1].append(middle[half:] + product(first, weight_ref[3 * behind + lon_tap], transposed))
    for row in range(2):
        total_ref[row] = aligned(*sums[row], lon_count, transposed)


def halo_kernel(transposed, total_ref, far_ref, near_ref, weight_ref, out_ref):
    frames, lon_count, channels = far_ref.shape
    parity = lax.rem(lax.axis_index("lat"), 2)
    for row, edge_ref in ((1 - parity, near_ref), (parity, far_ref)):
        tap = 2 - 2 * row if transposed else 2 * row
        value = flat(edge_ref[...])
        parts = [product(value, weight_ref[3 * tap + lon_tap], transposed) for lon_tap in range(3)]
        total = total_ref[row] + aligned(*parts, lon_count, transposed)
        out_ref[:, row] = total.astype(out_ref.dtype).reshape(frames, lon_count, channels)


def start_of(offsets_ref, frame):
    total_frames = offsets_ref.shape[0]
    inside = jnp.clip(frame, 0, total_frames - 1)
    return jnp.clip(inside - offsets_ref[inside], 0, total_frames - 5)


def weight_of(offsets_ref, mixing_ref, frame, target):
    start = start_of(offsets_ref, frame)
    slot = target - start
    good = (slot >= 0) & (slot <= 4) & (frame >= 0) & (frame < offsets_ref.shape[0])
    weight = mixing_ref[pl.ds(jnp.where(good, 5 * (frame - start) + slot, 0), 1), :]
    return jnp.where(good, weight, 0.0)


LAGS = 2 * REACH + 1


def table_kernel(offsets_ref, mixing_ref, after_ref, reads_ref, read_by_ref):
    del after_ref
    frames = reads_ref.shape[0] // LAGS
    base = lax.axis_index("tm") * frames
    for frame in range(frames):
        for lag in range(-REACH, REACH + 1):
            row = frame * LAGS + lag + REACH
            here, there = base + frame, base + frame + lag
            reads_ref[row : row + 1, :] = weight_of(offsets_ref, mixing_ref, here, there)
            read_by_ref[row : row + 1, :] = weight_of(offsets_ref, mixing_ref, there, here)


def mixed(table_ref, sources, rows, total_of, store):
    frames = sources[0][0].shape[0]
    for frame in range(frames):
        for row in rows:
            total = total_of(frame, row)
            for ref, first in sources:
                for k in range(frames):
                    lag = first + k - frame
                    if abs(lag) <= REACH:
                        line = frame * LAGS + lag + REACH
                        term = table_ref[line : line + 1, :] * ref[k, row].astype(jnp.float32)
                        total = term if total is None else total + term
            store(frame, row, total)


def own_kernel(table_ref, own_ref, total_ref):
    def store(frame, row, total):
        total_ref[frame, row] = total

    mixed(table_ref, [(own_ref, 0)], range(2), lambda *_: None, store)


def sided(first_ref, second_ref, run):
    side = lax.rem(lax.axis_index("tm") + lax.axis_index("lat"), 2)

    @pl.when(side == 1)
    def _():
        run(first_ref, second_ref)

    @pl.when(side == 0)
    def _():
        run(second_ref, first_ref)


def mid_kernel(table_ref, second_ref, total_ref, first_ref, hidden_ref, out_ref):
    frames = out_ref.shape[0]

    def store(frame, row, pre):
        sigma = 0.5 + 0.5 * jnp.tanh(0.5 * pre)
        slope = sigma * (1.0 + pre * (1.0 - sigma))
        out_ref[frame, row] = (hidden_ref[frame, row] * slope).astype(out_ref.dtype)

    def run(before, after):
        sources = [(before, -frames), (after, frames)]
        mixed(table_ref, sources, range(2), lambda frame, row: total_ref[frame, row], store)

    sided(first_ref, second_ref, run)


def hidden_kernel(cot_ref, proj_ref, out_ref):
    out_ref[...] = product(flat(cot_ref[...]), proj_ref[...], True).reshape(out_ref.shape)


def cut_kernel(x_ref, far_ref, near_ref):
    parity = lax.rem(lax.axis_index("lat"), 2)
    far_ref[...] = x_ref[:, parity]
    near_ref[...] = x_ref[:, 1 - parity]


def sum_kernel(far, table_ref, second_ref, total_ref, first_ref, out_ref):
    frames = out_ref.shape[0]
    parity = lax.rem(lax.axis_index("lat"), 2)
    row = parity if far else 1 - parity

    def store(frame, _, total):
        out_ref[frame] = total.astype(out_ref.dtype)

    def run(before, after):
        sources = [(before, -frames), (after, frames)]
        mixed(table_ref, sources, [row], lambda frame, _: total_ref[frame, row], store)

    sided(first_ref, second_ref, run)


def back_local_kernel(far_ref, near_ref, weight_ref, cot_ref, far_total, near_total):
    lon_count = far_ref.shape[1]
    parity = lax.rem(lax.axis_index("lat"), 2)
    far, near = flat(far_ref[...]), flat(near_ref[...])
    half = near.shape[0]
    both = jnp.concatenate([far, near], axis=0)
    tap = 2 * parity
    far_sums, near_sums = [], []
    for lon_tap in range(3):
        middle = product(both, weight_ref[3 + lon_tap], True)
        far_sums.append(middle[:half] + product(near, weight_ref[3 * tap + lon_tap], True))
        near_sums.append(middle[half:] + product(far, weight_ref[3 * (2 - tap) + lon_tap], True))
    for row, sums, out_ref in ((parity, far_sums, far_total), (1 - parity, near_sums, near_total)):
        out_ref[...] = aligned(*sums, lon_count, True) + flat(cot_ref[:, row]).astype(jnp.float32)


def back_halo(tap, total_ref, halo_ref, weight_ref, out_ref):
    value = flat(halo_ref[...])
    parts = [product(value, weight_ref[3 * tap + lon_tap], True) for lon_tap in range(3)]
    total = total_ref[...] + aligned(*parts, halo_ref.shape[1], True)
    out_ref[...] = total.astype(out_ref.dtype).reshape(out_ref.shape)


def final_kernel(far_total, far_halo, near_total, near_halo, weight_ref, out_ref, near_ref, far_ref, sems):
    parity = lax.rem(lax.axis_index("lat"), 2)
    back_halo(2 * parity, near_total, near_halo, weight_ref, near_ref)
    near_copy = pltpu.make_async_copy(near_ref, out_ref.at[:, 1 - parity], sems.at[0])
    near_copy.start()
    back_halo(2 - 2 * parity, far_total, far_halo, weight_ref, far_ref)
    far_copy = pltpu.make_async_copy(far_ref, out_ref.at[:, parity], sems.at[1])
    far_copy.start()
    near_copy.wait()
    far_copy.wait()


def call(kernel, out_shapes, specs, cost, out_specs=None, **extra):
    return pl.pallas_call(
        kernel,
        out_shape=out_shapes,
        in_specs=specs,
        out_specs=out_specs or jax.tree.map(lambda _: VMEM, out_shapes),
        compiler_params=pltpu.CompilerParams(vmem_limit_bytes=24 * 1024 * 1024),
        cost_estimate=pl.CostEstimate(flops=cost[0], bytes_accessed=cost[1], transcendentals=0),
        **extra,
    )


def convolve(block, far, near, weight, transposed, *added):
    frames, row_count, lon_count, channels = block.shape
    half = 2 * 3 * frames * row_count * lon_count * channels * channels
    sums = jax.ShapeDtypeStruct((row_count, frames * lon_count, channels), jnp.float32)
    total = call(
        functools.partial(local_kernel, transposed), sums, [VMEM] * (2 + len(added)), (2 * half, 2_000_000)
    )(block, weight, *added)
    far, near = swap(far, "lat", 1), swap(near, "lat", 0)
    result = jax.ShapeDtypeStruct(block.shape, jnp.bfloat16)
    return call(functools.partial(halo_kernel, transposed), result, [VMEM] * 4, (half, 2_000_000))(
        total, far, near, weight
    )


def body(trajectory, cotangent, conv_weight, proj_weight, mixing, offsets):
    frames, row_count, lon_count, channels = trajectory.shape
    block = jax.ShapeDtypeStruct(trajectory.shape, jnp.bfloat16)
    edge = jax.ShapeDtypeStruct((frames, lon_count, channels), jnp.bfloat16)
    far, near = call(cut_kernel, (edge, edge), [VMEM], (4_000_000_000, 600_000))(trajectory)
    wide = jax.ShapeDtypeStruct(trajectory.shape, jnp.float32)
    conv_out = convolve(trajectory, far, near, conv_weight, False)
    table = jax.ShapeDtypeStruct((frames * LAGS, channels), jnp.float32)
    reads, read_by = call(table_kernel, (table, table), [SMEM] + [VMEM] * 2, (1_000_000, 200_000))(
        offsets, mixing, conv_out
    )
    first, second = crossed(conv_out, 0), crossed(conv_out, 1)
    hidden = call(hidden_kernel, wide, [VMEM] * 2, (67_000_000, 1_000_000))(cotangent, proj_weight)
    own = call(own_kernel, wide, [VMEM] * 2, (10_000_000, 1_000_000))(reads, conv_out)
    g_pre = call(mid_kernel, block, [VMEM] * 5, (10_000_000, 1_400_000))(reads, second, own, first, hidden)
    first, second = crossed(g_pre, 0), crossed(g_pre, 1)
    own = call(own_kernel, wide, [VMEM] * 2, (10_000_000, 1_000_000))(read_by, g_pre)
    far, near = [
        call(functools.partial(sum_kernel, is_far), edge, [VMEM] * 4, (5_000_000, 700_000))(
            read_by, second, own, first
        )
        for is_far in (True, False)
    ]
    far_halo, near_halo = swap(far, "lat", 1), swap(near, "lat", 0)
    tap = 2 * 3 * frames * lon_count * channels * channels
    sums = jax.ShapeDtypeStruct((frames * lon_count, channels), jnp.float32)
    far_total, near_total = call(back_local_kernel, (sums, sums), [VMEM] * 4, (4 * tap, 2_000_000))(
        far, near, conv_weight, cotangent
    )
    return call(
        final_kernel, block, [VMEM] * 5, (2 * tap, 2_000_000), out_specs=pl.BlockSpec(memory_space=pl.ANY),
        scratch_shapes=[pltpu.VMEM(edge.shape, edge.dtype)] * 2 + [pltpu.SemaphoreType.DMA((2,))],
    )(far_total, far_halo, near_total, near_halo, conv_weight)


def solution(mesh):
    in_specs = (P("tm", "lat", None, None), P("tm", "lat", None, None), P(), P(), P(), P())
    out_specs = P("tm", "lat", None, None)
    return jax.shard_map(body, mesh=mesh, in_specs=in_specs, out_specs=out_specs, check_vma=False)
```

time: 56.5 us -> 54.8 us (0.970)
  local copies, waits for them, and re-layouts: 2.24 us -> 1.07 us
  waiting for transfers between devices: 13.2 us -> 12.4 us
    pallas_call x3 -> x10, Pallas kernels: 2.24 us -> 4.22 us  [the longest x1 1.12 us: body(): call(table_kernel, (table, table), [SMEM] + [VMEM] * 2, (1000000, 200000))]
    ppermute x4, waiting for transfers between devices: 8.66 us -> 6.83 us  [crossed(): lax.ppermute(value, ('tm', 'lat'), pairs + [(j, i) for i, j in pairs])]
    unnamed x14 -> x12, local copies, waits for them, and re-layouts: 2.24 us -> 1.07 us
    pallas_call x2 -> x1, Pallas kernels: 1.49 us -> 0.38 us  [convolve(): call(functools.partial(halo_kernel, transposed), result, [VMEM] * 4, (hal...]
    ppermute x4, waiting for transfers between devices: 4.52 us -> 5.61 us  [swap(): return lax.ppermute(value, axis, pairs + [(j, i) for i, j in pairs])]
    pallas_call x2 -> x1, Pallas kernels: 1.18 us -> 0.58 us  [convolve(): call(functools.partial(local_kernel, transposed), sums, [VMEM] * (2 + len...]
  transfers between devices with their start and end apart: 8 -> 8, of which waited for: 4 -> 5; matrix products, arithmetic and copies ran while one was open for 0% -> 0% of each run, Pallas kernels for 2% -> 6%
where the time goes in v5:
time: 54.8 us; the launch traced here: 54.5 us
  starting transfers between devices  35.6 us (65%)
  waiting for transfers between devices  12.4 us (23%)
  Pallas kernels  5.17 us (9%)
  local copies, waits for them, and re-layouts  1.07 us (2%)
    ppermute x4, starting transfers between devices, crossed(): lax.ppermute(value, ('tm', 'lat'), pairs + [(j, i) for i, j in pairs])  27.1 us
    ppermute x4, starting transfers between devices, swap(): return lax.ppermute(value, axis, pairs + [(j, i) for i, j in pairs])  8.51 us
    ppermute x4, waiting for transfers between devices, crossed(): lax.ppermute(value, ('tm', 'lat'), pairs + [(j, i) for i, j in pairs])  6.83 us
    ppermute x4, waiting for transfers between devices, swap(): return lax.ppermute(value, axis, pairs + [(j, i) for i, j in pairs])  5.61 us
    pallas_call x1, Pallas kernels, body(): call(table_kernel, (table, table), [SMEM] + [VMEM] * 2, (1000000, 200000))  1.12 us
  transfers between devices with their start and end apart: 8, of which 5 were waited for; matrix products, arithmetic and copies ran while one was open for 0% of the time, Pallas kernels for 6%

profile of v5, /device:TPU:6, one launch (start us, length us, event | category | flops | bytes accessed | tf_op | source)
XLA Modules:
  0.0 54.5 jit_solution(16193552880871652788)
XLA Ops:
  0.0 0.0 copy-start
  0.0 0.0 copy-start.2
  0.0 1.0 %copy-done.2 = bf16[4,2,64,256]{3,2,1,0:T(8,128)(2,1)S(1)} copy-done((bf16[4,2,64,256]{3,2,1,0:T(8,128)(2,1)S(1)}, bf16[4,2,64,256]{3,2,1,0:T(8,128)(2,1)}, u32[]{:S(2)}) %copy-start.2) | copy-done | bytes 262168
  1.1 2.8 %collective-permute-start = (bf16[4,64,256]{2,1,0:T(8,128)(2,1)S(1)}, bf16[4,64,256]{2,1,0:T(8,128)(2,1)S(1)}, u32[]{:S(2)}, u32[]{:S(2)}) collective-permute-start(bf16[4,64,256]{2,1,0:T(8,128)(2,1)S(1)} %get-tuple-element.11), channel_id=1, source_target_pairs={{1,2},{2,1},{5,6},{6,5},{9,10},{10,9},{13,14},{14,13},{17,18},{18,... | collective-permute-start | bytes 393224 | tf_op jit(solution)/shard_map/ppermute | solution.py:18
  3.8 1.9 %collective-permute-start.1 = (bf16[4,64,256]{2,1,0:T(8,128)(2,1)S(1)}, bf16[4,64,256]{2,1,0:T(8,128)(2,1)S(1)}, u32[]{:S(2)}, u32[]{:S(2)}) collective-permute-start(bf16[4,64,256]{2,1,0:T(8,128)(2,1)S(1)} %get-tuple-element.12), channel_id=1, source_target_pairs={{0,1},{2,3},{1,0},{3,2},{4,5},{6,7},{5,4},{7,6},{8,9},{10,11},{9,8... | collective-permute-start | bytes 393224 | tf_op jit(solution)/shard_map/ppermute | solution.py:18
  5.8 0.0 copy-done
  5.8 0.6 %shard_map.64.total_ref = f32[2,256,256]{2,1,0:T(8,128)S(1)} custom-call(bf16[4,2,64,256]{3,2,1,0:T(8,128)(2,1)S(1)} %copy-done.2, bf16[9,256,256]{2,1,0:T(8,128)(2,1)S(1)} %copy-done), custom_call_target="tpu_custom_call" | custom-call | flops 402653184 | bytes 2000000 | tf_op jit(solution)/shard_map/pallas_call | solution.py:234
  6.4 0.0 copy-start.1
  6.4 0.0 copy-start.3
  6.4 0.0 copy-start.4
  6.4 0.0 copy-start.5
  6.4 2.5 %collective-permute-done.far_ref = bf16[4,64,256]{2,1,0:T(8,128)(2,1)S(1)} collective-permute-done((bf16[4,64,256]{2,1,0:T(8,128)(2,1)S(1)}, bf16[4,64,256]{2,1,0:T(8,128)(2,1)S(1)}, u32[]{:S(2)}, u32[]{:S(2)}) %collective-permute-start) | collective-permute-done | bytes 131104 | tf_op jit(solution)/shard_map/ppermute | solution.py:18
  8.9 0.0 collective-permute-done.1.near_ref
  8.9 0.4 shard_map.66.after_ref.own_ref
  9.2 3.8 %collective-permute-start.3 = (bf16[4,2,64,256]{3,2,1,0:T(8,128)(2,1)S(1)}, bf16[4,2,64,256]{3,2,1,0:T(8,128)(2,1)S(1)}, u32[]{:S(2)}, u32[]{:S(2)}) collective-permute-start(bf16[4,2,64,256]{3,2,1,0:T(8,128)(2,1)S(1)} %shard_map.66.after_ref.own_ref), channel_id=1, source_target_pairs={{0,4},{8,12},{16,20},{24,28},{32,36},{40,44},{48,52},{56,60},{64,6... | collective-permute-start | bytes 786440 | tf_op jit(solution)/shard_map/ppermute | solution.py:27
  13.1 13.2 %collective-permute-start.2 = (bf16[4,2,64,256]{3,2,1,0:T(8,128)(2,1)S(1)}, bf16[4,2,64,256]{3,2,1,0:T(8,128)(2,1)S(1)}, u32[]{:S(2)}, u32[]{:S(2)}) collective-permute-start(bf16[4,2,64,256]{3,2,1,0:T(8,128)(2,1)S(1)} %shard_map.66.after_ref.own_ref), channel_id=1, source_target_pairs={{4,8},{12,16},{20,24},{28,32},{36,40},{44,48},{52,56},{60,64},{68,... | collective-permute-start | bytes 786440 | tf_op jit(solution)/shard_map/ppermute | solution.py:27
  26.3 0.0 copy-done.1
  26.3 0.0 copy-done.3
  26.3 0.3 shard_map.69.hidden_ref
  26.6 0.0 copy-done.4
  26.6 0.0 copy-done.5
  26.6 1.1 %shard_map.67 = (f32[36,256]{1,0:T(8,128)S(1)}, f32[36,256]{1,0:T(8,128)S(1)}) custom-call(s32[512]{0:T(512)S(1)} %copy-done.5, f32[25,256]{1,0:T(8,128)S(1)} %copy-done.4, bf16[4,2,64,256]{3,2,1,0:T(8,128)(2,1)S(1)} %shard_map.66.after_ref.own_ref), custom_call_target="tpu_custom_call" | custom-call | flops 1000000 | bytes 200000 | tf_op jit(solution)/shard_map/pallas_call | solution.py:252
  27.7 0.2 shard_map.68.total_ref
  27.9 0.0 collective-permute-done.3.first_ref
  27.9 2.7 %collective-permute-done.2.second_ref = bf16[4,2,64,256]{3,2,1,0:T(8,128)(2,1)S(1)} collective-permute-done((bf16[4,2,64,256]{3,2,1,0:T(8,128)(2,1)S(1)}, bf16[4,2,64,256]{3,2,1,0:T(8,128)(2,1)S(1)}, u32[]{:S(2)}, u32[]{:S(2)}) %collective-permute-start.2) | collective-permute-done | bytes 262176 | tf_op jit(solution)/shard_map/ppermute | solution.py:27
  30.6 0.4 shard_map.70.own_ref
  31.1 1.9 %collective-permute-start.5 = (bf16[4,2,64,256]{3,2,1,0:T(8,128)(2,1)S(1)}, bf16[4,2,64,256]{3,2,1,0:T(8,128)(2,1)S(1)}, u32[]{:S(2)}, u32[]{:S(2)}) collective-permute-start(bf16[4,2,64,256]{3,2,1,0:T(8,128)(2,1)S(1)} %shard_map.70.own_ref), channel_id=1, source_target_pairs={{0,4},{8,12},{16,20},{24,28},{32,36},{40,44},{48,52},{56,60},{64,6... | collective-permute-start | bytes 786440 | tf_op jit(solution)/shard_map/ppermute | solution.py:27
  33.0 8.1 %collective-permute-start.4 = (bf16[4,2,64,256]{3,2,1,0:T(8,128)(2,1)S(1)}, bf16[4,2,64,256]{3,2,1,0:T(8,128)(2,1)S(1)}, u32[]{:S(2)}, u32[]{:S(2)}) collective-permute-start(bf16[4,2,64,256]{3,2,1,0:T(8,128)(2,1)S(1)} %shard_map.70.own_ref), channel_id=1, source_target_pairs={{4,8},{12,16},{20,24},{28,32},{36,40},{44,48},{52,56},{60,64},{68,... | collective-permute-start | bytes 786440 | tf_op jit(solution)/shard_map/ppermute | solution.py:27
  41.2 0.2 shard_map.71.total_ref
  41.4 0.5 collective-permute-done.5.first_ref
  41.9 3.6 %collective-permute-done.4.second_ref = bf16[4,2,64,256]{3,2,1,0:T(8,128)(2,1)S(1)} collective-permute-done((bf16[4,2,64,256]{3,2,1,0:T(8,128)(2,1)S(1)}, bf16[4,2,64,256]{3,2,1,0:T(8,128)(2,1)S(1)}, u32[]{:S(2)}, u32[]{:S(2)}) %collective-permute-start.4) | collective-permute-done | bytes 262176 | tf_op jit(solution)/shard_map/ppermute | solution.py:27
  45.5 0.1 shard_map.72.far_ref
  45.6 1.9 %collective-permute-start.6 = (bf16[4,64,256]{2,1,0:T(8,128)(2,1)S(1)}, bf16[4,64,256]{2,1,0:T(8,128)(2,1)S(1)}, u32[]{:S(2)}, u32[]{:S(2)}) collective-permute-start(bf16[4,64,256]{2,1,0:T(8,128)(2,1)S(1)} %shard_map.72.far_ref), channel_id=1, source_target_pairs={{1,2},{2,1},{5,6},{6,5},{9,10},{10,9},{13,14},{14,13},{17,18},{18,... | collective-permute-start | bytes 393224 | tf_op jit(solution)/shard_map/ppermute | solution.py:18
  47.6 0.2 shard_map.73.near_ref
  47.7 1.9 %collective-permute-start.7 = (bf16[4,64,256]{2,1,0:T(8,128)(2,1)S(1)}, bf16[4,64,256]{2,1,0:T(8,128)(2,1)S(1)}, u32[]{:S(2)}, u32[]{:S(2)}) collective-permute-start(bf16[4,64,256]{2,1,0:T(8,128)(2,1)S(1)} %shard_map.73.near_ref), channel_id=1, source_target_pairs={{0,1},{2,3},{1,0},{3,2},{4,5},{6,7},{5,4},{7,6},{8,9},{10,11},{9,8... | collective-permute-start | bytes 393224 | tf_op jit(solution)/shard_map/ppermute | solution.py:18
  49.7 0.6 %shard_map.74 = (f32[256,256]{1,0:T(8,128)S(1)}, f32[256,256]{1,0:T(8,128)S(1)}) custom-call(bf16[4,64,256]{2,1,0:T(8,128)(2,1)S(1)} %shard_map.72.far_ref, bf16[4,64,256]{2,1,0:T(8,128)(2,1)S(1)} %shard_map.73.near_ref, bf16[9,256,256]{2,1,0:T(8,128)(2,1)S(1)} %copy-done, bf16[4,2,64,256]{3,2,1,0:T(8,128)(2,1)S(1)} %copy-done.1), custom_call_target="tpu_custom_call" | custom-call | flops 402653184 | bytes 2000000 | tf_op jit(solution)/shard_map/pallas_call | solution.py:270
  50.3 3.1 %collective-permute-done.6.far_halo = bf16[4,64,256]{2,1,0:T(8,128)(2,1)S(1)} collective-permute-done((bf16[4,64,256]{2,1,0:T(8,128)(2,1)S(1)}, bf16[4,64,256]{2,1,0:T(8,128)(2,1)S(1)}, u32[]{:S(2)}, u32[]{:S(2)}) %collective-permute-start.6) | collective-permute-done | bytes 131104 | tf_op jit(solution)/shard_map/ppermute | solution.py:18
  53.4 0.0 collective-permute-done.7.near_halo
  53.4 1.1 %shard_map.75 = bf16[4,2,64,256]{3,2,1,0:T(8,128)(2,1)} custom-call(f32[256,256]{1,0:T(8,128)S(1)} %get-tuple-element.15.far_total, bf16[4,64,256]{2,1,0:T(8,128)(2,1)S(1)} %collective-permute-done.6.far_halo, f32[256,256]{1,0:T(8,128)S(1)} %get-tuple-element.16.near_total, bf16[4,64,256]{2,1,0:T(8,128)(2,1)S(1)} %collective-permute-done.7.near_halo, ...), custom_call_target="tpu_custom_call" | custom-call | flops 201326592 | bytes 2000000 | tf_op jit(solution)/shard_map/pallas_call | solution.py:273
  (1 shorter events, 0.0 us)
Async XLA Ops:
  0.0 5.8 %copy-start = (bf16[9,256,256]{2,1,0:T(8,128)(2,1)S(1)}, bf16[9,256,256]{2,1,0:T(8,128)(2,1)}, u32[]{:S(2)}) copy-start(bf16[9,256,256]{2,1,0:T(8,128)(2,1)} %weight_ref.7) | copy-start | bytes 3538948
  0.0 1.0 %copy-start.2 = (bf16[4,2,64,256]{3,2,1,0:T(8,128)(2,1)S(1)}, bf16[4,2,64,256]{3,2,1,0:T(8,128)(2,1)}, u32[]{:S(2)}) copy-start(bf16[4,2,64,256]{3,2,1,0:T(8,128)(2,1)} %x_ref.3) | copy-start | bytes 786436
  1.1 7.8 %collective-permute-start = (bf16[4,64,256]{2,1,0:T(8,128)(2,1)S(1)}, bf16[4,64,256]{2,1,0:T(8,128)(2,1)S(1)}, u32[]{:S(2)}, u32[]{:S(2)}) collective-permute-start(bf16[4,64,256]{2,1,0:T(8,128)(2,1)S(1)} %get-tuple-element.11), channel_id=1, source_target_pairs={{1,2},{2,1},{5,6},{6,5},{9,10},{10,9},{13,14},{14,13},{17,18},{18,... | collective-permute-start | bytes 393224 | tf_op jit(solution)/shard_map/ppermute | solution.py:18
  3.8 5.0 %collective-permute-start.1 = (bf16[4,64,256]{2,1,0:T(8,128)(2,1)S(1)}, bf16[4,64,256]{2,1,0:T(8,128)(2,1)S(1)}, u32[]{:S(2)}, u32[]{:S(2)}) collective-permute-start(bf16[4,64,256]{2,1,0:T(8,128)(2,1)S(1)} %get-tuple-element.12), channel_id=1, source_target_pairs={{0,1},{2,3},{1,0},{3,2},{4,5},{6,7},{5,4},{7,6},{8,9},{10,11},{9,8... | collective-permute-start | bytes 393224 | tf_op jit(solution)/shard_map/ppermute | solution.py:18
  6.4 19.9 %copy-start.1 = (bf16[4,2,64,256]{3,2,1,0:T(8,128)(2,1)S(1)}, bf16[4,2,64,256]{3,2,1,0:T(8,128)(2,1)}, u32[]{:S(2)}) copy-start(bf16[4,2,64,256]{3,2,1,0:T(8,128)(2,1)} %cot_ref.3) | copy-start | bytes 786436
  6.4 19.9 %copy-start.3 = (bf16[256,256]{1,0:T(8,128)(2,1)S(1)}, bf16[256,256]{1,0:T(8,128)(2,1)}, u32[]{:S(2)}) copy-start(bf16[256,256]{1,0:T(8,128)(2,1)} %proj_ref.1) | copy-start | bytes 393220
  6.4 20.2 %copy-start.4 = (f32[25,256]{1,0:T(8,128)S(1)}, f32[25,256]{1,0:T(8,128)}, u32[]{:S(2)}) copy-start(f32[25,256]{1,0:T(8,128)} %mixing_ref.1) | copy-start | bytes 76804
  6.4 20.2 %copy-start.5 = (s32[512]{0:T(512)S(1)}, s32[512]{0:T(512)}, u32[]{:S(2)}) copy-start(s32[512]{0:T(512)} %offsets_ref.1) | copy-start | bytes 6148
  9.2 18.7 %collective-permute-start.3 = (bf16[4,2,64,256]{3,2,1,0:T(8,128)(2,1)S(1)}, bf16[4,2,64,256]{3,2,1,0:T(8,128)(2,1)S(1)}, u32[]{:S(2)}, u32[]{:S(2)}) collective-permute-start(bf16[4,2,64,256]{3,2,1,0:T(8,128)(2,1)S(1)} %shard_map.66.after_ref.own_ref), channel_id=1, source_target_pairs={{0,4},{8,12},{16,20},{24,28},{32,36},{40,44},{48,52},{56,60},{64,6... | collective-permute-start | bytes 786440 | tf_op jit(solution)/shard_map/ppermute | solution.py:27
  13.1 17.6 %collective-permute-start.2 = (bf16[4,2,64,256]{3,2,1,0:T(8,128)(2,1)S(1)}, bf16[4,2,64,256]{3,2,1,0:T(8,128)(2,1)S(1)}, u32[]{:S(2)}, u32[]{:S(2)}) collective-permute-start(bf16[4,2,64,256]{3,2,1,0:T(8,128)(2,1)S(1)} %shard_map.66.after_ref.own_ref), channel_id=1, source_target_pairs={{4,8},{12,16},{20,24},{28,32},{36,40},{44,48},{52,56},{60,64},{68,... | collective-permute-start | bytes 786440 | tf_op jit(solution)/shard_map/ppermute | solution.py:27
  31.1 10.8 %collective-permute-start.5 = (bf16[4,2,64,256]{3,2,1,0:T(8,128)(2,1)S(1)}, bf16[4,2,64,256]{3,2,1,0:T(8,128)(2,1)S(1)}, u32[]{:S(2)}, u32[]{:S(2)}) collective-permute-start(bf16[4,2,64,256]{3,2,1,0:T(8,128)(2,1)S(1)} %shard_map.70.own_ref), channel_id=1, source_target_pairs={{0,4},{8,12},{16,20},{24,28},{32,36},{40,44},{48,52},{56,60},{64,6... | collective-permute-start | bytes 786440 | tf_op jit(solution)/shard_map/ppermute | solution.py:27
  33.0 12.5 %collective-permute-start.4 = (bf16[4,2,64,256]{3,2,1,0:T(8,128)(2,1)S(1)}, bf16[4,2,64,256]{3,2,1,0:T(8,128)(2,1)S(1)}, u32[]{:S(2)}, u32[]{:S(2)}) collective-permute-start(bf16[4,2,64,256]{3,2,1,0:T(8,128)(2,1)S(1)} %shard_map.70.own_ref), channel_id=1, source_target_pairs={{4,8},{12,16},{20,24},{28,32},{36,40},{44,48},{52,56},{60,64},{68,... | collective-permute-start | bytes 786440 | tf_op jit(solution)/shard_map/ppermute | solution.py:27
  45.6 7.8 %collective-permute-start.6 = (bf16[4,64,256]{2,1,0:T(8,128)(2,1)S(1)}, bf16[4,64,256]{2,1,0:T(8,128)(2,1)S(1)}, u32[]{:S(2)}, u32[]{:S(2)}) collective-permute-start(bf16[4,64,256]{2,1,0:T(8,128)(2,1)S(1)} %shard_map.72.far_ref), channel_id=1, source_target_pairs={{1,2},{2,1},{5,6},{6,5},{9,10},{10,9},{13,14},{14,13},{17,18},{18,... | collective-permute-start | bytes 393224 | tf_op jit(solution)/shard_map/ppermute | solution.py:18
  47.7 5.7 %collective-permute-start.7 = (bf16[4,64,256]{2,1,0:T(8,128)(2,1)S(1)}, bf16[4,64,256]{2,1,0:T(8,128)(2,1)S(1)}, u32[]{:S(2)}, u32[]{:S(2)}) collective-permute-start(bf16[4,64,256]{2,1,0:T(8,128)(2,1)S(1)} %shard_map.73.near_ref), channel_id=1, source_target_pairs={{0,1},{2,3},{1,0},{3,2},{4,5},{6,7},{5,4},{7,6},{8,9},{10,11},{9,8... | collective-permute-start | bytes 393224 | tf_op jit(solution)/shard_map/ppermute | solution.py:18

commit v6 on v5

--- a/solution.py
+++ b/solution.py
@@ -22,7 +22,7 @@
     frames, bands = lax.axis_size("tm"), lax.axis_size("lat")
     pairs = []
     for band in range(bands):
-        for i in range((band + turn) % 2, frames - 1, 2):
+        for i in range((min(band, 1) + turn) % 2, frames - 1, 2):
             pairs.append((i * bands + band, (i + 1) * bands + band))
     return lax.ppermute(value, ("tm", "lat"), pairs + [(j, i) for i, j in pairs])
 
@@ -129,7 +129,7 @@
 
 
 def sided(first_ref, second_ref, run):
-    side = lax.rem(lax.axis_index("tm") + lax.axis_index("lat"), 2)
+    side = lax.rem(lax.axis_index("tm") + jnp.minimum(lax.axis_index("lat"), 1), 2)
 
     @pl.when(side == 1)
     def _():

time: 54.8 us -> 53.9 us (0.984)
  starting transfers between devices: 35.6 us -> 30.7 us
  waiting for transfers between devices: 12.4 us -> 16.5 us
    ppermute x4, starting transfers between devices: 27.1 us -> 22.2 us  [crossed(): lax.ppermute(value, ('tm', 'lat'), pairs + [(j, i) for i, j in pairs])]
    ppermute x4, waiting for transfers between devices: 6.83 us -> 10.8 us  [crossed(): lax.ppermute(value, ('tm', 'lat'), pairs + [(j, i) for i, j in pairs])]
where the time goes in v6:
time: 53.9 us; the launch traced here: 53.6 us
  starting transfers between devices  30.7 us (57%)
  waiting for transfers between devices  16.5 us (31%)
  Pallas kernels  5.15 us (10%)
  local copies, waits for them, and re-layouts  1.07 us (2%)
    ppermute x4, starting transfers between devices, crossed(): lax.ppermute(value, ('tm', 'lat'), pairs + [(j, i) for i, j in pairs])  22.2 us
    ppermute x4, waiting for transfers between devices, crossed(): lax.ppermute(value, ('tm', 'lat'), pairs + [(j, i) for i, j in pairs])  10.8 us
    ppermute x4, starting transfers between devices, swap(): return lax.ppermute(value, axis, pairs + [(j, i) for i, j in pairs])  8.51 us
    ppermute x4, waiting for transfers between devices, swap(): return lax.ppermute(value, axis, pairs + [(j, i) for i, j in pairs])  5.61 us
    pallas_call x1, Pallas kernels, body(): call(table_kernel, (table, table), [SMEM] + [VMEM] * 2, (1000000, 200000))  1.12 us
    pallas_call x1, Pallas kernels, body(): call(final_kernel, block, [VMEM] * 5, (2 * tap, 2000000), out_specs=pl.Bl...  1.08 us
  transfers between devices with their start and end apart: 8, of which 5 were waited for; matrix products, arithmetic and copies ran while one was open for 0% of the time, Pallas kernels for 6%

profile of v6, /device:TPU:6, one launch (start us, length us, event | category | flops | bytes accessed | tf_op | source)
XLA Modules:
  0.0 53.6 jit_solution(14971842646520619737)
XLA Ops:
  0.0 0.0 copy-start
  0.0 0.0 copy-start.2
  0.0 1.0 %copy-done.2 = bf16[4,2,64,256]{3,2,1,0:T(8,128)(2,1)S(1)} copy-done((bf16[4,2,64,256]{3,2,1,0:T(8,128)(2,1)S(1)}, bf16[4,2,64,256]{3,2,1,0:T(8,128)(2,1)}, u32[]{:S(2)}) %copy-start.2) | copy-done | bytes 262168
  1.1 2.8 %collective-permute-start = (bf16[4,64,256]{2,1,0:T(8,128)(2,1)S(1)}, bf16[4,64,256]{2,1,0:T(8,128)(2,1)S(1)}, u32[]{:S(2)}, u32[]{:S(2)}) collective-permute-start(bf16[4,64,256]{2,1,0:T(8,128)(2,1)S(1)} %get-tuple-element.11), channel_id=1, source_target_pairs={{1,2},{2,1},{5,6},{6,5},{9,10},{10,9},{13,14},{14,13},{17,18},{18,... | collective-permute-start | bytes 393224 | tf_op jit(solution)/shard_map/ppermute | solution.py:18
  3.8 1.9 %collective-permute-start.1 = (bf16[4,64,256]{2,1,0:T(8,128)(2,1)S(1)}, bf16[4,64,256]{2,1,0:T(8,128)(2,1)S(1)}, u32[]{:S(2)}, u32[]{:S(2)}) collective-permute-start(bf16[4,64,256]{2,1,0:T(8,128)(2,1)S(1)} %get-tuple-element.12), channel_id=1, source_target_pairs={{0,1},{2,3},{1,0},{3,2},{4,5},{6,7},{5,4},{7,6},{8,9},{10,11},{9,8... | collective-permute-start | bytes 393224 | tf_op jit(solution)/shard_map/ppermute | solution.py:18
  5.8 0.0 copy-done
  5.8 0.6 %shard_map.64.total_ref = f32[2,256,256]{2,1,0:T(8,128)S(1)} custom-call(bf16[4,2,64,256]{3,2,1,0:T(8,128)(2,1)S(1)} %copy-done.2, bf16[9,256,256]{2,1,0:T(8,128)(2,1)S(1)} %copy-done), custom_call_target="tpu_custom_call" | custom-call | flops 402653184 | bytes 2000000 | tf_op jit(solution)/shard_map/pallas_call | solution.py:234
  6.4 0.0 copy-start.1
  6.4 0.0 copy-start.3
  6.4 0.0 copy-start.4
  6.4 0.0 copy-start.5
  6.4 2.5 %collective-permute-done.far_ref = bf16[4,64,256]{2,1,0:T(8,128)(2,1)S(1)} collective-permute-done((bf16[4,64,256]{2,1,0:T(8,128)(2,1)S(1)}, bf16[4,64,256]{2,1,0:T(8,128)(2,1)S(1)}, u32[]{:S(2)}, u32[]{:S(2)}) %collective-permute-start) | collective-permute-done | bytes 131104 | tf_op jit(solution)/shard_map/ppermute | solution.py:18
  8.9 0.0 collective-permute-done.1.near_ref
  8.9 0.4 shard_map.66.after_ref.own_ref
  9.2 14.1 %collective-permute-start.3 = (bf16[4,2,64,256]{3,2,1,0:T(8,128)(2,1)S(1)}, bf16[4,2,64,256]{3,2,1,0:T(8,128)(2,1)S(1)}, u32[]{:S(2)}, u32[]{:S(2)}) collective-permute-start(bf16[4,2,64,256]{3,2,1,0:T(8,128)(2,1)S(1)} %shard_map.66.after_ref.own_ref), channel_id=1, source_target_pairs={{0,4},{8,12},{16,20},{24,28},{32,36},{40,44},{48,52},{56,60},{64,6... | collective-permute-start | bytes 786440 | tf_op jit(solution)/shard_map/ppermute | solution.py:27
  23.4 1.9 %collective-permute-start.2 = (bf16[4,2,64,256]{3,2,1,0:T(8,128)(2,1)S(1)}, bf16[4,2,64,256]{3,2,1,0:T(8,128)(2,1)S(1)}, u32[]{:S(2)}, u32[]{:S(2)}) collective-permute-start(bf16[4,2,64,256]{3,2,1,0:T(8,128)(2,1)S(1)} %shard_map.66.after_ref.own_ref), channel_id=1, source_target_pairs={{4,8},{12,16},{20,24},{28,32},{36,40},{44,48},{52,56},{60,64},{68,... | collective-permute-start | bytes 786440 | tf_op jit(solution)/shard_map/ppermute | solution.py:27
  25.3 0.0 copy-done.1
  25.3 0.0 copy-done.3
  25.3 0.3 shard_map.69.hidden_ref
  25.6 0.0 copy-done.4
  25.6 0.0 copy-done.5
  25.6 1.1 %shard_map.67 = (f32[36,256]{1,0:T(8,128)S(1)}, f32[36,256]{1,0:T(8,128)S(1)}) custom-call(s32[512]{0:T(512)S(1)} %copy-done.5, f32[25,256]{1,0:T(8,128)S(1)} %copy-done.4, bf16[4,2,64,256]{3,2,1,0:T(8,128)(2,1)S(1)} %shard_map.66.after_ref.own_ref), custom_call_target="tpu_custom_call" | custom-call | flops 1000000 | bytes 200000 | tf_op jit(solution)/shard_map/pallas_call | solution.py:252
  26.7 0.2 shard_map.68.total_ref
  26.9 0.8 %collective-permute-done.3.first_ref = bf16[4,2,64,256]{3,2,1,0:T(8,128)(2,1)S(1)} collective-permute-done((bf16[4,2,64,256]{3,2,1,0:T(8,128)(2,1)S(1)}, bf16[4,2,64,256]{3,2,1,0:T(8,128)(2,1)S(1)}, u32[]{:S(2)}, u32[]{:S(2)}) %collective-permute-start.3) | collective-permute-done | bytes 262176 | tf_op jit(solution)/shard_map/ppermute | solution.py:27
  27.7 3.9 %collective-permute-done.2.second_ref = bf16[4,2,64,256]{3,2,1,0:T(8,128)(2,1)S(1)} collective-permute-done((bf16[4,2,64,256]{3,2,1,0:T(8,128)(2,1)S(1)}, bf16[4,2,64,256]{3,2,1,0:T(8,128)(2,1)S(1)}, u32[]{:S(2)}, u32[]{:S(2)}) %collective-permute-start.2) | collective-permute-done | bytes 262176 | tf_op jit(solution)/shard_map/ppermute | solution.py:27
  31.6 0.4 shard_map.70.own_ref
  32.1 4.2 %collective-permute-start.5 = (bf16[4,2,64,256]{3,2,1,0:T(8,128)(2,1)S(1)}, bf16[4,2,64,256]{3,2,1,0:T(8,128)(2,1)S(1)}, u32[]{:S(2)}, u32[]{:S(2)}) collective-permute-start(bf16[4,2,64,256]{3,2,1,0:T(8,128)(2,1)S(1)} %shard_map.70.own_ref), channel_id=1, source_target_pairs={{0,4},{8,12},{16,20},{24,28},{32,36},{40,44},{48,52},{56,60},{64,6... | collective-permute-start | bytes 786440 | tf_op jit(solution)/shard_map/ppermute | solution.py:27
  36.3 1.9 %collective-permute-start.4 = (bf16[4,2,64,256]{3,2,1,0:T(8,128)(2,1)S(1)}, bf16[4,2,64,256]{3,2,1,0:T(8,128)(2,1)S(1)}, u32[]{:S(2)}, u32[]{:S(2)}) collective-permute-start(bf16[4,2,64,256]{3,2,1,0:T(8,128)(2,1)S(1)} %shard_map.70.own_ref), channel_id=1, source_target_pairs={{4,8},{12,16},{20,24},{28,32},{36,40},{44,48},{52,56},{60,64},{68,... | collective-permute-start | bytes 786440 | tf_op jit(solution)/shard_map/ppermute | solution.py:27
  38.2 0.2 shard_map.71.total_ref
  38.4 6.1 %collective-permute-done.5.first_ref = bf16[4,2,64,256]{3,2,1,0:T(8,128)(2,1)S(1)} collective-permute-done((bf16[4,2,64,256]{3,2,1,0:T(8,128)(2,1)S(1)}, bf16[4,2,64,256]{3,2,1,0:T(8,128)(2,1)S(1)}, u32[]{:S(2)}, u32[]{:S(2)}) %collective-permute-start.5) | collective-permute-done | bytes 262176 | tf_op jit(solution)/shard_map/ppermute | solution.py:27
  44.6 0.0 collective-permute-done.4.second_ref
  44.6 0.1 shard_map.72.far_ref
  44.7 1.9 %collective-permute-start.6 = (bf16[4,64,256]{2,1,0:T(8,128)(2,1)S(1)}, bf16[4,64,256]{2,1,0:T(8,128)(2,1)S(1)}, u32[]{:S(2)}, u32[]{:S(2)}) collective-permute-start(bf16[4,64,256]{2,1,0:T(8,128)(2,1)S(1)} %shard_map.72.far_ref), channel_id=1, source_target_pairs={{1,2},{2,1},{5,6},{6,5},{9,10},{10,9},{13,14},{14,13},{17,18},{18,... | collective-permute-start | bytes 393224 | tf_op jit(solution)/shard_map/ppermute | solution.py:18
  46.6 0.2 shard_map.73.near_ref
  46.8 1.9 %collective-permute-start.7 = (bf16[4,64,256]{2,1,0:T(8,128)(2,1)S(1)}, bf16[4,64,256]{2,1,0:T(8,128)(2,1)S(1)}, u32[]{:S(2)}, u32[]{:S(2)}) collective-permute-start(bf16[4,64,256]{2,1,0:T(8,128)(2,1)S(1)} %shard_map.73.near_ref), channel_id=1, source_target_pairs={{0,1},{2,3},{1,0},{3,2},{4,5},{6,7},{5,4},{7,6},{8,9},{10,11},{9,8... | collective-permute-start | bytes 393224 | tf_op jit(solution)/shard_map/ppermute | solution.py:18
  48.7 0.6 %shard_map.74 = (f32[256,256]{1,0:T(8,128)S(1)}, f32[256,256]{1,0:T(8,128)S(1)}) custom-call(bf16[4,64,256]{2,1,0:T(8,128)(2,1)S(1)} %shard_map.72.far_ref, bf16[4,64,256]{2,1,0:T(8,128)(2,1)S(1)} %shard_map.73.near_ref, bf16[9,256,256]{2,1,0:T(8,128)(2,1)S(1)} %copy-done, bf16[4,2,64,256]{3,2,1,0:T(8,128)(2,1)S(1)} %copy-done.1), custom_call_target="tpu_custom_call" | custom-call | flops 402653184 | bytes 2000000 | tf_op jit(solution)/shard_map/pallas_call | solution.py:270
  49.4 3.1 %collective-permute-done.6.far_halo = bf16[4,64,256]{2,1,0:T(8,128)(2,1)S(1)} collective-permute-done((bf16[4,64,256]{2,1,0:T(8,128)(2,1)S(1)}, bf16[4,64,256]{2,1,0:T(8,128)(2,1)S(1)}, u32[]{:S(2)}, u32[]{:S(2)}) %collective-permute-start.6) | collective-permute-done | bytes 131104 | tf_op jit(solution)/shard_map/ppermute | solution.py:18
  52.5 0.0 collective-permute-done.7.near_halo
  52.5 1.1 %shard_map.75 = bf16[4,2,64,256]{3,2,1,0:T(8,128)(2,1)} custom-call(f32[256,256]{1,0:T(8,128)S(1)} %get-tuple-element.15.far_total, bf16[4,64,256]{2,1,0:T(8,128)(2,1)S(1)} %collective-permute-done.6.far_halo, f32[256,256]{1,0:T(8,128)S(1)} %get-tuple-element.16.near_total, bf16[4,64,256]{2,1,0:T(8,128)(2,1)S(1)} %collective-permute-done.7.near_halo, ...), custom_call_target="tpu_custom_call" | custom-call | flops 201326592 | bytes 2000000 | tf_op jit(solution)/shard_map/pallas_call | solution.py:273
  (1 shorter events, 0.0 us)
Async XLA Ops:
  0.0 5.8 %copy-start = (bf16[9,256,256]{2,1,0:T(8,128)(2,1)S(1)}, bf16[9,256,256]{2,1,0:T(8,128)(2,1)}, u32[]{:S(2)}) copy-start(bf16[9,256,256]{2,1,0:T(8,128)(2,1)} %weight_ref.7) | copy-start | bytes 3538948
  0.0 1.0 %copy-start.2 = (bf16[4,2,64,256]{3,2,1,0:T(8,128)(2,1)S(1)}, bf16[4,2,64,256]{3,2,1,0:T(8,128)(2,1)}, u32[]{:S(2)}) copy-start(bf16[4,2,64,256]{3,2,1,0:T(8,128)(2,1)} %x_ref.3) | copy-start | bytes 786436
  1.1 7.8 %collective-permute-start = (bf16[4,64,256]{2,1,0:T(8,128)(2,1)S(1)}, bf16[4,64,256]{2,1,0:T(8,128)(2,1)S(1)}, u32[]{:S(2)}, u32[]{:S(2)}) collective-permute-start(bf16[4,64,256]{2,1,0:T(8,128)(2,1)S(1)} %get-tuple-element.11), channel_id=1, source_target_pairs={{1,2},{2,1},{5,6},{6,5},{9,10},{10,9},{13,14},{14,13},{17,18},{18,... | collective-permute-start | bytes 393224 | tf_op jit(solution)/shard_map/ppermute | solution.py:18
  3.8 5.0 %collective-permute-start.1 = (bf16[4,64,256]{2,1,0:T(8,128)(2,1)S(1)}, bf16[4,64,256]{2,1,0:T(8,128)(2,1)S(1)}, u32[]{:S(2)}, u32[]{:S(2)}) collective-permute-start(bf16[4,64,256]{2,1,0:T(8,128)(2,1)S(1)} %get-tuple-element.12), channel_id=1, source_target_pairs={{0,1},{2,3},{1,0},{3,2},{4,5},{6,7},{5,4},{7,6},{8,9},{10,11},{9,8... | collective-permute-start | bytes 393224 | tf_op jit(solution)/shard_map/ppermute | solution.py:18
  6.4 19.0 %copy-start.1 = (bf16[4,2,64,256]{3,2,1,0:T(8,128)(2,1)S(1)}, bf16[4,2,64,256]{3,2,1,0:T(8,128)(2,1)}, u32[]{:S(2)}) copy-start(bf16[4,2,64,256]{3,2,1,0:T(8,128)(2,1)} %cot_ref.3) | copy-start | bytes 786436
  6.4 18.9 %copy-start.3 = (bf16[256,256]{1,0:T(8,128)(2,1)S(1)}, bf16[256,256]{1,0:T(8,128)(2,1)}, u32[]{:S(2)}) copy-start(bf16[256,256]{1,0:T(8,128)(2,1)} %proj_ref.1) | copy-start | bytes 393220
  6.4 19.2 %copy-start.4 = (f32[25,256]{1,0:T(8,128)S(1)}, f32[25,256]{1,0:T(8,128)}, u32[]{:S(2)}) copy-start(f32[25,256]{1,0:T(8,128)} %mixing_ref.1) | copy-start | bytes 76804
  6.4 19.2 %copy-start.5 = (s32[512]{0:T(512)S(1)}, s32[512]{0:T(512)}, u32[]{:S(2)}) copy-start(s32[512]{0:T(512)} %offsets_ref.1) | copy-start | bytes 6148
  9.2 18.5 %collective-permute-start.3 = (bf16[4,2,64,256]{3,2,1,0:T(8,128)(2,1)S(1)}, bf16[4,2,64,256]{3,2,1,0:T(8,128)(2,1)S(1)}, u32[]{:S(2)}, u32[]{:S(2)}) collective-permute-start(bf16[4,2,64,256]{3,2,1,0:T(8,128)(2,1)S(1)} %shard_map.66.after_ref.own_ref), channel_id=1, source_target_pairs={{0,4},{8,12},{16,20},{24,28},{32,36},{40,44},{48,52},{56,60},{64,6... | collective-permute-start | bytes 786440 | tf_op jit(solution)/shard_map/ppermute | solution.py:27
  23.4 8.3 %collective-permute-start.2 = (bf16[4,2,64,256]{3,2,1,0:T(8,128)(2,1)S(1)}, bf16[4,2,64,256]{3,2,1,0:T(8,128)(2,1)S(1)}, u32[]{:S(2)}, u32[]{:S(2)}) collective-permute-start(bf16[4,2,64,256]{3,2,1,0:T(8,128)(2,1)S(1)} %shard_map.66.after_ref.own_ref), channel_id=1, source_target_pairs={{4,8},{12,16},{20,24},{28,32},{36,40},{44,48},{52,56},{60,64},{68,... | collective-permute-start | bytes 786440 | tf_op jit(solution)/shard_map/ppermute | solution.py:27
  32.1 12.5 %collective-permute-start.5 = (bf16[4,2,64,256]{3,2,1,0:T(8,128)(2,1)S(1)}, bf16[4,2,64,256]{3,2,1,0:T(8,128)(2,1)S(1)}, u32[]{:S(2)}, u32[]{:S(2)}) collective-permute-start(bf16[4,2,64,256]{3,2,1,0:T(8,128)(2,1)S(1)} %shard_map.70.own_ref), channel_id=1, source_target_pairs={{0,4},{8,12},{16,20},{24,28},{32,36},{40,44},{48,52},{56,60},{64,6... | collective-permute-start | bytes 786440 | tf_op jit(solution)/shard_map/ppermute | solution.py:27
  36.3 8.3 %collective-permute-start.4 = (bf16[4,2,64,256]{3,2,1,0:T(8,128)(2,1)S(1)}, bf16[4,2,64,256]{3,2,1,0:T(8,128)(2,1)S(1)}, u32[]{:S(2)}, u32[]{:S(2)}) collective-permute-start(bf16[4,2,64,256]{3,2,1,0:T(8,128)(2,1)S(1)} %shard_map.70.own_ref), channel_id=1, source_target_pairs={{4,8},{12,16},{20,24},{28,32},{36,40},{44,48},{52,56},{60,64},{68,... | collective-permute-start | bytes 786440 | tf_op jit(solution)/shard_map/ppermute | solution.py:27
  44.7 7.8 %collective-permute-start.6 = (bf16[4,64,256]{2,1,0:T(8,128)(2,1)S(1)}, bf16[4,64,256]{2,1,0:T(8,128)(2,1)S(1)}, u32[]{:S(2)}, u32[]{:S(2)}) collective-permute-start(bf16[4,64,256]{2,1,0:T(8,128)(2,1)S(1)} %shard_map.72.far_ref), channel_id=1, source_target_pairs={{1,2},{2,1},{5,6},{6,5},{9,10},{10,9},{13,14},{14,13},{17,18},{18,... | collective-permute-start | bytes 393224 | tf_op jit(solution)/shard_map/ppermute | solution.py:18
  46.8 5.7 %collective-permute-start.7 = (bf16[4,64,256]{2,1,0:T(8,128)(2,1)S(1)}, bf16[4,64,256]{2,1,0:T(8,128)(2,1)S(1)}, u32[]{:S(2)}, u32[]{:S(2)}) collective-permute-start(bf16[4,64,256]{2,1,0:T(8,128)(2,1)S(1)} %shard_map.73.near_ref), channel_id=1, source_target_pairs={{0,1},{2,3},{1,0},{3,2},{4,5},{6,7},{5,4},{7,6},{8,9},{10,11},{9,8... | collective-permute-start | bytes 393224 | tf_op jit(solution)/shard_map/ppermute | solution.py:18

commit v7 on v6

--- a/solution.py
+++ b/solution.py
@@ -2,6 +2,7 @@
 
 import jax
 import jax.numpy as jnp
+import numpy as np
 from jax import lax
 from jax.experimental import pallas as pl
 from jax.experimental.pallas import tpu as pltpu
@@ -18,12 +19,21 @@
     return lax.ppermute(value, axis, pairs + [(j, i) for i, j in pairs])
 
 
+def turn_of(link, band, where):
+    place = link % 16
+    plain = 2 * (place % 2)
+    turned = where(place % 8 == 7, 1, where(place < 8, plain, 2 - plain))
+    return where(band == 0, plain, turned)
+
+
 def crossed(value, turn):
     frames, bands = lax.axis_size("tm"), lax.axis_size("lat")
-    pairs = []
-    for band in range(bands):
-        for i in range((min(band, 1) + turn) % 2, frames - 1, 2):
-            pairs.append((i * bands + band, (i + 1) * bands + band))
+    pairs = [
+        (i * bands + band, (i + 1) * bands + band)
+        for band in range(bands)
+        for i in range(frames - 1)
+        if turn_of(i, band, np.where) == turn
+    ]
     return lax.ppermute(value, ("tm", "lat"), pairs + [(j, i) for i, j in pairs])
 
 
@@ -128,19 +138,16 @@
     mixed(table_ref, [(own_ref, 0)], range(2), lambda *_: None, store)
 
 
-def sided(first_ref, second_ref, run):
-    side = lax.rem(lax.axis_index("tm") + jnp.minimum(lax.axis_index("lat"), 1), 2)
-
-    @pl.when(side == 1)
-    def _():
-        run(first_ref, second_ref)
-
-    @pl.when(side == 0)
-    def _():
-        run(second_ref, first_ref)
-
-
-def mid_kernel(table_ref, second_ref, total_ref, first_ref, hidden_ref, out_ref):
+def sided(refs, run):
+    block, band = lax.axis_index("tm"), lax.axis_index("lat")
+    left, right = turn_of(block + 15, band, jnp.where), turn_of(block, band, jnp.where)
+    for i in range(3):
+        for j in range(3):
+            if i != j:
+                pl.when((left == i) & (right == j))(functools.partial(run, refs[i], refs[j]))
+
+
+def mid_kernel(table_ref, third_ref, second_ref, first_ref, total_ref, hidden_ref, out_ref):
     frames = out_ref.shape[0]
 
     def store(frame, row, pre):
@@ -152,7 +159,7 @@
         sources = [(before, -frames), (after, frames)]
         mixed(table_ref, sources, range(2), lambda frame, row: total_ref[frame, row], store)
 
-    sided(first_ref, second_ref, run)
+    sided((first_ref, second_ref, third_ref), run)
 
 
 def hidden_kernel(cot_ref, proj_ref, out_ref):
@@ -165,7 +172,7 @@
     near_ref[...] = x_ref[:, 1 - parity]
 
 
-def sum_kernel(far, table_ref, second_ref, total_ref, first_ref, out_ref):
+def sum_kernel(far, table_ref, third_ref, second_ref, first_ref, total_ref, out_ref):
     frames = out_ref.shape[0]
     parity = lax.rem(lax.axis_index("lat"), 2)
     row = parity if far else 1 - parity
@@ -177,7 +184,7 @@
         sources = [(before, -frames), (after, frames)]
         mixed(table_ref, sources, [row], lambda frame, _: total_ref[frame, row], store)
 
-    sided(first_ref, second_ref, run)
+    sided((first_ref, second_ref, third_ref), run)
 
 
 def back_local_kernel(far_ref, near_ref, weight_ref, cot_ref, far_total, near_total):
@@ -252,15 +259,17 @@
     reads, read_by = call(table_kernel, (table, table), [SMEM] + [VMEM] * 2, (1_000_000, 200_000))(
         offsets, mixing, conv_out
     )
-    first, second = crossed(conv_out, 0), crossed(conv_out, 1)
+    first, second, third = [crossed(conv_out, turn) for turn in range(3)]
     hidden = call(hidden_kernel, wide, [VMEM] * 2, (67_000_000, 1_000_000))(cotangent, proj_weight)
     own = call(own_kernel, wide, [VMEM] * 2, (10_000_000, 1_000_000))(reads, conv_out)
-    g_pre = call(mid_kernel, block, [VMEM] * 5, (10_000_000, 1_400_000))(reads, second, own, first, hidden)
-    first, second = crossed(g_pre, 0), crossed(g_pre, 1)
+    g_pre = call(mid_kernel, block, [VMEM] * 6, (10_000_000, 1_400_000))(
+        reads, third, second, first, own, hidden
+    )
+    first, second, third = [crossed(g_pre, turn) for turn in range(3)]
     own = call(own_kernel, wide, [VMEM] * 2, (10_000_000, 1_000_000))(read_by, g_pre)
     far, near = [
-        call(functools.partial(sum_kernel, is_far), edge, [VMEM] * 4, (5_000_000, 700_000))(
-            read_by, second, own, first
+        call(functools.partial(sum_kernel, is_far), edge, [VMEM] * 5, (5_000_000, 700_000))(
+            read_by, third, second, first, own
         )
         for is_far in (True, False)
     ]

time: 53.9 us -> 52.7 us (0.978)
  waiting for transfers between devices: 16.5 us -> 12.3 us
  starting transfers between devices: 30.7 us -> 33.5 us
    ppermute x4 -> x6, waiting for transfers between devices: 10.8 us -> 6.74 us  [crossed(): lax.ppermute(value, ('tm', 'lat'), pairs + [(j, i) for i, j in pairs])]
    ppermute x4 -> x6, starting transfers between devices: 22.2 us -> 24.9 us  [crossed(): lax.ppermute(value, ('tm', 'lat'), pairs + [(j, i) for i, j in pairs])]
  transfers between devices with their start and end apart: 8 -> 10, of which waited for: 5 -> 4; matrix products, arithmetic and copies ran while one was open for 0% -> 0% of each run, Pallas kernels for 6% -> 6%
where the time goes in v7:
time: 52.7 us; the launch traced here: 52.3 us
  starting transfers between devices  33.5 us (64%)
  waiting for transfers between devices  12.3 us (23%)
  Pallas kernels  5.22 us (10%)
  local copies, waits for them, and re-layouts  1.07 us (2%)
    ppermute x6, starting transfers between devices, crossed(): lax.ppermute(value, ('tm', 'lat'), pairs + [(j, i) for i, j in pairs])  24.9 us
    ppermute x4, starting transfers between devices, swap(): return lax.ppermute(value, axis, pairs + [(j, i) for i, j in pairs])  8.51 us
    ppermute x6, waiting for transfers between devices, crossed(): lax.ppermute(value, ('tm', 'lat'), pairs + [(j, i) for i, j in pairs])  6.74 us
    ppermute x4, waiting for transfers between devices, swap(): return lax.ppermute(value, axis, pairs + [(j, i) for i, j in pairs])  5.57 us
    pallas_call x1, Pallas kernels, body(): call(table_kernel, (table, table), [SMEM] + [VMEM] * 2, (1000000, 200000))  1.12 us
    pallas_call x1, Pallas kernels, body(): call(final_kernel, block, [VMEM] * 5, (2 * tap, 2000000), out_specs=pl.Bl...  1.08 us
    unnamed x12, local copies, waits for them, and re-layouts  1.07 us
  transfers between devices with their start and end apart: 10, of which 4 were waited for; matrix products, arithmetic and copies ran while one was open for 0% of the time, Pallas kernels for 6%

profile of v7, /device:TPU:6, one launch (start us, length us, event | category | flops | bytes accessed | tf_op | source)
XLA Modules:
  0.0 52.3 jit_solution(13590300691856942711)
XLA Ops:
  0.0 0.0 copy-start
  0.0 0.0 copy-start.2
  0.0 1.0 %copy-done.2 = bf16[4,2,64,256]{3,2,1,0:T(8,128)(2,1)S(1)} copy-done((bf16[4,2,64,256]{3,2,1,0:T(8,128)(2,1)S(1)}, bf16[4,2,64,256]{3,2,1,0:T(8,128)(2,1)}, u32[]{:S(2)}) %copy-start.2) | copy-done | bytes 262168
  1.1 2.8 %collective-permute-start = (bf16[4,64,256]{2,1,0:T(8,128)(2,1)S(1)}, bf16[4,64,256]{2,1,0:T(8,128)(2,1)S(1)}, u32[]{:S(2)}, u32[]{:S(2)}) collective-permute-start(bf16[4,64,256]{2,1,0:T(8,128)(2,1)S(1)} %get-tuple-element.11), channel_id=1, source_target_pairs={{1,2},{2,1},{5,6},{6,5},{9,10},{10,9},{13,14},{14,13},{17,18},{18,... | collective-permute-start | bytes 393224 | tf_op jit(solution)/shard_map/ppermute | solution.py:19
  3.8 1.9 %collective-permute-start.1 = (bf16[4,64,256]{2,1,0:T(8,128)(2,1)S(1)}, bf16[4,64,256]{2,1,0:T(8,128)(2,1)S(1)}, u32[]{:S(2)}, u32[]{:S(2)}) collective-permute-start(bf16[4,64,256]{2,1,0:T(8,128)(2,1)S(1)} %get-tuple-element.12), channel_id=1, source_target_pairs={{0,1},{2,3},{1,0},{3,2},{4,5},{6,7},{5,4},{7,6},{8,9},{10,11},{9,8... | collective-permute-start | bytes 393224 | tf_op jit(solution)/shard_map/ppermute | solution.py:19
  5.8 0.0 copy-done
  5.8 0.6 %shard_map.64.total_ref = f32[2,256,256]{2,1,0:T(8,128)S(1)} custom-call(bf16[4,2,64,256]{3,2,1,0:T(8,128)(2,1)S(1)} %copy-done.2, bf16[9,256,256]{2,1,0:T(8,128)(2,1)S(1)} %copy-done), custom_call_target="tpu_custom_call" | custom-call | flops 402653184 | bytes 2000000 | tf_op jit(solution)/shard_map/pallas_call | solution.py:241
  6.4 0.0 copy-start.1
  6.4 0.0 copy-start.3
  6.4 0.0 copy-start.4
  6.4 0.0 copy-start.5
  6.4 2.5 %collective-permute-done.far_ref = bf16[4,64,256]{2,1,0:T(8,128)(2,1)S(1)} collective-permute-done((bf16[4,64,256]{2,1,0:T(8,128)(2,1)S(1)}, bf16[4,64,256]{2,1,0:T(8,128)(2,1)S(1)}, u32[]{:S(2)}, u32[]{:S(2)}) %collective-permute-start) | collective-permute-done | bytes 131104 | tf_op jit(solution)/shard_map/ppermute | solution.py:19
  8.9 0.0 collective-permute-done.1.near_ref
  8.9 0.4 shard_map.66.after_ref.own_ref
  9.2 3.8 %collective-permute-start.4 = (bf16[4,2,64,256]{3,2,1,0:T(8,128)(2,1)S(1)}, bf16[4,2,64,256]{3,2,1,0:T(8,128)(2,1)S(1)}, u32[]{:S(2)}, u32[]{:S(2)}) collective-permute-start(bf16[4,2,64,256]{3,2,1,0:T(8,128)(2,1)S(1)} %shard_map.66.after_ref.own_ref), channel_id=1, source_target_pairs={{0,4},{8,12},{16,20},{24,28},{32,36},{40,44},{48,52},{56,60},{64,6... | collective-permute-start | bytes 786440 | tf_op jit(solution)/shard_map/ppermute | solution.py:37
  13.1 11.0 %collective-permute-start.3 = (bf16[4,2,64,256]{3,2,1,0:T(8,128)(2,1)S(1)}, bf16[4,2,64,256]{3,2,1,0:T(8,128)(2,1)S(1)}, u32[]{:S(2)}, u32[]{:S(2)}) collective-permute-start(bf16[4,2,64,256]{3,2,1,0:T(8,128)(2,1)S(1)} %shard_map.66.after_ref.own_ref), channel_id=1, source_target_pairs={{29,33},{61,65},{93,97},{125,129},{157,161},{189,193},{221,225},{2... | collective-permute-start | bytes 786440 | tf_op jit(solution)/shard_map/ppermute | solution.py:37
  24.1 0.7 %collective-permute-start.2 = (bf16[4,2,64,256]{3,2,1,0:T(8,128)(2,1)S(1)}, bf16[4,2,64,256]{3,2,1,0:T(8,128)(2,1)S(1)}, u32[]{:S(2)}, u32[]{:S(2)}) collective-permute-start(bf16[4,2,64,256]{3,2,1,0:T(8,128)(2,1)S(1)} %shard_map.66.after_ref.own_ref), channel_id=1, source_target_pairs={{4,8},{12,16},{20,24},{28,32},{36,40},{44,48},{52,56},{60,64},{68,... | collective-permute-start | bytes 786440 | tf_op jit(solution)/shard_map/ppermute | solution.py:37
  24.7 0.0 copy-done.1
  24.8 0.0 copy-done.3
  24.8 0.2 shard_map.69.hidden_ref
  25.0 0.0 copy-done.4
  25.0 0.0 copy-done.5
  25.0 1.1 %shard_map.67 = (f32[36,256]{1,0:T(8,128)S(1)}, f32[36,256]{1,0:T(8,128)S(1)}) custom-call(s32[512]{0:T(512)S(1)} %copy-done.5, f32[25,256]{1,0:T(8,128)S(1)} %copy-done.4, bf16[4,2,64,256]{3,2,1,0:T(8,128)(2,1)S(1)} %shard_map.66.after_ref.own_ref), custom_call_target="tpu_custom_call" | custom-call | flops 1000000 | bytes 200000 | tf_op jit(solution)/shard_map/pallas_call | solution.py:259
  26.2 0.2 shard_map.68.total_ref
  26.4 0.0 collective-permute-done.4.first_ref
  26.4 2.0 %collective-permute-done.3.second_ref = bf16[4,2,64,256]{3,2,1,0:T(8,128)(2,1)S(1)} collective-permute-done((bf16[4,2,64,256]{3,2,1,0:T(8,128)(2,1)S(1)}, bf16[4,2,64,256]{3,2,1,0:T(8,128)(2,1)S(1)}, u32[]{:S(2)}, u32[]{:S(2)}) %collective-permute-start.3) | collective-permute-done | bytes 262176 | tf_op jit(solution)/shard_map/ppermute | solution.py:37
  28.4 0.0 collective-permute-done.2.third_ref
  28.4 0.5 shard_map.70.own_ref
  28.9 1.9 %collective-permute-start.7 = (bf16[4,2,64,256]{3,2,1,0:T(8,128)(2,1)S(1)}, bf16[4,2,64,256]{3,2,1,0:T(8,128)(2,1)S(1)}, u32[]{:S(2)}, u32[]{:S(2)}) collective-permute-start(bf16[4,2,64,256]{3,2,1,0:T(8,128)(2,1)S(1)} %shard_map.70.own_ref), channel_id=1, source_target_pairs={{0,4},{8,12},{16,20},{24,28},{32,36},{40,44},{48,52},{56,60},{64,6... | collective-permute-start | bytes 786440 | tf_op jit(solution)/shard_map/ppermute | solution.py:37
  30.8 6.9 %collective-permute-start.6 = (bf16[4,2,64,256]{3,2,1,0:T(8,128)(2,1)S(1)}, bf16[4,2,64,256]{3,2,1,0:T(8,128)(2,1)S(1)}, u32[]{:S(2)}, u32[]{:S(2)}) collective-permute-start(bf16[4,2,64,256]{3,2,1,0:T(8,128)(2,1)S(1)} %shard_map.70.own_ref), channel_id=1, source_target_pairs={{29,33},{61,65},{93,97},{125,129},{157,161},{189,193},{221,225},{2... | collective-permute-start | bytes 786440 | tf_op jit(solution)/shard_map/ppermute | solution.py:37
  37.7 0.7 %collective-permute-start.5 = (bf16[4,2,64,256]{3,2,1,0:T(8,128)(2,1)S(1)}, bf16[4,2,64,256]{3,2,1,0:T(8,128)(2,1)S(1)}, u32[]{:S(2)}, u32[]{:S(2)}) collective-permute-start(bf16[4,2,64,256]{3,2,1,0:T(8,128)(2,1)S(1)} %shard_map.70.own_ref), channel_id=1, source_target_pairs={{4,8},{12,16},{20,24},{28,32},{36,40},{44,48},{52,56},{60,64},{68,... | collective-permute-start | bytes 786440 | tf_op jit(solution)/shard_map/ppermute | solution.py:37
  38.4 0.2 shard_map.71.total_ref
  38.6 0.0 collective-permute-done.7.first_ref
  38.6 4.7 %collective-permute-done.6.second_ref = bf16[4,2,64,256]{3,2,1,0:T(8,128)(2,1)S(1)} collective-permute-done((bf16[4,2,64,256]{3,2,1,0:T(8,128)(2,1)S(1)}, bf16[4,2,64,256]{3,2,1,0:T(8,128)(2,1)S(1)}, u32[]{:S(2)}, u32[]{:S(2)}) %collective-permute-start.6) | collective-permute-done | bytes 262176 | tf_op jit(solution)/shard_map/ppermute | solution.py:37
  43.3 0.0 collective-permute-done.5.third_ref
  43.3 0.1 shard_map.72.far_ref
  43.4 1.9 %collective-permute-start.8 = (bf16[4,64,256]{2,1,0:T(8,128)(2,1)S(1)}, bf16[4,64,256]{2,1,0:T(8,128)(2,1)S(1)}, u32[]{:S(2)}, u32[]{:S(2)}) collective-permute-start(bf16[4,64,256]{2,1,0:T(8,128)(2,1)S(1)} %shard_map.72.far_ref), channel_id=1, source_target_pairs={{1,2},{2,1},{5,6},{6,5},{9,10},{10,9},{13,14},{14,13},{17,18},{18,... | collective-permute-start | bytes 393224 | tf_op jit(solution)/shard_map/ppermute | solution.py:19
  45.4 0.2 shard_map.73.near_ref
  45.6 1.9 %collective-permute-start.9 = (bf16[4,64,256]{2,1,0:T(8,128)(2,1)S(1)}, bf16[4,64,256]{2,1,0:T(8,128)(2,1)S(1)}, u32[]{:S(2)}, u32[]{:S(2)}) collective-permute-start(bf16[4,64,256]{2,1,0:T(8,128)(2,1)S(1)} %shard_map.73.near_ref), channel_id=1, source_target_pairs={{0,1},{2,3},{1,0},{3,2},{4,5},{6,7},{5,4},{7,6},{8,9},{10,11},{9,8... | collective-permute-start | bytes 393224 | tf_op jit(solution)/shard_map/ppermute | solution.py:19
  47.5 0.6 %shard_map.74 = (f32[256,256]{1,0:T(8,128)S(1)}, f32[256,256]{1,0:T(8,128)S(1)}) custom-call(bf16[4,64,256]{2,1,0:T(8,128)(2,1)S(1)} %shard_map.72.far_ref, bf16[4,64,256]{2,1,0:T(8,128)(2,1)S(1)} %shard_map.73.near_ref, bf16[9,256,256]{2,1,0:T(8,128)(2,1)S(1)} %copy-done, bf16[4,2,64,256]{3,2,1,0:T(8,128)(2,1)S(1)} %copy-done.1), custom_call_target="tpu_custom_call" | custom-call | flops 402653184 | bytes 2000000 | tf_op jit(solution)/shard_map/pallas_call | solution.py:279
  48.1 3.1 %collective-permute-done.8.far_halo = bf16[4,64,256]{2,1,0:T(8,128)(2,1)S(1)} collective-permute-done((bf16[4,64,256]{2,1,0:T(8,128)(2,1)S(1)}, bf16[4,64,256]{2,1,0:T(8,128)(2,1)S(1)}, u32[]{:S(2)}, u32[]{:S(2)}) %collective-permute-start.8) | collective-permute-done | bytes 131104 | tf_op jit(solution)/shard_map/ppermute | solution.py:19
  51.2 0.0 collective-permute-done.9.near_halo
  51.2 1.1 %shard_map.75 = bf16[4,2,64,256]{3,2,1,0:T(8,128)(2,1)} custom-call(f32[256,256]{1,0:T(8,128)S(1)} %get-tuple-element.15.far_total, bf16[4,64,256]{2,1,0:T(8,128)(2,1)S(1)} %collective-permute-done.8.far_halo, f32[256,256]{1,0:T(8,128)S(1)} %get-tuple-element.16.near_total, bf16[4,64,256]{2,1,0:T(8,128)(2,1)S(1)} %collective-permute-done.9.near_halo, ...), custom_call_target="tpu_custom_call" | custom-call | flops 201326592 | bytes 2000000 | tf_op jit(solution)/shard_map/pallas_call | solution.py:282
  (1 shorter events, 0.0 us)
Async XLA Ops:
  0.0 5.8 %copy-start = (bf16[9,256,256]{2,1,0:T(8,128)(2,1)S(1)}, bf16[9,256,256]{2,1,0:T(8,128)(2,1)}, u32[]{:S(2)}) copy-start(bf16[9,256,256]{2,1,0:T(8,128)(2,1)} %weight_ref.7) | copy-start | bytes 3538948
  0.0 1.0 %copy-start.2 = (bf16[4,2,64,256]{3,2,1,0:T(8,128)(2,1)S(1)}, bf16[4,2,64,256]{3,2,1,0:T(8,128)(2,1)}, u32[]{:S(2)}) copy-start(bf16[4,2,64,256]{3,2,1,0:T(8,128)(2,1)} %x_ref.3) | copy-start | bytes 786436
  1.1 7.8 %collective-permute-start = (bf16[4,64,256]{2,1,0:T(8,128)(2,1)S(1)}, bf16[4,64,256]{2,1,0:T(8,128)(2,1)S(1)}, u32[]{:S(2)}, u32[]{:S(2)}) collective-permute-start(bf16[4,64,256]{2,1,0:T(8,128)(2,1)S(1)} %get-tuple-element.11), channel_id=1, source_target_pairs={{1,2},{2,1},{5,6},{6,5},{9,10},{10,9},{13,14},{14,13},{17,18},{18,... | collective-permute-start | bytes 393224 | tf_op jit(solution)/shard_map/ppermute | solution.py:19
  3.8 5.0 %collective-permute-start.1 = (bf16[4,64,256]{2,1,0:T(8,128)(2,1)S(1)}, bf16[4,64,256]{2,1,0:T(8,128)(2,1)S(1)}, u32[]{:S(2)}, u32[]{:S(2)}) collective-permute-start(bf16[4,64,256]{2,1,0:T(8,128)(2,1)S(1)} %get-tuple-element.12), channel_id=1, source_target_pairs={{0,1},{2,3},{1,0},{3,2},{4,5},{6,7},{5,4},{7,6},{8,9},{10,11},{9,8... | collective-permute-start | bytes 393224 | tf_op jit(solution)/shard_map/ppermute | solution.py:19
  6.4 18.4 %copy-start.1 = (bf16[4,2,64,256]{3,2,1,0:T(8,128)(2,1)S(1)}, bf16[4,2,64,256]{3,2,1,0:T(8,128)(2,1)}, u32[]{:S(2)}) copy-start(bf16[4,2,64,256]{3,2,1,0:T(8,128)(2,1)} %cot_ref.3) | copy-start | bytes 786436
  6.4 18.4 %copy-start.3 = (bf16[256,256]{1,0:T(8,128)(2,1)S(1)}, bf16[256,256]{1,0:T(8,128)(2,1)}, u32[]{:S(2)}) copy-start(bf16[256,256]{1,0:T(8,128)(2,1)} %proj_ref.1) | copy-start | bytes 393220
  6.4 18.6 %copy-start.4 = (f32[25,256]{1,0:T(8,128)S(1)}, f32[25,256]{1,0:T(8,128)}, u32[]{:S(2)}) copy-start(f32[25,256]{1,0:T(8,128)} %mixing_ref.1) | copy-start | bytes 76804
  6.4 18.6 %copy-start.5 = (s32[512]{0:T(512)S(1)}, s32[512]{0:T(512)}, u32[]{:S(2)}) copy-start(s32[512]{0:T(512)} %offsets_ref.1) | copy-start | bytes 6148
  9.2 17.1 %collective-permute-start.4 = (bf16[4,2,64,256]{3,2,1,0:T(8,128)(2,1)S(1)}, bf16[4,2,64,256]{3,2,1,0:T(8,128)(2,1)S(1)}, u32[]{:S(2)}, u32[]{:S(2)}) collective-permute-start(bf16[4,2,64,256]{3,2,1,0:T(8,128)(2,1)S(1)} %shard_map.66.after_ref.own_ref), channel_id=1, source_target_pairs={{0,4},{8,12},{16,20},{24,28},{32,36},{40,44},{48,52},{56,60},{64,6... | collective-permute-start | bytes 786440 | tf_op jit(solution)/shard_map/ppermute | solution.py:37
  13.1 15.3 %collective-permute-start.3 = (bf16[4,2,64,256]{3,2,1,0:T(8,128)(2,1)S(1)}, bf16[4,2,64,256]{3,2,1,0:T(8,128)(2,1)S(1)}, u32[]{:S(2)}, u32[]{:S(2)}) collective-permute-start(bf16[4,2,64,256]{3,2,1,0:T(8,128)(2,1)S(1)} %shard_map.66.after_ref.own_ref), channel_id=1, source_target_pairs={{29,33},{61,65},{93,97},{125,129},{157,161},{189,193},{221,225},{2... | collective-permute-start | bytes 786440 | tf_op jit(solution)/shard_map/ppermute | solution.py:37
  24.1 4.3 %collective-permute-start.2 = (bf16[4,2,64,256]{3,2,1,0:T(8,128)(2,1)S(1)}, bf16[4,2,64,256]{3,2,1,0:T(8,128)(2,1)S(1)}, u32[]{:S(2)}, u32[]{:S(2)}) collective-permute-start(bf16[4,2,64,256]{3,2,1,0:T(8,128)(2,1)S(1)} %shard_map.66.after_ref.own_ref), channel_id=1, source_target_pairs={{4,8},{12,16},{20,24},{28,32},{36,40},{44,48},{52,56},{60,64},{68,... | collective-permute-start | bytes 786440 | tf_op jit(solution)/shard_map/ppermute | solution.py:37
  28.9 9.7 %collective-permute-start.7 = (bf16[4,2,64,256]{3,2,1,0:T(8,128)(2,1)S(1)}, bf16[4,2,64,256]{3,2,1,0:T(8,128)(2,1)S(1)}, u32[]{:S(2)}, u32[]{:S(2)}) collective-permute-start(bf16[4,2,64,256]{3,2,1,0:T(8,128)(2,1)S(1)} %shard_map.70.own_ref), channel_id=1, source_target_pairs={{0,4},{8,12},{16,20},{24,28},{32,36},{40,44},{48,52},{56,60},{64,6... | collective-permute-start | bytes 786440 | tf_op jit(solution)/shard_map/ppermute | solution.py:37
  30.8 12.5 %collective-permute-start.6 = (bf16[4,2,64,256]{3,2,1,0:T(8,128)(2,1)S(1)}, bf16[4,2,64,256]{3,2,1,0:T(8,128)(2,1)S(1)}, u32[]{:S(2)}, u32[]{:S(2)}) collective-permute-start(bf16[4,2,64,256]{3,2,1,0:T(8,128)(2,1)S(1)} %shard_map.70.own_ref), channel_id=1, source_target_pairs={{29,33},{61,65},{93,97},{125,129},{157,161},{189,193},{221,225},{2... | collective-permute-start | bytes 786440 | tf_op jit(solution)/shard_map/ppermute | solution.py:37
  37.7 5.6 %collective-permute-start.5 = (bf16[4,2,64,256]{3,2,1,0:T(8,128)(2,1)S(1)}, bf16[4,2,64,256]{3,2,1,0:T(8,128)(2,1)S(1)}, u32[]{:S(2)}, u32[]{:S(2)}) collective-permute-start(bf16[4,2,64,256]{3,2,1,0:T(8,128)(2,1)S(1)} %shard_map.70.own_ref), channel_id=1, source_target_pairs={{4,8},{12,16},{20,24},{28,32},{36,40},{44,48},{52,56},{60,64},{68,... | collective-permute-start | bytes 786440 | tf_op jit(solution)/shard_map/ppermute | solution.py:37
  43.4 7.8 %collective-permute-start.8 = (bf16[4,64,256]{2,1,0:T(8,128)(2,1)S(1)}, bf16[4,64,256]{2,1,0:T(8,128)(2,1)S(1)}, u32[]{:S(2)}, u32[]{:S(2)}) collective-permute-start(bf16[4,64,256]{2,1,0:T(8,128)(2,1)S(1)} %shard_map.72.far_ref), channel_id=1, source_target_pairs={{1,2},{2,1},{5,6},{6,5},{9,10},{10,9},{13,14},{14,13},{17,18},{18,... | collective-permute-start | bytes 393224 | tf_op jit(solution)/shard_map/ppermute | solution.py:19
  45.6 5.7 %collective-permute-start.9 = (bf16[4,64,256]{2,1,0:T(8,128)(2,1)S(1)}, bf16[4,64,256]{2,1,0:T(8,128)(2,1)S(1)}, u32[]{:S(2)}, u32[]{:S(2)}) collective-permute-start(bf16[4,64,256]{2,1,0:T(8,128)(2,1)S(1)} %shard_map.73.near_ref), channel_id=1, source_target_pairs={{0,1},{2,3},{1,0},{3,2},{4,5},{6,7},{5,4},{7,6},{8,9},{10,11},{9,8... | collective-permute-start | bytes 393224 | tf_op jit(solution)/shard_map/ppermute | solution.py:19

commit v8 on v7

--- a/solution.py
+++ b/solution.py
@@ -23,7 +23,7 @@
     place = link % 16
     plain = 2 * (place % 2)
     turned = where(place % 8 == 7, 1, where(place < 8, plain, 2 - plain))
-    return where(band == 0, plain, turned)
+    return where(band == 0, place % 2, turned)
 
 
 def crossed(value, turn):

time: 52.7 us -> 52.6 us (level)
  no operation moved by 1% of the time
where the time goes in v8:
time: 52.6 us; the launch traced here: 52.3 us
  starting transfers between devices  33.5 us (64%)
  waiting for transfers between devices  12.3 us (23%)
  Pallas kernels  5.22 us (10%)
  local copies, waits for them, and re-layouts  1.07 us (2%)
    ppermute x6, starting transfers between devices, crossed(): lax.ppermute(value, ('tm', 'lat'), pairs + [(j, i) for i, j in pairs])  24.9 us
    ppermute x4, starting transfers between devices, swap(): return lax.ppermute(value, axis, pairs + [(j, i) for i, j in pairs])  8.51 us
    ppermute x6, waiting for transfers between devices, crossed(): lax.ppermute(value, ('tm', 'lat'), pairs + [(j, i) for i, j in pairs])  6.74 us
    ppermute x4, waiting for transfers between devices, swap(): return lax.ppermute(value, axis, pairs + [(j, i) for i, j in pairs])  5.57 us
    pallas_call x1, Pallas kernels, body(): call(table_kernel, (table, table), [SMEM] + [VMEM] * 2, (1000000, 200000))  1.12 us
    pallas_call x1, Pallas kernels, body(): call(final_kernel, block, [VMEM] * 5, (2 * tap, 2000000), out_specs=pl.Bl...  1.08 us
    unnamed x12, local copies, waits for them, and re-layouts  1.07 us
  transfers between devices with their start and end apart: 10, of which 4 were waited for; matrix products, arithmetic and copies ran while one was open for 0% of the time, Pallas kernels for 6%

profile of v8, /device:TPU:6, one launch (start us, length us, event | category | flops | bytes accessed | tf_op | source)
XLA Modules:
  0.0 52.3 jit_solution(624997407455128982)
XLA Ops:
  0.0 0.0 copy-start
  0.0 0.0 copy-start.2
  0.0 1.0 %copy-done.2 = bf16[4,2,64,256]{3,2,1,0:T(8,128)(2,1)S(1)} copy-done((bf16[4,2,64,256]{3,2,1,0:T(8,128)(2,1)S(1)}, bf16[4,2,64,256]{3,2,1,0:T(8,128)(2,1)}, u32[]{:S(2)}) %copy-start.2) | copy-done | bytes 262168
  1.1 2.8 %collective-permute-start = (bf16[4,64,256]{2,1,0:T(8,128)(2,1)S(1)}, bf16[4,64,256]{2,1,0:T(8,128)(2,1)S(1)}, u32[]{:S(2)}, u32[]{:S(2)}) collective-permute-start(bf16[4,64,256]{2,1,0:T(8,128)(2,1)S(1)} %get-tuple-element.11), channel_id=1, source_target_pairs={{1,2},{2,1},{5,6},{6,5},{9,10},{10,9},{13,14},{14,13},{17,18},{18,... | collective-permute-start | bytes 393224 | tf_op jit(solution)/shard_map/ppermute | solution.py:19
  3.8 1.9 %collective-permute-start.1 = (bf16[4,64,256]{2,1,0:T(8,128)(2,1)S(1)}, bf16[4,64,256]{2,1,0:T(8,128)(2,1)S(1)}, u32[]{:S(2)}, u32[]{:S(2)}) collective-permute-start(bf16[4,64,256]{2,1,0:T(8,128)(2,1)S(1)} %get-tuple-element.12), channel_id=1, source_target_pairs={{0,1},{2,3},{1,0},{3,2},{4,5},{6,7},{5,4},{7,6},{8,9},{10,11},{9,8... | collective-permute-start | bytes 393224 | tf_op jit(solution)/shard_map/ppermute | solution.py:19
  5.8 0.0 copy-done
  5.8 0.6 %shard_map.64.total_ref = f32[2,256,256]{2,1,0:T(8,128)S(1)} custom-call(bf16[4,2,64,256]{3,2,1,0:T(8,128)(2,1)S(1)} %copy-done.2, bf16[9,256,256]{2,1,0:T(8,128)(2,1)S(1)} %copy-done), custom_call_target="tpu_custom_call" | custom-call | flops 402653184 | bytes 2000000 | tf_op jit(solution)/shard_map/pallas_call | solution.py:241
  6.4 0.0 copy-start.1
  6.4 0.0 copy-start.3
  6.4 0.0 copy-start.4
  6.4 0.0 copy-start.5
  6.4 2.5 %collective-permute-done.far_ref = bf16[4,64,256]{2,1,0:T(8,128)(2,1)S(1)} collective-permute-done((bf16[4,64,256]{2,1,0:T(8,128)(2,1)S(1)}, bf16[4,64,256]{2,1,0:T(8,128)(2,1)S(1)}, u32[]{:S(2)}, u32[]{:S(2)}) %collective-permute-start) | collective-permute-done | bytes 131104 | tf_op jit(solution)/shard_map/ppermute | solution.py:19
  8.9 0.0 collective-permute-done.1.near_ref
  8.9 0.4 shard_map.66.after_ref.own_ref
  9.2 3.8 %collective-permute-start.4 = (bf16[4,2,64,256]{3,2,1,0:T(8,128)(2,1)S(1)}, bf16[4,2,64,256]{3,2,1,0:T(8,128)(2,1)S(1)}, u32[]{:S(2)}, u32[]{:S(2)}) collective-permute-start(bf16[4,2,64,256]{3,2,1,0:T(8,128)(2,1)S(1)} %shard_map.66.after_ref.own_ref), channel_id=1, source_target_pairs={{0,4},{8,12},{16,20},{24,28},{32,36},{40,44},{48,52},{56,60},{64,6... | collective-permute-start | bytes 786440 | tf_op jit(solution)/shard_map/ppermute | solution.py:37
  13.1 11.0 %collective-permute-start.3 = (bf16[4,2,64,256]{3,2,1,0:T(8,128)(2,1)S(1)}, bf16[4,2,64,256]{3,2,1,0:T(8,128)(2,1)S(1)}, u32[]{:S(2)}, u32[]{:S(2)}) collective-permute-start(bf16[4,2,64,256]{3,2,1,0:T(8,128)(2,1)S(1)} %shard_map.66.after_ref.own_ref), channel_id=1, source_target_pairs={{4,8},{12,16},{20,24},{28,32},{36,40},{44,48},{52,56},{60,64},{68,... | collective-permute-start | bytes 786440 | tf_op jit(solution)/shard_map/ppermute | solution.py:37
  24.1 0.7 %collective-permute-start.2 = (bf16[4,2,64,256]{3,2,1,0:T(8,128)(2,1)S(1)}, bf16[4,2,64,256]{3,2,1,0:T(8,128)(2,1)S(1)}, u32[]{:S(2)}, u32[]{:S(2)}) collective-permute-start(bf16[4,2,64,256]{3,2,1,0:T(8,128)(2,1)S(1)} %shard_map.66.after_ref.own_ref), channel_id=1, source_target_pairs={{5,9},{13,17},{21,25},{33,37},{41,45},{49,53},{57,61},{69,73},{77,... | collective-permute-start | bytes 786440 | tf_op jit(solution)/shard_map/ppermute | solution.py:37
  24.7 0.0 copy-done.1
  24.8 0.0 copy-done.3
  24.8 0.2 shard_map.69.hidden_ref
  25.0 0.0 copy-done.4
  25.0 0.0 copy-done.5
  25.0 1.1 %shard_map.67 = (f32[36,256]{1,0:T(8,128)S(1)}, f32[36,256]{1,0:T(8,128)S(1)}) custom-call(s32[512]{0:T(512)S(1)} %copy-done.5, f32[25,256]{1,0:T(8,128)S(1)} %copy-done.4, bf16[4,2,64,256]{3,2,1,0:T(8,128)(2,1)S(1)} %shard_map.66.after_ref.own_ref), custom_call_target="tpu_custom_call" | custom-call | flops 1000000 | bytes 200000 | tf_op jit(solution)/shard_map/pallas_call | solution.py:259
  26.2 0.2 shard_map.68.total_ref
  26.4 0.0 collective-permute-done.4.first_ref
  26.4 2.0 %collective-permute-done.3.second_ref = bf16[4,2,64,256]{3,2,1,0:T(8,128)(2,1)S(1)} collective-permute-done((bf16[4,2,64,256]{3,2,1,0:T(8,128)(2,1)S(1)}, bf16[4,2,64,256]{3,2,1,0:T(8,128)(2,1)S(1)}, u32[]{:S(2)}, u32[]{:S(2)}) %collective-permute-start.3) | collective-permute-done | bytes 262176 | tf_op jit(solution)/shard_map/ppermute | solution.py:37
  28.4 0.0 collective-permute-done.2.third_ref
  28.4 0.5 shard_map.70.own_ref
  28.9 1.9 %collective-permute-start.7 = (bf16[4,2,64,256]{3,2,1,0:T(8,128)(2,1)S(1)}, bf16[4,2,64,256]{3,2,1,0:T(8,128)(2,1)S(1)}, u32[]{:S(2)}, u32[]{:S(2)}) collective-permute-start(bf16[4,2,64,256]{3,2,1,0:T(8,128)(2,1)S(1)} %shard_map.70.own_ref), channel_id=1, source_target_pairs={{0,4},{8,12},{16,20},{24,28},{32,36},{40,44},{48,52},{56,60},{64,6... | collective-permute-start | bytes 786440 | tf_op jit(solution)/shard_map/ppermute | solution.py:37
  30.8 6.9 %collective-permute-start.6 = (bf16[4,2,64,256]{3,2,1,0:T(8,128)(2,1)S(1)}, bf16[4,2,64,256]{3,2,1,0:T(8,128)(2,1)S(1)}, u32[]{:S(2)}, u32[]{:S(2)}) collective-permute-start(bf16[4,2,64,256]{3,2,1,0:T(8,128)(2,1)S(1)} %shard_map.70.own_ref), channel_id=1, source_target_pairs={{4,8},{12,16},{20,24},{28,32},{36,40},{44,48},{52,56},{60,64},{68,... | collective-permute-start | bytes 786440 | tf_op jit(solution)/shard_map/ppermute | solution.py:37
  37.7 0.7 %collective-permute-start.5 = (bf16[4,2,64,256]{3,2,1,0:T(8,128)(2,1)S(1)}, bf16[4,2,64,256]{3,2,1,0:T(8,128)(2,1)S(1)}, u32[]{:S(2)}, u32[]{:S(2)}) collective-permute-start(bf16[4,2,64,256]{3,2,1,0:T(8,128)(2,1)S(1)} %shard_map.70.own_ref), channel_id=1, source_target_pairs={{5,9},{13,17},{21,25},{33,37},{41,45},{49,53},{57,61},{69,73},{77,... | collective-permute-start | bytes 786440 | tf_op jit(solution)/shard_map/ppermute | solution.py:37
  38.4 0.2 shard_map.71.total_ref
  38.6 0.0 collective-permute-done.7.first_ref
  38.6 4.7 %collective-permute-done.6.second_ref = bf16[4,2,64,256]{3,2,1,0:T(8,128)(2,1)S(1)} collective-permute-done((bf16[4,2,64,256]{3,2,1,0:T(8,128)(2,1)S(1)}, bf16[4,2,64,256]{3,2,1,0:T(8,128)(2,1)S(1)}, u32[]{:S(2)}, u32[]{:S(2)}) %collective-permute-start.6) | collective-permute-done | bytes 262176 | tf_op jit(solution)/shard_map/ppermute | solution.py:37
  43.3 0.0 collective-permute-done.5.third_ref
  43.3 0.1 shard_map.72.far_ref
  43.4 1.9 %collective-permute-start.8 = (bf16[4,64,256]{2,1,0:T(8,128)(2,1)S(1)}, bf16[4,64,256]{2,1,0:T(8,128)(2,1)S(1)}, u32[]{:S(2)}, u32[]{:S(2)}) collective-permute-start(bf16[4,64,256]{2,1,0:T(8,128)(2,1)S(1)} %shard_map.72.far_ref), channel_id=1, source_target_pairs={{1,2},{2,1},{5,6},{6,5},{9,10},{10,9},{13,14},{14,13},{17,18},{18,... | collective-permute-start | bytes 393224 | tf_op jit(solution)/shard_map/ppermute | solution.py:19
  45.4 0.2 shard_map.73.near_ref
  45.6 1.9 %collective-permute-start.9 = (bf16[4,64,256]{2,1,0:T(8,128)(2,1)S(1)}, bf16[4,64,256]{2,1,0:T(8,128)(2,1)S(1)}, u32[]{:S(2)}, u32[]{:S(2)}) collective-permute-start(bf16[4,64,256]{2,1,0:T(8,128)(2,1)S(1)} %shard_map.73.near_ref), channel_id=1, source_target_pairs={{0,1},{2,3},{1,0},{3,2},{4,5},{6,7},{5,4},{7,6},{8,9},{10,11},{9,8... | collective-permute-start | bytes 393224 | tf_op jit(solution)/shard_map/ppermute | solution.py:19
  47.5 0.6 %shard_map.74 = (f32[256,256]{1,0:T(8,128)S(1)}, f32[256,256]{1,0:T(8,128)S(1)}) custom-call(bf16[4,64,256]{2,1,0:T(8,128)(2,1)S(1)} %shard_map.72.far_ref, bf16[4,64,256]{2,1,0:T(8,128)(2,1)S(1)} %shard_map.73.near_ref, bf16[9,256,256]{2,1,0:T(8,128)(2,1)S(1)} %copy-done, bf16[4,2,64,256]{3,2,1,0:T(8,128)(2,1)S(1)} %copy-done.1), custom_call_target="tpu_custom_call" | custom-call | flops 402653184 | bytes 2000000 | tf_op jit(solution)/shard_map/pallas_call | solution.py:279
  48.1 3.1 %collective-permute-done.8.far_halo = bf16[4,64,256]{2,1,0:T(8,128)(2,1)S(1)} collective-permute-done((bf16[4,64,256]{2,1,0:T(8,128)(2,1)S(1)}, bf16[4,64,256]{2,1,0:T(8,128)(2,1)S(1)}, u32[]{:S(2)}, u32[]{:S(2)}) %collective-permute-start.8) | collective-permute-done | bytes 131104 | tf_op jit(solution)/shard_map/ppermute | solution.py:19
  51.2 0.0 collective-permute-done.9.near_halo
  51.2 1.1 %shard_map.75 = bf16[4,2,64,256]{3,2,1,0:T(8,128)(2,1)} custom-call(f32[256,256]{1,0:T(8,128)S(1)} %get-tuple-element.15.far_total, bf16[4,64,256]{2,1,0:T(8,128)(2,1)S(1)} %collective-permute-done.8.far_halo, f32[256,256]{1,0:T(8,128)S(1)} %get-tuple-element.16.near_total, bf16[4,64,256]{2,1,0:T(8,128)(2,1)S(1)} %collective-permute-done.9.near_halo, ...), custom_call_target="tpu_custom_call" | custom-call | flops 201326592 | bytes 2000000 | tf_op jit(solution)/shard_map/pallas_call | solution.py:282
  (1 shorter events, 0.0 us)
Async XLA Ops:
  0.0 5.8 %copy-start = (bf16[9,256,256]{2,1,0:T(8,128)(2,1)S(1)}, bf16[9,256,256]{2,1,0:T(8,128)(2,1)}, u32[]{:S(2)}) copy-start(bf16[9,256,256]{2,1,0:T(8,128)(2,1)} %weight_ref.7) | copy-start | bytes 3538948
  0.0 1.0 %copy-start.2 = (bf16[4,2,64,256]{3,2,1,0:T(8,128)(2,1)S(1)}, bf16[4,2,64,256]{3,2,1,0:T(8,128)(2,1)}, u32[]{:S(2)}) copy-start(bf16[4,2,64,256]{3,2,1,0:T(8,128)(2,1)} %x_ref.3) | copy-start | bytes 786436
  1.1 7.8 %collective-permute-start = (bf16[4,64,256]{2,1,0:T(8,128)(2,1)S(1)}, bf16[4,64,256]{2,1,0:T(8,128)(2,1)S(1)}, u32[]{:S(2)}, u32[]{:S(2)}) collective-permute-start(bf16[4,64,256]{2,1,0:T(8,128)(2,1)S(1)} %get-tuple-element.11), channel_id=1, source_target_pairs={{1,2},{2,1},{5,6},{6,5},{9,10},{10,9},{13,14},{14,13},{17,18},{18,... | collective-permute-start | bytes 393224 | tf_op jit(solution)/shard_map/ppermute | solution.py:19
  3.8 5.0 %collective-permute-start.1 = (bf16[4,64,256]{2,1,0:T(8,128)(2,1)S(1)}, bf16[4,64,256]{2,1,0:T(8,128)(2,1)S(1)}, u32[]{:S(2)}, u32[]{:S(2)}) collective-permute-start(bf16[4,64,256]{2,1,0:T(8,128)(2,1)S(1)} %get-tuple-element.12), channel_id=1, source_target_pairs={{0,1},{2,3},{1,0},{3,2},{4,5},{6,7},{5,4},{7,6},{8,9},{10,11},{9,8... | collective-permute-start | bytes 393224 | tf_op jit(solution)/shard_map/ppermute | solution.py:19
  6.4 18.4 %copy-start.1 = (bf16[4,2,64,256]{3,2,1,0:T(8,128)(2,1)S(1)}, bf16[4,2,64,256]{3,2,1,0:T(8,128)(2,1)}, u32[]{:S(2)}) copy-start(bf16[4,2,64,256]{3,2,1,0:T(8,128)(2,1)} %cot_ref.3) | copy-start | bytes 786436
  6.4 18.4 %copy-start.3 = (bf16[256,256]{1,0:T(8,128)(2,1)S(1)}, bf16[256,256]{1,0:T(8,128)(2,1)}, u32[]{:S(2)}) copy-start(bf16[256,256]{1,0:T(8,128)(2,1)} %proj_ref.1) | copy-start | bytes 393220
  6.4 18.6 %copy-start.4 = (f32[25,256]{1,0:T(8,128)S(1)}, f32[25,256]{1,0:T(8,128)}, u32[]{:S(2)}) copy-start(f32[25,256]{1,0:T(8,128)} %mixing_ref.1) | copy-start | bytes 76804
  6.4 18.6 %copy-start.5 = (s32[512]{0:T(512)S(1)}, s32[512]{0:T(512)}, u32[]{:S(2)}) copy-start(s32[512]{0:T(512)} %offsets_ref.1) | copy-start | bytes 6148
  9.2 17.1 %collective-permute-start.4 = (bf16[4,2,64,256]{3,2,1,0:T(8,128)(2,1)S(1)}, bf16[4,2,64,256]{3,2,1,0:T(8,128)(2,1)S(1)}, u32[]{:S(2)}, u32[]{:S(2)}) collective-permute-start(bf16[4,2,64,256]{3,2,1,0:T(8,128)(2,1)S(1)} %shard_map.66.after_ref.own_ref), channel_id=1, source_target_pairs={{0,4},{8,12},{16,20},{24,28},{32,36},{40,44},{48,52},{56,60},{64,6... | collective-permute-start | bytes 786440 | tf_op jit(solution)/shard_map/ppermute | solution.py:37
  13.1 15.3 %collective-permute-start.3 = (bf16[4,2,64,256]{3,2,1,0:T(8,128)(2,1)S(1)}, bf16[4,2,64,256]{3,2,1,0:T(8,128)(2,1)S(1)}, u32[]{:S(2)}, u32[]{:S(2)}) collective-permute-start(bf16[4,2,64,256]{3,2,1,0:T(8,128)(2,1)S(1)} %shard_map.66.after_ref.own_ref), channel_id=1, source_target_pairs={{4,8},{12,16},{20,24},{28,32},{36,40},{44,48},{52,56},{60,64},{68,... | collective-permute-start | bytes 786440 | tf_op jit(solution)/shard_map/ppermute | solution.py:37
  24.1 4.3 %collective-permute-start.2 = (bf16[4,2,64,256]{3,2,1,0:T(8,128)(2,1)S(1)}, bf16[4,2,64,256]{3,2,1,0:T(8,128)(2,1)S(1)}, u32[]{:S(2)}, u32[]{:S(2)}) collective-permute-start(bf16[4,2,64,256]{3,2,1,0:T(8,128)(2,1)S(1)} %shard_map.66.after_ref.own_ref), channel_id=1, source_target_pairs={{5,9},{13,17},{21,25},{33,37},{41,45},{49,53},{57,61},{69,73},{77,... | collective-permute-start | bytes 786440 | tf_op jit(solution)/shard_map/ppermute | solution.py:37
  28.9 9.7 %collective-permute-start.7 = (bf16[4,2,64,256]{3,2,1,0:T(8,128)(2,1)S(1)}, bf16[4,2,64,256]{3,2,1,0:T(8,128)(2,1)S(1)}, u32[]{:S(2)}, u32[]{:S(2)}) collective-permute-start(bf16[4,2,64,256]{3,2,1,0:T(8,128)(2,1)S(1)} %shard_map.70.own_ref), channel_id=1, source_target_pairs={{0,4},{8,12},{16,20},{24,28},{32,36},{40,44},{48,52},{56,60},{64,6... | collective-permute-start | bytes 786440 | tf_op jit(solution)/shard_map/ppermute | solution.py:37
  30.8 12.5 %collective-permute-start.6 = (bf16[4,2,64,256]{3,2,1,0:T(8,128)(2,1)S(1)}, bf16[4,2,64,256]{3,2,1,0:T(8,128)(2,1)S(1)}, u32[]{:S(2)}, u32[]{:S(2)}) collective-permute-start(bf16[4,2,64,256]{3,2,1,0:T(8,128)(2,1)S(1)} %shard_map.70.own_ref), channel_id=1, source_target_pairs={{4,8},{12,16},{20,24},{28,32},{36,40},{44,48},{52,56},{60,64},{68,... | collective-permute-start | bytes 786440 | tf_op jit(solution)/shard_map/ppermute | solution.py:37
  37.7 5.6 %collective-permute-start.5 = (bf16[4,2,64,256]{3,2,1,0:T(8,128)(2,1)S(1)}, bf16[4,2,64,256]{3,2,1,0:T(8,128)(2,1)S(1)}, u32[]{:S(2)}, u32[]{:S(2)}) collective-permute-start(bf16[4,2,64,256]{3,2,1,0:T(8,128)(2,1)S(1)} %shard_map.70.own_ref), channel_id=1, source_target_pairs={{5,9},{13,17},{21,25},{33,37},{41,45},{49,53},{57,61},{69,73},{77,... | collective-permute-start | bytes 786440 | tf_op jit(solution)/shard_map/ppermute | solution.py:37
  43.4 7.8 %collective-permute-start.8 = (bf16[4,64,256]{2,1,0:T(8,128)(2,1)S(1)}, bf16[4,64,256]{2,1,0:T(8,128)(2,1)S(1)}, u32[]{:S(2)}, u32[]{:S(2)}) collective-permute-start(bf16[4,64,256]{2,1,0:T(8,128)(2,1)S(1)} %shard_map.72.far_ref), channel_id=1, source_target_pairs={{1,2},{2,1},{5,6},{6,5},{9,10},{10,9},{13,14},{14,13},{17,18},{18,... | collective-permute-start | bytes 393224 | tf_op jit(solution)/shard_map/ppermute | solution.py:19
  45.6 5.7 %collective-permute-start.9 = (bf16[4,64,256]{2,1,0:T(8,128)(2,1)S(1)}, bf16[4,64,256]{2,1,0:T(8,128)(2,1)S(1)}, u32[]{:S(2)}, u32[]{:S(2)}) collective-permute-start(bf16[4,64,256]{2,1,0:T(8,128)(2,1)S(1)} %shard_map.73.near_ref), channel_id=1, source_target_pairs={{0,1},{2,3},{1,0},{3,2},{4,5},{6,7},{5,4},{7,6},{8,9},{10,11},{9,8... | collective-permute-start | bytes 393224 | tf_op jit(solution)/shard_map/ppermute | solution.py:19
